TPU v7x, 32 devices: a whole 2x2x4 slice. The times are simulated.
32 devices in a mesh: grp: 4 (over x, core), dev: 8 (over z, y).
Axes of the slice: x: 2, y: 2, z: 4, core: 2. Of those that a mesh axis runs over, the one named last changes fastest.
Arguments:
- records: bfloat16 [128, 4, 2048], P(('grp', 'dev')), may hold values from -6 to 6
- usable: int32 [128, 4], replicated, may hold values 0 or 1
- panel_ids: int32 [2], replicated, may hold values from 0 to 7
Outputs:
- xcorr: bfloat16 [2, 16, 128, 512], P(None, None, ('grp', 'dev'))
Inputs may be any that keep to these rules, and one draw needn't show every extreme that they name: `panel_ids`: each entry names a panel.
All inputs are finite; a program needn't handle non-finite values.
Results may differ from a plain program's by a relative error of at most 0.0075.
Values may be sent and summed in bfloat16 or wider, within the bound.
No kernel may reach another device: no remote copies, remote signals or barrier semaphores. Data moves between devices by JAX's collectives and lax.ppermute only.
A program may use at most 64 MiB of HBM per device.

v0:
```python
import math

import jax
import jax.numpy as jnp
from jax import lax
from jax.sharding import PartitionSpec as P

NLAG = 512
SRC_DEV = 2
STEPS = 2


def broadcast(block, axis, source):
    block = jnp.where(lax.axis_index(axis) == source, block, jnp.zeros_like(block))
    return lax.psum(block, axis)


def forward_table(length, bin_count):
    samples = jnp.arange(length, dtype=jnp.int32)[:, None]
    bin_index = jnp.arange(1, bin_count + 1, dtype=jnp.int32)[None, :]
    phases = 2.0 * math.pi / length * (samples * bin_index % length).astype(jnp.float32)
    return jnp.concatenate([jnp.cos(phases), -jnp.sin(phases)], axis=1).astype(jnp.bfloat16)


def lag_table(length, bin_count, lag_count):
    bin_index = jnp.arange(1, bin_count + 1, dtype=jnp.int32)[:, None]
    lag_index = jnp.arange(lag_count, dtype=jnp.int32)[None, :] - lag_count // 2
    phases = 2.0 * math.pi / length * (bin_index * lag_index % length).astype(jnp.float32)
    factor = 1.0 / math.sqrt(bin_count)
    return jnp.concatenate([jnp.cos(phases) * factor, -jnp.sin(phases) * factor], axis=0).astype(
        jnp.bfloat16
    )


def band_matrix(bin_count, radius):
    positions = jnp.arange(bin_count, dtype=jnp.int32)
    nearby = jnp.abs(positions[:, None] - positions[None, :]) <= radius
    return nearby.astype(jnp.float32) / (2 * radius + 1)


def whiten(records, bin_count, radius):
    row_count, windows, length = records.shape
    flattened = records.reshape(row_count * windows, length)
    spectra = jnp.dot(
        flattened, forward_table(length, bin_count), preferred_element_type=jnp.float32
    )
    real_part = spectra[:, :bin_count]
    imag_part = spectra[:, bin_count:]
    amplitude = jnp.sqrt(real_part * real_part + imag_part * imag_part)
    smooth = jnp.dot(amplitude, band_matrix(bin_count, radius), precision=lax.Precision.HIGHEST)
    whitened = spectra / (jnp.concatenate([smooth, smooth], axis=1) + 1e-06)
    return whitened.astype(jnp.bfloat16).reshape(row_count, windows, 2 * bin_count)


def paired(left, right):
    return jnp.einsum("swf,rwf->srf", left, right, preferred_element_type=jnp.float32)


def cross_spectra(sources, source_mask, receivers, receiver_mask, ltable, bin_count):
    source_re = sources[:, :, :bin_count]
    source_im = sources[:, :, bin_count:]
    recv_re = receivers[:, :, :bin_count]
    recv_im = receivers[:, :, bin_count:]
    real_sum = paired(source_re, recv_re) + paired(source_im, recv_im)
    imag_sum = paired(source_im, recv_re) - paired(source_re, recv_im)
    counts = jnp.dot(source_mask, receiver_mask.T, precision=lax.Precision.HIGHEST)
    denom = jnp.maximum(counts, 1.0)[:, :, None]
    stacked = jnp.concatenate([real_sum / denom, imag_sum / denom], axis=2).astype(jnp.bfloat16)
    source_count = sources.shape[0]
    recv_count = receivers.shape[0]
    lagged = jnp.dot(
        stacked.reshape(source_count * recv_count, 2 * bin_count),
        ltable,
        preferred_element_type=jnp.float32,
    )
    return lagged.reshape(source_count, recv_count, ltable.shape[1]).astype(jnp.bfloat16)


def on_device(records, usable, panel_ids):
    channels, windows, length = records.shape
    bin_count = length // 2
    radius = bin_count // 16
    halves = channels // SRC_DEV
    group_count = lax.axis_size("grp")
    member_count = lax.axis_size("dev")
    whitened = whiten(records, bin_count, radius)
    first_channel = (lax.axis_index("grp") * member_count + lax.axis_index("dev")) * channels
    own_mask = lax.dynamic_slice_in_dim(usable, first_channel, channels, 0)
    masked = whitened * own_mask.astype(jnp.bfloat16)[:, :, None]
    receiver_mask = own_mask.astype(jnp.float32)
    grouped_mask = usable.astype(jnp.float32).reshape(
        group_count, member_count, halves, SRC_DEV, windows
    )
    ltable = lag_table(length, bin_count, NLAG)
    results = []
    for step_index in range(STEPS):
        chosen = panel_ids[step_index]
        owning = chosen // halves
        within = chosen % halves
        source_rows = lax.dynamic_slice_in_dim(masked, within * SRC_DEV, SRC_DEV, 0)
        source_mask = grouped_mask[owning][:, within].reshape(member_count * SRC_DEV, windows)
        gathered = lax.all_gather(source_rows, "dev", axis=0, tiled=True)
        whole_panel = broadcast(gathered, "grp", owning)
        results.append(
            cross_spectra(whole_panel, source_mask, masked, receiver_mask, ltable, bin_count)
        )
    return jnp.stack(results)


def solution(mesh):
    placed = (P(("grp", "dev"), None, None), P(), P())
    return jax.shard_map(
        on_device,
        mesh=mesh,
        in_specs=placed,
        out_specs=P(None, None, ("grp", "dev"), None),
        check_vma=False,
    )
```

profile of v0, /device:TPU:25, one launch (start us, length us, event | category | flops | bytes accessed | tf_op | source)
XLA Modules:
  0.0 209.5 jit_solution(17972493040792916233)
XLA Ops:
  6.5 1.3 fusion.49
  13.7 35.0 %cosine_convert_fusion = (bf16[2048,1024]{1,0:T(8,128)(2,1)}, bf16[2048,1024]{1,0:T(8,128)(2,1)}) fusion(s32[1024]{0:T(1024)S(1)} %iota_add_fusion), kind=kLoop, calls=%fused_computation.11 | loop fusion | flops 35651584 | bytes 8392704 | tf_op jit(solution)/shard_map/convert.6
  48.7 4.1 %fusion.12 = f32[16,2048]{1,0:T(8,128)S(1)} fusion(bf16[16,2048]{1,0:T(8,128)(2,1)S(1)} %reshape.47, bf16[2048,1024]{1,0:T(8,128)(2,1)} %get-tuple-element.18, bf16[2048,1024]{1,0:T(8,128)(2,1)} %get-tuple-element.17), kind=kOutput, calls=%fused_computation.23 | convolution fusion | flops 150994944 | bytes 8585216 | tf_op jit(solution)/shard_map/dot_general | solution.py:44
  52.9 1.1 fusion.10
  54.0 2.5 %copy.42 = bf16[4,4,2048]{1,0,2:T(4,128)(2,1)} copy(bf16[4,4,2048]{2,1,0:T(4,128)(2,1)S(1)} %reshape.48) | data formatting | bytes 131072 | tf_op jit(solution)/shard_map/reshape | solution.py:52
  56.6 1.7 broadcast_multiply_fusion
  58.3 3.0 %constant_dynamic-slice_fusion.3 = (bf16[2,4,2048]{1,0,2:T(2,128)(2,1)}, bf16[2,4,2048]{1,0,2:T(2,128)(2,1)S(1)}) fusion(bf16[4,4,2048]{1,0,2:T(4,128)(2,1)S(1)} %bitcast.53, s32[]{:T(128)S(6)} %select_n.82, s32[]{:T(128)S(6)} %select_n.92), kind=kLoop, calls=%fused_computation.69 | loop fusion | bytes 131080 | tf_op jit(solution)/shard_map/dynamic_slice | solution.py:100
  61.3 2.6 %copy.43 = bf16[2,4,2048]{2,1,0:T(4,128)(2,1)S(1)} copy(bf16[2,4,2048]{1,0,2:T(2,128)(2,1)} %get-tuple-element.7) | data formatting | bytes 65536 | tf_op jit(solution)/shard_map/dynamic_slice | solution.py:100
  63.9 22.1 %all_gather.6 = bf16[16,4,2048]{2,1,0:T(4,128)(2,1)S(1)} all-gather(bf16[2,4,2048]{2,1,0:T(4,128)(2,1)S(1)} %copy.43), channel_id=1, replica_groups=mesh['grp'=4,'dev'=8] {'dev'}, dimensions={0}, use_global_device_ids=true | all-gather | bytes 294912 | tf_op jit(solution)/shard_map/all_gather | solution.py:102
  86.7 25.0 %all_gather.7 = bf16[16,4,2048]{2,1,0:T(4,128)(2,1)S(1)} all-gather(bf16[2,4,2048]{2,1,0:T(4,128)(2,1)S(1)} %copy.52), channel_id=1, replica_groups=mesh['grp'=4,'dev'=8] {'dev'}, dimensions={0}, use_global_device_ids=true | all-gather | bytes 294912 | tf_op jit(solution)/shard_map/all_gather | solution.py:102
  111.6 1.0 copy_select_fusion.1
  112.6 1.0 copy_select_fusion
  113.9 10.1 %multiply_convert_fusion.1 = (bf16[1024,512]{1,0:T(8,128)(2,1)}, bf16[1024,512]{1,0:T(8,128)(2,1)}) fusion(s32[512]{0:T(512)S(1)} %iota_add_fusion.1, s32[1024]{0:T(1024)S(1)} %iota_add_fusion), kind=kLoop, calls=%fused_computation.33 | loop fusion | flops 9961472 | bytes 2103296 | tf_op jit(solution)/shard_map/convert.2
  124.0 0.9 convolution_maximum_fusion.1
  124.9 0.8 convolution_maximum_fusion
  125.7 36.0 %all-reduce.3.cloned.1.call-done = (bf16[16,4,2048]{2,0,1:T(8,128)(2,1)}, bf16[16,4,2048]{2,0,1:T(8,128)(2,1)}) async-done(((bf16[16,4,2048]{2,0,1:T(8,128)(2,1)}, bf16[16,4,2048]{2,0,1:T(8,128)(2,1)}), (bf16[16,4,2048]{2,0,1:T(8,128)(2,1)}, bf16[16,4,2048]{2,0,1:T(8,128)(2,1)})) %all-reduce.3.cloned.1.call-update) | async-done | bytes 524304 | tf_op jit(solution)/shard_map/psum | solution.py:15
  161.7 1.8 fusion.47
  164.2 2.5 %fusion.50 = f32[1024,4,16]{2,1,0:T(4,128)} fusion(bf16[4,4,2048]{1,0,2:T(4,128)(2,1)S(1)} %bitcast.54, bf16[16,4,1024]{0,1,2:T(4,128)(2,1)S(1)} %copy.45), kind=kOutput, calls=%fused_computation.81 | convolution fusion | flops 524288 | bytes 458752 | tf_op jit(solution)/shard_map/swf,rwf->srf/dot_general | solution.py:56
  167.5 1.1 copy-done.5
  168.5 2.6 %fusion.51 = f32[1024,4,16]{2,1,0:T(4,128)} fusion(bf16[4,4,2048]{1,0,2:T(4,128)(2,1)S(1)} %bitcast.55, bf16[16,4,1024]{0,1,2:T(4,128)(2,1)S(1)} %copy.46), kind=kOutput, calls=%fused_computation.82 | convolution fusion | flops 524288 | bytes 458752 | tf_op jit(solution)/shard_map/swf,rwf->srf/dot_general | solution.py:56
  171.1 3.5 %bitcast_divide_fusion.3 = bf16[16,4,1024]{0,1,2:T(4,128)(2,1)} fusion(f32[1024,4,16]{2,1,0:T(4,128)S(1)} %copy-done.17, bf16[4,4,2048]{1,0,2:T(4,128)(2,1)S(1)} %bitcast.56, bf16[16,4,1024]{0,1,2:T(4,128)(2,1)} %copy-done.5, f32[16,4]{0,1:T(4,128)S(1)} %copy-done.15), kind=kOutput, calls=%fused_computation.31 | convolution fusion | flops 720896 | bytes 590080 | tf_op jit(solution)/shard_map/swf,rwf->srf/dot_general | solution.py:56
  174.6 2.2 %copy.48 = bf16[16,4,1024]{2,0,1:T(8,128)(2,1)} copy(bf16[16,4,1024]{0,1,2:T(4,128)(2,1)} %bitcast_divide_fusion.3) | data formatting | bytes 262144 | tf_op jit(solution)/shard_map/div | solution.py:68
  176.8 3.9 %bitcast_divide_fusion.2 = bf16[16,4,1024]{0,1,2:T(4,128)(2,1)} fusion(f32[1024,4,16]{2,1,0:T(4,128)} %fusion.51, bf16[4,4,2048]{1,0,2:T(4,128)(2,1)S(1)} %bitcast.57, bf16[16,4,1024]{0,1,2:T(4,128)(2,1)S(1)} %copy-done.4, f32[16,4]{0,1:T(4,128)S(1)} %copy-done.15), kind=kOutput, calls=%fused_computation.30 | convolution fusion | flops 720896 | bytes 590080 | tf_op jit(solution)/shard_map/swf,rwf->srf/dot_general | solution.py:56
  180.6 2.2 %copy.51 = bf16[16,4,1024]{2,0,1:T(8,128)(2,1)} copy(bf16[16,4,1024]{0,1,2:T(4,128)(2,1)} %bitcast_divide_fusion.2) | data formatting | bytes 262144 | tf_op jit(solution)/shard_map/div | solution.py:68
  183.5 2.5 %fusion.52 = f32[1024,4,16]{2,1,0:T(4,128)} fusion(bf16[4,4,2048]{1,0,2:T(4,128)(2,1)S(1)} %bitcast.58, bf16[16,4,1024]{0,1,2:T(4,128)(2,1)S(1)} %copy.54), kind=kOutput, calls=%fused_computation.83 | convolution fusion | flops 524288 | bytes 458752 | tf_op jit(solution)/shard_map/swf,rwf->srf/dot_general | solution.py:56
  186.8 2.6 %fusion.53 = f32[1024,4,16]{2,1,0:T(4,128)} fusion(bf16[4,4,2048]{1,0,2:T(4,128)(2,1)S(1)} %bitcast.59, bf16[16,4,1024]{0,1,2:T(4,128)(2,1)S(1)} %copy.55), kind=kOutput, calls=%fused_computation.84 | convolution fusion | flops 524288 | bytes 458752 | tf_op jit(solution)/shard_map/swf,rwf->srf/dot_general | solution.py:56
  189.3 2.2 %bitcast_divide_fusion.1 = bf16[16,4,1024]{0,1,2:T(4,128)(2,1)} fusion(f32[1024,4,16]{2,1,0:T(4,128)S(1)} %copy-done.16, bf16[4,4,2048]{1,0,2:T(4,128)(2,1)S(1)} %bitcast.60, bf16[16,4,1024]{0,1,2:T(4,128)(2,1)S(1)} %copy.55, f32[16,4]{0,1:T(4,128)S(1)} %copy-done.14), kind=kOutput, calls=%fused_computation.29 | convolution fusion | flops 720896 | bytes 590080 | tf_op jit(solution)/shard_map/swf,rwf->srf/dot_general | solution.py:56
  191.6 2.2 %copy.56 = bf16[16,4,1024]{2,0,1:T(8,128)(2,1)} copy(bf16[16,4,1024]{0,1,2:T(4,128)(2,1)} %bitcast_divide_fusion.1) | data formatting | bytes 262144 | tf_op jit(solution)/shard_map/div | solution.py:68
  193.7 4.2 %bitcast_divide_fusion = bf16[16,4,1024]{0,1,2:T(4,128)(2,1)} fusion(f32[1024,4,16]{2,1,0:T(4,128)} %fusion.53, bf16[4,4,2048]{1,0,2:T(4,128)(2,1)S(1)} %bitcast.61, bf16[16,4,1024]{0,1,2:T(4,128)(2,1)} %copy-done.2, f32[16,4]{0,1:T(4,128)S(1)} %copy-done.14), kind=kOutput, calls=%fused_computation.28 | convolution fusion | flops 720896 | bytes 590080 | tf_op jit(solution)/shard_map/swf,rwf->srf/dot_general | solution.py:56
  198.0 1.5 copy.59
  199.5 1.8 fusion.26
  201.9 0.8 copy.60
  (55 shorter events, 5.1 us)
Async XLA Ops:
  6.5 155.1 %all-reduce.3.cloned.1.call-start = ((), (), s32[]{:S(2)}) async-start(), calls=%async_computation | async-start | bytes 1048576 | tf_op jit(solution)/shard_map/psum | solution.py:15
  13.7 35.0 %copy-start.12 = (bf16[4,4,2048]{2,1,0:T(4,128)(2,1)S(1)}, bf16[4,4,2048]{2,1,0:T(4,128)(2,1)}, u32[]{:S(2)}) copy-start(bf16[4,4,2048]{2,1,0:T(4,128)(2,1)} %param.3) | copy-start | bytes 196612
  61.3 52.4 %copy-start.13 = (s32[128,4]{0,1:T(4,128)S(1)}, s32[128,4]{0,1:T(4,128)}, u32[]{:S(2)}) copy-start(s32[128,4]{0,1:T(4,128)} %param.4) | copy-start | bytes 6148
  164.2 2.6 %copy-start.3 = (bf16[16,4,1024]{0,1,2:T(4,128)(2,1)}, bf16[16,4,1024]{0,1,2:T(4,128)(2,1)S(1)}, u32[]{:S(2)}) copy-start(bf16[16,4,1024]{0,1,2:T(4,128)(2,1)S(1)} %copy.45) | copy-start | bytes 393220
  164.2 2.5 %copy-start.8 = (bf16[16,4,1024]{2,0,1:T(8,128)(2,1)S(1)}, bf16[16,4,1024]{2,0,1:T(8,128)(2,1)}, u32[]{:S(2)}) copy-start(bf16[16,4,1024]{2,0,1:T(8,128)(2,1)} %get-tuple-element.10) | copy-start | bytes 393220
  167.4 1.1 copy-start.5
  168.5 2.6 %copy-start.15 = (f32[16,4]{0,1:T(4,128)S(1)}, f32[16,4]{0,1:T(4,128)}, u32[]{:S(2)}) copy-start(f32[16,4]{0,1:T(4,128)} %convolution_maximum_fusion.1) | copy-start | bytes 772
  168.5 2.6 %copy-start.17 = (f32[1024,4,16]{2,1,0:T(4,128)S(1)}, f32[1024,4,16]{2,1,0:T(4,128)}, u32[]{:S(2)}) copy-start(f32[1024,4,16]{2,1,0:T(4,128)} %fusion.50) | copy-start | bytes 786436
  171.1 5.7 %copy-start.4 = (bf16[16,4,1024]{0,1,2:T(4,128)(2,1)S(1)}, bf16[16,4,1024]{0,1,2:T(4,128)(2,1)}, u32[]{:S(2)}) copy-start(bf16[16,4,1024]{0,1,2:T(4,128)(2,1)} %copy-done.3) | copy-start | bytes 393220
  176.8 6.0 %copy-start.7 = (bf16[16,4,1024]{2,0,1:T(8,128)(2,1)S(1)}, bf16[16,4,1024]{2,0,1:T(8,128)(2,1)}, u32[]{:S(2)}) copy-start(bf16[16,4,1024]{2,0,1:T(8,128)(2,1)} %get-tuple-element.22) | copy-start | bytes 393220
  183.5 2.6 %copy-start.2 = (bf16[16,4,1024]{0,1,2:T(4,128)(2,1)}, bf16[16,4,1024]{0,1,2:T(4,128)(2,1)S(1)}, u32[]{:S(2)}) copy-start(bf16[16,4,1024]{0,1,2:T(4,128)(2,1)S(1)} %copy.54) | copy-start | bytes 393220
  183.5 2.5 %copy-start.6 = (bf16[16,4,1024]{2,0,1:T(8,128)(2,1)S(1)}, bf16[16,4,1024]{2,0,1:T(8,128)(2,1)}, u32[]{:S(2)}) copy-start(bf16[16,4,1024]{2,0,1:T(8,128)(2,1)} %get-tuple-element.21) | copy-start | bytes 393220
  186.8 2.6 %copy-start.14 = (f32[16,4]{0,1:T(4,128)S(1)}, f32[16,4]{0,1:T(4,128)}, u32[]{:S(2)}) copy-start(f32[16,4]{0,1:T(4,128)} %convolution_maximum_fusion) | copy-start | bytes 772
  186.8 2.6 %copy-start.16 = (f32[1024,4,16]{2,1,0:T(4,128)S(1)}, f32[1024,4,16]{2,1,0:T(4,128)}, u32[]{:S(2)}) copy-start(f32[1024,4,16]{2,1,0:T(4,128)} %fusion.52) | copy-start | bytes 786436
  193.7 5.8 %copy-start = (bf16[1024,512]{1,0:T(8,128)(2,1)S(1)}, bf16[1024,512]{1,0:T(8,128)(2,1)}, u32[]{:S(2)}) copy-start(bf16[1024,512]{1,0:T(8,128)(2,1)} %get-tuple-element.15) | copy-start | bytes 3145732
  193.7 5.8 %copy-start.9 = (bf16[16,4,1024]{2,0,1:T(8,128)(2,1)S(1)}, bf16[16,4,1024]{2,0,1:T(8,128)(2,1)}, u32[]{:S(2)}) copy-start(bf16[16,4,1024]{2,0,1:T(8,128)(2,1)} %copy.48) | copy-start | bytes 393220
  193.7 5.8 %copy-start.10 = (bf16[16,4,1024]{2,0,1:T(8,128)(2,1)S(1)}, bf16[16,4,1024]{2,0,1:T(8,128)(2,1)}, u32[]{:S(2)}) copy-start(bf16[16,4,1024]{2,0,1:T(8,128)(2,1)} %copy.51) | copy-start | bytes 393220
  199.5 1.8 copy-start.1
  199.5 1.8 copy-start.11
Sparse Core Ops, SparseCore 0:
  113.8 47.8 all-reduce.2
where the time goes:
time: 213 us; the launch traced here: 209 us
  other arithmetic  49.7 us (23%)
  blocking collectives  47 us (22%)
  waiting for transfers between devices  36 us (17%)
  matrix products  33.2 us (16%)
  local copies, waits for them, and re-layouts  24.9 us (12%)
  between operations  18.6 us (9%)
    all_gather x2, blocking collectives, on_device(): gathered = lax.all_gather(source_rows, 'dev', axis=0, tiled=True)  47 us
    another operation x2, other arithmetic  45.1 us
    psum x1, waiting for transfers between devices, broadcast(): return lax.psum(block, axis)  36 us
    dot_general x8, matrix products, paired(): jnp.einsum('swf,rwf->srf', left, right, preferred_element_type=jnp.float32)  24 us
    dynamic_slice x3, local copies, waits for them, and re-layouts, on_device(): source_rows = lax.dynamic_slice_in_dim(masked, within * SRC_DEV, SRC_DEV, 0)  6.29 us
    div x2, local copies, waits for them, and re-layouts, cross_spectra(): real_sum / denom  4.31 us
  transfers between devices with their start and end apart: 1, of which 1 were waited for; matrix products, arithmetic and copies ran while one was open for 6% of the time, Pallas kernels for 0%

commit v1 on v0

v1 whole, which is shorter than its diff:
```python
import functools
import math

import jax
import jax.numpy as jnp
import ml_dtypes
import numpy as np
from jax import lax
from jax.experimental import pallas as pl
from jax.experimental.pallas import tpu as pltpu
from jax.sharding import PartitionSpec as P

NLAG = 512
SRC_DEV = 2
STEPS = 2
RADIX = 16
AXES = ("grp", "dev")
SMEM = pl.BlockSpec(memory_space=pltpu.SMEM)
VMEM = pl.BlockSpec(memory_space=pltpu.VMEM)
AHEAD = pl.CostEstimate(flops=5_000_000_000, bytes_accessed=1_000_000, transcendentals=0)
PARAMS = pltpu.CompilerParams(vmem_limit_bytes=16 * 1024 * 1024)


def bin_order(bin_count):
    per = bin_count // RADIX
    order = []
    for q in range(RADIX // 2):
        for h in range(2):
            order.append(RADIX * np.arange(per) + 2 * q + h + 1)
    return np.concatenate(order)


def tables_kernel(length, table_ref, twiddle_ref):
    points = length // RADIX
    per = points // 2
    row = lax.broadcasted_iota(jnp.int32, (points, points), 0)
    lane = lax.broadcasted_iota(jnp.int32, (points, points), 1)
    phases = (2.0 * math.pi / points) * (row * (lane % per) % points).astype(jnp.float32)
    cosine, sine = jnp.cos(phases), jnp.sin(phases)
    for h in range(2):
        inside = (lane >= per) if h else (lane < per)
        c, s = jnp.where(inside, cosine, 0.0), jnp.where(inside, sine, 0.0)
        for part, values in enumerate(((c, -s), (s, c))):
            rows = slice((2 * h + part) * points, (2 * h + part + 1) * points)
            whole = jnp.concatenate(values, axis=1)
            high = whole.astype(jnp.bfloat16)
            table_ref[0, rows, :] = high
            table_ref[1, rows, :] = (whole - high.astype(jnp.float32)).astype(jnp.bfloat16)
    residue = lax.broadcasted_iota(jnp.int32, (RADIX, points), 0) + 1
    sample = lax.broadcasted_iota(jnp.int32, (RADIX, points), 1)
    phases = (2.0 * math.pi / length) * (residue * sample).astype(jnp.float32)
    twiddle_ref[0] = jnp.cos(phases)
    twiddle_ref[1] = -jnp.sin(phases)


def lag_table(length, bin_count, lag_count):
    bins = bin_order(bin_count)[:, None]
    lags = np.arange(lag_count)[None, :] - lag_count // 2
    phases = 2.0 * np.pi / length * (bins * lags % length)
    factor = 1.0 / math.sqrt(bin_count)
    cosine, sine = np.cos(phases) * factor, -np.sin(phases) * factor
    return np.concatenate([cosine, sine], axis=0).astype(ml_dtypes.bfloat16)


def real_dft(values):
    n = len(values)
    if n == 1:
        return [(values[0], None)]
    if n == 2:
        return [(values[0] + values[1], None), (values[0] - values[1], None)]
    even, odd = real_dft(values[0::2]), real_dft(values[1::2])
    quarter = n // 4
    out = [None] * (n // 2 + 1)
    for r in range(quarter + 1):
        (er, ei), (orr, oi) = even[r], odd[r]
        cosine, sine = math.cos(2 * math.pi * r / n), math.sin(2 * math.pi * r / n)
        if r == 0:
            tr, ti = orr, None
        elif r == quarter:
            tr, ti = None, -orr
        elif 8 * r == n:
            tr, ti = (orr + oi) * cosine, (oi - orr) * cosine
        else:
            tr, ti = orr * cosine + oi * sine, oi * cosine - orr * sine
        plus_re = er if tr is None else er + tr
        minus_re = er if tr is None else er - tr
        if ei is None:
            plus_im, minus_im = ti, ti
        elif ti is None:
            plus_im, minus_im = ei, -ei
        else:
            plus_im, minus_im = ei + ti, ti - ei
        out[r] = (plus_re, plus_im)
        if r < quarter:
            out[n // 2 - r] = (minus_re, minus_im)
    return out


def spectrum(samples, twiddle_ref, table_ref):
    rows, length = samples.shape
    points = length // RADIX
    half = real_dft([samples[:, i * points : (i + 1) * points] for i in range(RADIX)])
    lanes = []
    for residue in range(1, RADIX + 1):
        folded = min(residue, RADIX - residue)
        re, im = half[folded]
        if residue > RADIX // 2 and im is not None:
            im = -im
        cosine = twiddle_ref[0, residue - 1 : residue, :]
        sine = twiddle_ref[1, residue - 1 : residue, :]
        if im is None:
            lanes.append((re * cosine, re * sine))
        else:
            lanes.append((re * cosine - im * sine, re * sine + im * cosine))
    blocks = []
    for q in range(RADIX // 2):
        (ar, ai), (br, bi) = lanes[2 * q], lanes[2 * q + 1]
        blocks.append(jnp.concatenate([ar, ai, br, bi], axis=1))
    stacked = jnp.concatenate(blocks, axis=0)
    high = stacked.astype(jnp.bfloat16)
    low = (stacked - high.astype(jnp.float32)).astype(jnp.bfloat16)
    both = jnp.dot(
        jnp.concatenate([high, low], axis=0), table_ref[0], preferred_element_type=jnp.float32
    )
    count = stacked.shape[0]
    out = both[:count] + both[count:]
    out = out + jnp.dot(high, table_ref[1], preferred_element_type=jnp.float32)
    width = out.shape[1] // 2
    re = [out[q * rows : (q + 1) * rows, :width] for q in range(RADIX // 2)]
    im = [out[q * rows : (q + 1) * rows, width:] for q in range(RADIX // 2)]
    return re, im


def scales(re, im, radius, mask):
    amp = [jnp.sqrt(a * a + b * b) for a, b in zip(re, im)]
    rows, width = amp[0].shape
    per = width // 2
    reach = radius // RADIX
    lane = lax.broadcasted_iota(jnp.int32, (rows, width), 1)
    place = lane % per
    upper = lane >= per
    swapped = [pltpu.roll(a, per, 1) for a in amp]
    pair = [a + b for a, b in zip(amp, swapped)]
    total = pair[0]
    for value in pair[1:]:
        total = total + value

    def shifted(value, by):
        moved = pltpu.roll(value, (-by) % width, 1)
        inside = (place + by >= 0) & (place + by < per)
        return jnp.where(inside, moved, 0.0)

    centre = total
    for by in range(1, reach):
        centre = centre + shifted(total, by) + shifted(total, -by)
    before = jnp.zeros_like(total)
    out = []
    for a, b, both in zip(amp, swapped, pair):
        upto = before + a + jnp.where(upper, b, 0.0)
        before_here = before + jnp.where(upper, b, 0.0)
        onward = total - before_here
        before = before + both
        out.append((upto, onward))
    result = []
    for upto, onward in out:
        summed = centre + shifted(upto, reach) + shifted(onward, -reach)
        result.append(mask / (summed * (1.0 / (2 * radius + 1)) + 1e-06))
    return result


def whiten_rows(samples, radius, mask, twiddle_ref, table_ref, relay_ref, out_ref):
    rows = samples.shape[0]
    blocks = RADIX // 2
    re, im = spectrum(samples, twiddle_ref, table_ref)
    scale = scales(re, im, radius, mask)
    for part, values in enumerate((re, im)):
        for q in range(blocks):
            relay_ref[pl.ds(part * rows * blocks + q, rows, stride=blocks), :] = (
                values[q] * scale[q]
            )
    out_ref[...] = relay_ref[...].astype(jnp.bfloat16)


def holdings(member_bits):
    held = [(0, 0)]
    for bit in member_bits[:-1]:
        held += [(k ^ bit, 1 - odd) for k, odd in held]
    brought = [(k ^ member_bits[-1], 1 - odd) for k, odd in held]
    return held, brought


def panel_order(member_bits):
    held, brought = holdings(member_bits)
    flip = lambda pieces: [(k, 1 - odd) for k, odd in pieces]
    return held + flip(held) + brought + flip(brought)


def prepare_kernel(radius, order, ids_ref, usable_ref, raw_ref, twiddle_ref, table_ref, *rest):
    spectra_ref, inverse_ref, choice_ref, mask_ref, samples, relay = rest
    channels, windows, _ = raw_ref.shape
    halves = channels // SRC_DEV
    groups, members = lax.axis_size("grp"), lax.axis_size("dev")
    group, member = lax.axis_index("grp"), lax.axis_index("dev")
    core = group % SRC_DEV
    first = (group * members + member) * channels
    flags = usable_ref[...].astype(jnp.float32).astype(jnp.bfloat16)
    total = flags.shape[1]

    def flags_of(picks):
        return lax.dot_general(
            picks.astype(jnp.bfloat16), flags, (((1,), (1,)), ((), ())),
            preferred_element_type=jnp.float32,
        )

    def at_window(rows_flags):
        rows = rows_flags.shape[0]
        row = lax.broadcasted_iota(jnp.int32, (rows, windows), 0)
        column = lax.broadcasted_iota(jnp.int32, (rows, windows), 1)
        kept = jnp.where(row % windows == column, rows_flags, 0.0)
        return jnp.sum(kept, axis=1, keepdims=True)

    owning = [ids_ref[t] // halves for t in range(STEPS)]
    within = [ids_ref[t] % halves for t in range(STEPS)]

    for r in range(channels):
        samples[r * windows : (r + 1) * windows, :] = raw_ref[r].astype(jnp.float32)
    rows = channels * windows
    row = lax.broadcasted_iota(jnp.int32, (rows, total), 0)
    lane = lax.broadcasted_iota(jnp.int32, (rows, total), 1)
    own = jnp.where(lane == first + row // windows, 1.0, 0.0)
    mask = at_window(flags_of(own))
    whiten_rows(samples[...], radius, mask, twiddle_ref, table_ref, relay, spectra_ref)

    rows = STEPS * windows
    row = lax.broadcasted_iota(jnp.int32, (rows, total), 0)
    lane = lax.broadcasted_iota(jnp.int32, (rows, total), 1)
    picks = jnp.zeros((rows, total), jnp.float32)
    for t in range(STEPS):
        channel = (owning[t] * members + member) * channels + within[t] * SRC_DEV + core
        picks = jnp.where((row // windows == t) & (lane == channel), 1.0, picks)
    mask_ref[...] = jnp.broadcast_to(at_window(flags_of(picks)), mask_ref.shape)

    row = lax.broadcasted_iota(jnp.int32, choice_ref.shape, 0)
    choice = jnp.zeros(choice_ref.shape, jnp.float32)
    for t in range(STEPS):
        picked = (t * groups + (owning[t] ^ group)) * halves + within[t]
        choice = jnp.where(row == picked, 1.0, choice)
    choice_ref[...] = choice

    rows = STEPS * channels
    row = lax.broadcasted_iota(jnp.int32, (rows, total), 0)
    lane = lax.broadcasted_iota(jnp.int32, (rows, total), 1)
    received = flags_of(jnp.where(lane == first + row % channels, 1.0, 0.0))
    blocks = []
    for k, odd in order:
        picks = jnp.zeros((rows, total), jnp.float32)
        for t in range(STEPS):
            channel = (
                (owning[t] * members + (member ^ k)) * channels
                + within[t] * SRC_DEV
                + (core + odd) % SRC_DEV
            )
            picks = jnp.where((row // channels == t) & (lane == channel), 1.0, picks)
        blocks.append(picks)
    sent = flags_of(jnp.concatenate(blocks, axis=0))
    both = sent * jnp.concatenate([received] * len(order), axis=0)
    counts = jnp.sum(both, axis=1, keepdims=True)
    inverse_ref[...] = jnp.broadcast_to(1.0 / jnp.maximum(counts, 1.0), inverse_ref.shape)


def source_kernel(radius, *refs):
    choice_ref, mask_ref = refs[:2]
    twiddle_ref, table_ref, out_ref, samples, relay = refs[-5:]
    raws = refs[2:-5]
    channels, windows, length = raws[0].shape
    halves = channels // SRC_DEV
    core = lax.axis_index("grp") % SRC_DEV
    points = length // RADIX
    for step in range(STEPS):
        held = [jnp.zeros((windows, points), jnp.float32)] * RADIX
        for k, raw_ref in enumerate(raws):
            for h in range(halves):
                index = (step * len(raws) + k) * halves + h
                here = jnp.broadcast_to(choice_ref[index : index + 1, :], (windows, points)) > 0.0
                row = raw_ref[h * SRC_DEV + core].astype(jnp.float32)
                for n in range(RADIX):
                    held[n] = jnp.where(here, row[:, n * points : (n + 1) * points], held[n])
        for n in range(RADIX):
            samples[step * windows : (step + 1) * windows, n * points : (n + 1) * points] = held[n]
    whiten_rows(samples[...], radius, mask_ref[:, :1], twiddle_ref, table_ref, relay, out_ref)


def lagged_rows(windows, pieces, recv_ref, inverse, table_ref, products, stacked):
    blocks = RADIX // 2
    receivers = recv_ref.shape[0] // (2 * windows * blocks)

    def row_set(ref, base, first, rows):
        out = []
        for part in range(2):
            held = []
            for w in range(0, windows, 2):
                start = base + (part * rows + first + w) * blocks
                both = ref[start : start + 2 * blocks, :].astype(jnp.float32)
                held += [both[:blocks], both[blocks:]]
            out.append(held)
        return out

    own = [row_set(recv_ref, 0, r * windows, receivers * windows) for r in range(receivers)]
    pairs = len(pieces) * STEPS * receivers
    for p, (ref, base) in enumerate(pieces):
        for step in range(STEPS):
            a, b = row_set(ref, base, step * windows, STEPS * windows)
            for r in range(receivers):
                c, e = own[r]
                re = im = None
                for w in range(windows):
                    re_w = a[w] * c[w] + b[w] * e[w]
                    im_w = b[w] * c[w] - a[w] * e[w]
                    re = re_w if re is None else re + re_w
                    im = im_w if im is None else im + im_w
                pair = (p * STEPS + step) * receivers + r
                products[0, pair * blocks : (pair + 1) * blocks, :] = re
                products[1, pair * blocks : (pair + 1) * blocks, :] = im
    width = products.shape[2]
    for part in range(2):
        for q in range(blocks):
            column = (part * blocks + q) * width
            values = products[part, pl.ds(q, pairs, stride=blocks), :] * inverse
            stacked[:, column : column + width] = values.astype(jnp.bfloat16)
    return jnp.dot(stacked[...], table_ref[...], preferred_element_type=jnp.float32)


def pieces_of(ref, windows):
    rows = 2 * STEPS * windows * (RADIX // 2)
    return [(ref, base) for base in range(0, ref.shape[0], rows)]


def part_kernel(windows, first, inverse_ref, recv_ref, table_ref, *refs):
    out_ref, products, stacked = refs[-3:]
    pieces = [piece for ref in refs[:-3] for piece in pieces_of(ref, windows)]
    inverse = inverse_ref[first : first + out_ref.shape[0], :]
    out_ref[...] = lagged_rows(windows, pieces, recv_ref, inverse, table_ref, products, stacked)


def last_kernel(windows, order, inverse_ref, recv_ref, table_ref, piece_ref, *refs):
    out_ref, products, stacked = refs[-3:]
    pieces = pieces_of(piece_ref, windows)
    rows = stacked.shape[0]
    inverse = inverse_ref[inverse_ref.shape[0] - rows :, :]
    member = lax.axis_index("dev")
    core = lax.axis_index("grp") % SRC_DEV
    receivers = out_ref.shape[2]

    def place(rows_ref, some):
        for p, (k, odd) in enumerate(some):
            source = (member ^ k) * SRC_DEV + (core + odd) % SRC_DEV
            for step in range(STEPS):
                pair = (p * STEPS + step) * receivers
                out_ref[step, source] = rows_ref[pair : pair + receivers, :].astype(jnp.bfloat16)

    done = 0
    for ref in refs[:-3]:
        count = ref.shape[0] // (STEPS * receivers)
        place(ref, order[done : done + count])
        done += count
    lagged = lagged_rows(windows, pieces, recv_ref, inverse, table_ref, products, stacked)
    place(lagged, order[done:])


def on_device(records, usable, panel_ids):
    channels, windows, length = records.shape
    bin_count = length // 2
    radius = bin_count // 16
    halves = channels // SRC_DEV
    groups = lax.axis_size("grp")
    members = lax.axis_size("dev")
    blocks = RADIX // 2
    width = bin_count // blocks

    def exchange(value, group_bit, member_bit):
        flip = group_bit * members + member_bit
        pairs = [(i, i ^ flip) for i in range(groups * members)]
        return lax.ppermute(value, AXES, pairs)

    points = length // RADIX
    table, twiddle = pl.pallas_call(
        functools.partial(tables_kernel, length),
        out_shape=[
            jax.ShapeDtypeStruct((2, 4 * points, 2 * points), jnp.bfloat16),
            jax.ShapeDtypeStruct((2, RADIX, points), jnp.float32),
        ],
        in_specs=[],
        out_specs=[VMEM] * 2,
        compiler_params=PARAMS,
        cost_estimate=AHEAD,
        name="short_tables",
    )()
    ltable = jnp.asarray(lag_table(length, bin_count, NLAG))
    member_bits = []
    bit = members // 2
    while bit:
        member_bits.append(bit)
        bit //= 2
    order = panel_order(member_bits)

    raws = {0: records}
    bit = groups // 2
    while bit > 1:
        raws.update({k ^ bit ^ 1: exchange(v, bit ^ 1, 0) for k, v in raws.items()})
        bit //= 2
    raws.update({k ^ 1: exchange(v, 1, 0) for k, v in raws.items()})
    raws = [raws[k] for k in range(groups)]

    row_count = channels * windows
    pairs = len(order) * STEPS * channels
    receivers, inverse, choice, mask = pl.pallas_call(
        functools.partial(prepare_kernel, radius, order),
        out_shape=[
            jax.ShapeDtypeStruct((2 * row_count * blocks, width), jnp.bfloat16),
            jax.ShapeDtypeStruct((pairs, width), jnp.float32),
            jax.ShapeDtypeStruct((STEPS * groups * halves, width), jnp.float32),
            jax.ShapeDtypeStruct((STEPS * windows, width), jnp.float32),
        ],
        in_specs=[SMEM] + [VMEM] * 4,
        out_specs=[VMEM] * 4,
        scratch_shapes=[
            pltpu.VMEM((row_count, length), jnp.float32),
            pltpu.VMEM((2 * row_count * blocks, width), jnp.float32),
        ],
        compiler_params=PARAMS,
        cost_estimate=AHEAD,
        name="receiver_spectra",
    )(panel_ids, usable.T, records, twiddle, table)

    source_rows = STEPS * windows
    piece = pl.pallas_call(
        functools.partial(source_kernel, radius),
        out_shape=jax.ShapeDtypeStruct((2 * source_rows * blocks, width), jnp.bfloat16),
        in_specs=[VMEM] * (groups + 4),
        out_specs=VMEM,
        scratch_shapes=[
            pltpu.VMEM((source_rows, length), jnp.float32),
            pltpu.VMEM((2 * source_rows * blocks, width), jnp.float32),
        ],
        compiler_params=PARAMS,
        name="source_spectra",
    )(choice, mask, *raws, twiddle, table)

    held = piece
    for bit in member_bits[:-1]:
        held = jnp.concatenate([held, exchange(held, 1, bit)], axis=0)
    brought = exchange(held, 1, member_bits[-1])
    held_other = exchange(held, 1, 0)
    brought_other = exchange(brought, 1, 0)

    def part(first, *buffers):
        rows = sum(b.shape[0] for b in buffers) // (2 * windows * blocks) * channels
        return pl.pallas_call(
            functools.partial(part_kernel, windows, first),
            out_shape=jax.ShapeDtypeStruct((rows, NLAG), jnp.float32),
            in_specs=[VMEM] * (3 + len(buffers)),
            out_specs=VMEM,
            scratch_shapes=[
                pltpu.VMEM((2, rows * blocks, width), jnp.float32),
                pltpu.VMEM((rows, 2 * bin_count), jnp.bfloat16),
            ],
            compiler_params=PARAMS,
            name="correlate_part",
        )(inverse, receivers, ltable, *buffers)

    early = part(0, held, held_other)
    middle = part(pairs // 2, brought)
    rows = pairs // 4
    return pl.pallas_call(
        functools.partial(last_kernel, windows, order),
        out_shape=jax.ShapeDtypeStruct(
            (STEPS, members * SRC_DEV, channels, NLAG), jnp.bfloat16
        ),
        in_specs=[VMEM] * 6,
        out_specs=VMEM,
        scratch_shapes=[
            pltpu.VMEM((2, rows * blocks, width), jnp.float32),
            pltpu.VMEM((rows, 2 * bin_count), jnp.bfloat16),
        ],
        compiler_params=PARAMS,
        name="correlate_last",
    )(inverse, receivers, ltable, brought_other, early, middle)


def solution(mesh):
    placed = (P(AXES, None, None), P(), P())
    return jax.shard_map(
        on_device,
        mesh=mesh,
        in_specs=placed,
        out_specs=P(None, None, AXES, None),
        check_vma=False,
    )
```

time: 213 us -> 24.4 us (0.11); the launches traced: 209 us -> 24.3 us
  other arithmetic: 49.7 us -> 0.01 us
  blocking collectives: 47 us -> 0 us
  matrix products: 33.2 us -> 0 us
  local copies, waits for them, and re-layouts: 24.9 us -> 0.01 us
  waiting for transfers between devices: 36 us -> 15.2 us
  between operations: 18.6 us -> 0.06 us
  starting transfers between devices: 0.01 us -> 4.52 us
  Pallas kernels: 0 us -> 4.43 us
    all_gather x2 -> x0, blocking collectives: 47 us -> none  [on_device(): gathered = lax.all_gather(source_rows, 'dev', axis=0, tiled=True)]
    another operation x3 -> x0, other arithmetic: 45.2 us -> none
    psum x1 -> x0, waiting for transfers between devices: 36 us -> none  [broadcast(): return lax.psum(block, axis)]
    dot_general x14 -> x0, matrix products: 33.2 us -> none  [the longest x8 24 us: paired(): jnp.einsum('swf,rwf->srf', left, right, preferred_element_type=jnp.float32)]
    ppermute x0 -> x8, waiting for transfers between devices: none -> 15.2 us  [exchange(): return lax.ppermute(value, AXES, pairs)]
    div x4 -> x0, local copies, waits for them, and re-layouts: 7.99 us -> none  [the longest x2 4.31 us: cross_spectra(): real_sum / denom]
    dynamic_slice x4 -> x0, local copies, waits for them, and re-layouts: 6.3 us -> none  [the longest x3 6.29 us: on_device(): source_rows = lax.dynamic_slice_in_dim(masked, within * SRC_DEV, SRC_DEV, 0)]
    slice x6 -> x0, local copies, waits for them, and re-layouts: 5.88 us -> none  [the longest x3 3.19 us: cross_spectra(): source_re = sources[:, :, :bin_count]]
  transfers between devices with their start and end apart: 1 -> 8, of which waited for: 1 -> 4; matrix products, arithmetic and copies ran while one was open for 6% -> 0% of each run, Pallas kernels for 0% -> 11%
where the time goes in v1:
time: 24.4 us; the launch traced here: 24.3 us
  waiting for transfers between devices  15.2 us (62%)
  starting transfers between devices  4.52 us (19%)
  Pallas kernels  4.43 us (18%)
    ppermute x8, waiting for transfers between devices, exchange(): return lax.ppermute(value, AXES, pairs)  15.2 us
    ppermute x8, starting transfers between devices, exchange(): return lax.ppermute(value, AXES, pairs)  4.52 us
    pallas_call x2, Pallas kernels, part(): pl.pallas_call(functools.partial(part_kernel, windows, first), out_shape=...  1.23 us
    pallas_call x1, Pallas kernels, on_device(): pl.pallas_call(functools.partial(last_kernel, windows, order), out_shape=...  1.19 us
    pallas_call x1, Pallas kernels, on_device(): pl.pallas_call(functools.partial(prepare_kernel, radius, order), out_shap...  1.17 us
  transfers between devices with their start and end apart: 8, of which 4 were waited for; matrix products, arithmetic and copies ran while one was open for 0% of the time, Pallas kernels for 11%

profile of v1, /device:TPU:25, one launch (start us, length us, event | category | flops | bytes accessed | tf_op | source)
XLA Modules:
  0.0 24.3 jit_solution(702050521805872417)
XLA Ops:
  0.0 0.0 copy-start.1
  0.0 0.0 copy-start.3
  0.0 0.0 copy-start.2
  0.0 0.7 %collective-permute-start = (bf16[4,4,2048]{2,1,0:T(4,128)(2,1)}, bf16[4,4,2048]{2,1,0:T(4,128)(2,1)S(1)}, u32[]{:S(2)}, u32[]{:S(2)}) collective-permute-start(bf16[4,4,2048]{2,1,0:T(4,128)(2,1)} %refs_2_.1), channel_id=1, source_target_pairs={{0,8},{1,9},{2,10},{3,11},{4,12},{5,13},{6,14},{7,15},{8,0},{9,1},... | collective-permute-start | bytes 196616 | tf_op jit(solution)/shard_map/ppermute | solution.py:383
  0.8 1.2 %collective-permute-start.1 = (bf16[4,4,2048]{2,1,0:T(4,128)(2,1)}, bf16[4,4,2048]{2,1,0:T(4,128)(2,1)S(1)}, u32[]{:S(2)}, u32[]{:S(2)}) collective-permute-start(bf16[4,4,2048]{2,1,0:T(4,128)(2,1)} %refs_2_.1), channel_id=1, source_target_pairs={{0,24},{1,25},{2,26},{3,27},{4,28},{5,29},{6,30},{7,31},{8,16},{9,... | collective-permute-start | bytes 196616 | tf_op jit(solution)/shard_map/ppermute | solution.py:383
  1.9 0.4 %short_tables.1 = (bf16[2,512,256]{2,1,0:T(8,128)(2,1)S(1)}, f32[2,16,128]{2,1,0:T(8,128)S(1)}) custom-call(), custom_call_target="tpu_custom_call" | custom-call | flops 5000000000 | bytes 1000000 | tf_op jit(solution)/shard_map/short_tables/pallas_call | solution.py:386
  2.3 2.4 %collective-permute-done.1.refs_5_ = bf16[4,4,2048]{2,1,0:T(4,128)(2,1)S(1)} collective-permute-done((bf16[4,4,2048]{2,1,0:T(4,128)(2,1)}, bf16[4,4,2048]{2,1,0:T(4,128)(2,1)S(1)}, u32[]{:S(2)}, u32[]{:S(2)}) %collective-permute-start.1) | collective-permute-done | bytes 65568 | tf_op jit(solution)/shard_map/ppermute | solution.py:383
  4.7 0.1 collective-permute-start.2
  4.9 0.0 copy-done.1
  4.9 0.0 copy-done.3
  4.9 0.0 copy-done.2
  4.9 0.0 copy-start
  4.9 1.2 %receiver_spectra.1 = (bf16[256,128]{1,0:T(8,128)(2,1)S(1)}, f32[128,128]{1,0:T(8,128)S(1)}, f32[16,128]{1,0:T(8,128)S(1)}, f32[8,128]{1,0:T(8,128)S(1)}) custom-call(s32[2]{0:T(128)S(1)} %copy-done.3, s32[4,128]{1,0:T(4,128)S(1)} %bitcast.1, bf16[4,4,2048]{2,1,0:T(4,128)(2,1)S(1)} %copy-done.1, f32[2,16,128]{2,1,0:T(8,128)S(1)} %get-tuple-element.11.twiddle_ref.refs_6_, ...), custom_call_target="tpu_custom_call" | custom-call | flops 5000000000 | bytes 1000000 | tf_op jit(solution)/shard_map/receiver_spectra/pallas_call | solution.py:416
  6.0 0.0 collective-permute-done.refs_3_
  6.1 0.0 collective-permute-done.2.refs_4_
  6.1 0.5 %source_spectra.1 = bf16[128,128]{1,0:T(8,128)(2,1)S(1)} custom-call(f32[16,128]{1,0:T(8,128)S(1)} %get-tuple-element.15.refs_0_, f32[8,128]{1,0:T(8,128)S(1)} %get-tuple-element.16.refs_1_, bf16[4,4,2048]{2,1,0:T(4,128)(2,1)S(1)} %copy-done.1, bf16[4,4,2048]{2,1,0:T(4,128)(2,1)S(1)} %collective-permute-done.refs_3_, ...), custom_call_target="tpu_custom_call" | custom-call | tf_op jit(solution)/shard_map/source_spectra/pallas_call | solution.py:436
  6.5 0.4 %collective-permute-start.3 = (bf16[128,128]{1,0:T(8,128)(2,1)S(1)}, bf16[128,128]{1,0:T(8,128)(2,1)S(1)}, u32[]{:S(2)}, u32[]{:S(2)}) collective-permute-start(bf16[128,128]{1,0:T(8,128)(2,1)S(1)} %source_spectra.1), channel_id=1, source_target_pairs={{0,12},{1,13},{2,14},{3,15},{4,8},{5,9},{6,10},{7,11},{8,4},{9,5},... | collective-permute-start | bytes 98312 | tf_op jit(solution)/shard_map/ppermute | solution.py:383
  6.9 4.8 %collective-permute-done.3 = bf16[128,128]{1,0:T(8,128)(2,1)S(1)} collective-permute-done((bf16[128,128]{1,0:T(8,128)(2,1)S(1)}, bf16[128,128]{1,0:T(8,128)(2,1)S(1)}, u32[]{:S(2)}, u32[]{:S(2)}) %collective-permute-start.3) | collective-permute-done | bytes 32800 | tf_op jit(solution)/shard_map/ppermute | solution.py:383
  11.8 0.0 collective-permute-start.4
  11.8 4.1 %collective-permute-done.4 = bf16[256,128]{1,0:T(8,128)(2,1)S(1)} collective-permute-done((bf16[256,128]{1,0:T(8,128)(2,1)S(1)}, bf16[256,128]{1,0:T(8,128)(2,1)S(1)}, u32[]{:S(2)}, u32[]{:S(2)}) %collective-permute-start.4) | collective-permute-done | bytes 65568 | tf_op jit(solution)/shard_map/ppermute | solution.py:383
  15.9 1.6 %collective-permute-start.5 = (bf16[512,128]{1,0:T(8,128)(2,1)S(1)}, bf16[512,128]{1,0:T(8,128)(2,1)S(1)}, u32[]{:S(2)}, u32[]{:S(2)}) collective-permute-start(bf16[512,128]{1,0:T(8,128)(2,1)S(1)} %pad_maximum_fusion.refs_0_), channel_id=1, source_target_pairs={{0,9},{1,8},{2,11},{3,10},{4,13},{5,12},{6,15},{7,14},{8,1},{9,0},... | collective-permute-start | bytes 393224 | tf_op jit(solution)/shard_map/ppermute | solution.py:383
  17.5 0.1 collective-permute-start.7
  17.6 3.9 %collective-permute-done.5.refs_0_ = bf16[512,128]{1,0:T(8,128)(2,1)S(1)} collective-permute-done((bf16[512,128]{1,0:T(8,128)(2,1)S(1)}, bf16[512,128]{1,0:T(8,128)(2,1)S(1)}, u32[]{:S(2)}, u32[]{:S(2)}) %collective-permute-start.5) | collective-permute-done | bytes 131104 | tf_op jit(solution)/shard_map/ppermute | solution.py:383
  21.4 0.4 %collective-permute-start.6 = (bf16[512,128]{1,0:T(8,128)(2,1)S(1)}, bf16[512,128]{1,0:T(8,128)(2,1)S(1)}, u32[]{:S(2)}, u32[]{:S(2)}) collective-permute-start(bf16[512,128]{1,0:T(8,128)(2,1)S(1)} %collective-permute-done.5.refs_0_), channel_id=1, source_target_pairs={{0,8},{1,9},{2,10},{3,11},{4,12},{5,13},{6,14},{7,15},{8,0},{9,1},... | collective-permute-start | bytes 393224 | tf_op jit(solution)/shard_map/ppermute | solution.py:383
  21.8 0.0 copy-done
  21.8 0.5 %correlate_part.3.refs_1_ = f32[32,512]{1,0:T(8,128)S(1)} custom-call(f32[128,128]{1,0:T(8,128)S(1)} %get-tuple-element.13.inverse_ref, bf16[256,128]{1,0:T(8,128)(2,1)S(1)} %get-tuple-element.14.recv_ref, bf16[2048,512]{1,0:T(8,128)(2,1)S(1)} %copy-done, bf16[512,128]{1,0:T(8,128)(2,1)S(1)} %collective-permute-done.5.refs_0_), custom_call_target="tpu_custom_call" | custom-call | tf_op jit(solution)/shard_map/correlate_part/pallas_call | solution.py:458
  22.3 0.0 collective-permute-done.7.refs_1_
  22.4 0.7 %correlate_part.2.refs_0_ = f32[64,512]{1,0:T(8,128)S(1)} custom-call(f32[128,128]{1,0:T(8,128)S(1)} %get-tuple-element.13.inverse_ref, bf16[256,128]{1,0:T(8,128)(2,1)S(1)} %get-tuple-element.14.recv_ref, bf16[2048,512]{1,0:T(8,128)(2,1)S(1)} %copy-done, bf16[512,128]{1,0:T(8,128)(2,1)S(1)} %pad_maximum_fusion.refs_0_, ...), custom_call_target="tpu_custom_call" | custom-call | tf_op jit(solution)/shard_map/correlate_part/pallas_call | solution.py:458
  23.1 0.0 collective-permute-done.6.piece_ref
  23.1 1.2 %correlate_last.1 = bf16[2,16,4,512]{3,2,1,0:T(4,128)(2,1)} custom-call(f32[128,128]{1,0:T(8,128)S(1)} %get-tuple-element.13.inverse_ref, bf16[256,128]{1,0:T(8,128)(2,1)S(1)} %get-tuple-element.14.recv_ref, bf16[2048,512]{1,0:T(8,128)(2,1)S(1)} %copy-done, bf16[512,128]{1,0:T(8,128)(2,1)S(1)} %collective-permute-done.6.piece_ref, ...), custom_call_target="tpu_custom_call" | custom-call | tf_op jit(solution)/shard_map/correlate_last/pallas_call | solution.py:474
  (2 shorter events, 0.0 us)
Async XLA Ops:
  0.0 4.9 %copy-start.1 = (bf16[4,4,2048]{2,1,0:T(4,128)(2,1)S(1)}, bf16[4,4,2048]{2,1,0:T(4,128)(2,1)}, u32[]{:S(2)}) copy-start(bf16[4,4,2048]{2,1,0:T(4,128)(2,1)} %refs_2_.1) | copy-start | bytes 196612
  0.0 4.9 %copy-start.3 = (s32[2]{0:T(128)S(1)}, s32[2]{0:T(128)}, u32[]{:S(2)}) copy-start(s32[2]{0:T(128)} %ids_ref.1) | copy-start | bytes 28
  0.0 4.9 %copy-start.2 = (s32[128,4]{0,1:T(4,128)S(1)}, s32[128,4]{0,1:T(4,128)}, u32[]{:S(2)}) copy-start(s32[128,4]{0,1:T(4,128)} %param.5) | copy-start | bytes 6148
  0.0 6.0 %collective-permute-start = (bf16[4,4,2048]{2,1,0:T(4,128)(2,1)}, bf16[4,4,2048]{2,1,0:T(4,128)(2,1)S(1)}, u32[]{:S(2)}, u32[]{:S(2)}) collective-permute-start(bf16[4,4,2048]{2,1,0:T(4,128)(2,1)} %refs_2_.1), channel_id=1, source_target_pairs={{0,8},{1,9},{2,10},{3,11},{4,12},{5,13},{6,14},{7,15},{8,0},{9,1},... | collective-permute-start | bytes 196616 | tf_op jit(solution)/shard_map/ppermute | solution.py:383
  0.8 4.0 %collective-permute-start.1 = (bf16[4,4,2048]{2,1,0:T(4,128)(2,1)}, bf16[4,4,2048]{2,1,0:T(4,128)(2,1)S(1)}, u32[]{:S(2)}, u32[]{:S(2)}) collective-permute-start(bf16[4,4,2048]{2,1,0:T(4,128)(2,1)} %refs_2_.1), channel_id=1, source_target_pairs={{0,24},{1,25},{2,26},{3,27},{4,28},{5,29},{6,30},{7,31},{8,16},{9,... | collective-permute-start | bytes 196616 | tf_op jit(solution)/shard_map/ppermute | solution.py:383
  4.7 1.3 %collective-permute-start.2 = (bf16[4,4,2048]{2,1,0:T(4,128)(2,1)S(1)}, bf16[4,4,2048]{2,1,0:T(4,128)(2,1)S(1)}, u32[]{:S(2)}, u32[]{:S(2)}) collective-permute-start(bf16[4,4,2048]{2,1,0:T(4,128)(2,1)S(1)} %collective-permute-done.1.refs_5_), channel_id=1, source_target_pairs={{0,8},{1,9},{2,10},{3,11},{4,12},{5,13},{6,14},{7,15},{8,0},{9,1},... | collective-permute-start | bytes 196616 | tf_op jit(solution)/shard_map/ppermute | solution.py:383
  4.9 17.0 %copy-start = (bf16[2048,512]{1,0:T(8,128)(2,1)S(1)}, bf16[2048,512]{1,0:T(8,128)(2,1)}, u32[]{:S(2)}) copy-start(bf16[2048,512]{1,0:T(8,128)(2,1)} %constant.2.clone.table_ref) | copy-start | bytes 6291460
  6.5 5.2 %collective-permute-start.3 = (bf16[128,128]{1,0:T(8,128)(2,1)S(1)}, bf16[128,128]{1,0:T(8,128)(2,1)S(1)}, u32[]{:S(2)}, u32[]{:S(2)}) collective-permute-start(bf16[128,128]{1,0:T(8,128)(2,1)S(1)} %source_spectra.1), channel_id=1, source_target_pairs={{0,12},{1,13},{2,14},{3,15},{4,8},{5,9},{6,10},{7,11},{8,4},{9,5},... | collective-permute-start | bytes 98312 | tf_op jit(solution)/shard_map/ppermute | solution.py:383
  11.8 4.1 %collective-permute-start.4 = (bf16[256,128]{1,0:T(8,128)(2,1)S(1)}, bf16[256,128]{1,0:T(8,128)(2,1)S(1)}, u32[]{:S(2)}, u32[]{:S(2)}) collective-permute-start(bf16[256,128]{1,0:T(8,128)(2,1)S(1)} %pad_maximum_fusion.1), channel_id=1, source_target_pairs={{0,10},{1,11},{2,8},{3,9},{4,14},{5,15},{6,12},{7,13},{8,2},{9,3},... | collective-permute-start | bytes 196616 | tf_op jit(solution)/shard_map/ppermute | solution.py:383
  15.9 5.6 %collective-permute-start.5 = (bf16[512,128]{1,0:T(8,128)(2,1)S(1)}, bf16[512,128]{1,0:T(8,128)(2,1)S(1)}, u32[]{:S(2)}, u32[]{:S(2)}) collective-permute-start(bf16[512,128]{1,0:T(8,128)(2,1)S(1)} %pad_maximum_fusion.refs_0_), channel_id=1, source_target_pairs={{0,9},{1,8},{2,11},{3,10},{4,13},{5,12},{6,15},{7,14},{8,1},{9,0},... | collective-permute-start | bytes 393224 | tf_op jit(solution)/shard_map/ppermute | solution.py:383
  17.5 4.9 %collective-permute-start.7 = (bf16[512,128]{1,0:T(8,128)(2,1)S(1)}, bf16[512,128]{1,0:T(8,128)(2,1)S(1)}, u32[]{:S(2)}, u32[]{:S(2)}) collective-permute-start(bf16[512,128]{1,0:T(8,128)(2,1)S(1)} %pad_maximum_fusion.refs_0_), channel_id=1, source_target_pairs={{0,8},{1,9},{2,10},{3,11},{4,12},{5,13},{6,14},{7,15},{8,0},{9,1},... | collective-permute-start | bytes 393224 | tf_op jit(solution)/shard_map/ppermute | solution.py:383
  21.4 1.6 %collective-permute-start.6 = (bf16[512,128]{1,0:T(8,128)(2,1)S(1)}, bf16[512,128]{1,0:T(8,128)(2,1)S(1)}, u32[]{:S(2)}, u32[]{:S(2)}) collective-permute-start(bf16[512,128]{1,0:T(8,128)(2,1)S(1)} %collective-permute-done.5.refs_0_), channel_id=1, source_target_pairs={{0,8},{1,9},{2,10},{3,11},{4,12},{5,13},{6,14},{7,15},{8,0},{9,1},... | collective-permute-start | bytes 393224 | tf_op jit(solution)/shard_map/ppermute | solution.py:383

commit v2 on v1

--- a/solution.py
+++ b/solution.py
@@ -18,6 +18,7 @@
 SMEM = pl.BlockSpec(memory_space=pltpu.SMEM)
 VMEM = pl.BlockSpec(memory_space=pltpu.VMEM)
 AHEAD = pl.CostEstimate(flops=5_000_000_000, bytes_accessed=1_000_000, transcendentals=0)
+BESIDE = pl.CostEstimate(flops=1_000_000_000, bytes_accessed=1_000_000, transcendentals=0)
 PARAMS = pltpu.CompilerParams(vmem_limit_bytes=16 * 1024 * 1024)
 
 
@@ -195,41 +196,38 @@
     return held + flip(held) + brought + flip(brought)
 
 
-def prepare_kernel(radius, order, ids_ref, usable_ref, raw_ref, twiddle_ref, table_ref, *rest):
-    spectra_ref, inverse_ref, choice_ref, mask_ref, samples, relay = rest
-    channels, windows, _ = raw_ref.shape
-    halves = channels // SRC_DEV
-    groups, members = lax.axis_size("grp"), lax.axis_size("dev")
+def flags_of(picks, flags):
+    return lax.dot_general(
+        picks.astype(jnp.bfloat16),
+        flags,
+        (((1,), (1,)), ((), ())),
+        preferred_element_type=jnp.float32,
+    )
+
+
+def at_window(rows_flags):
+    row = lax.broadcasted_iota(jnp.int32, rows_flags.shape, 0)
+    column = lax.broadcasted_iota(jnp.int32, rows_flags.shape, 1)
+    kept = jnp.where(row % rows_flags.shape[1] == column, rows_flags, 0.0)
+    return jnp.sum(kept, axis=1, keepdims=True)
+
+
+def choice_kernel(halves, channels, ids_ref, usable_ref, after_ref, choice_ref, mask_ref, take_ref):
+    del after_ref
+    windows, total = usable_ref.shape
+    members = lax.axis_size("dev")
     group, member = lax.axis_index("grp"), lax.axis_index("dev")
-    core = group % SRC_DEV
-    first = (group * members + member) * channels
+    core, plane = group % SRC_DEV, group // SRC_DEV
     flags = usable_ref[...].astype(jnp.float32).astype(jnp.bfloat16)
-    total = flags.shape[1]
-
-    def flags_of(picks):
-        return lax.dot_general(
-            picks.astype(jnp.bfloat16), flags, (((1,), (1,)), ((), ())),
-            preferred_element_type=jnp.float32,
-        )
-
-    def at_window(rows_flags):
-        rows = rows_flags.shape[0]
-        row = lax.broadcasted_iota(jnp.int32, (rows, windows), 0)
-        column = lax.broadcasted_iota(jnp.int32, (rows, windows), 1)
-        kept = jnp.where(row % windows == column, rows_flags, 0.0)
-        return jnp.sum(kept, axis=1, keepdims=True)
-
     owning = [ids_ref[t] // halves for t in range(STEPS)]
     within = [ids_ref[t] % halves for t in range(STEPS)]
 
-    for r in range(channels):
-        samples[r * windows : (r + 1) * windows, :] = raw_ref[r].astype(jnp.float32)
-    rows = channels * windows
-    row = lax.broadcasted_iota(jnp.int32, (rows, total), 0)
-    lane = lax.broadcasted_iota(jnp.int32, (rows, total), 1)
-    own = jnp.where(lane == first + row // windows, 1.0, 0.0)
-    mask = at_window(flags_of(own))
-    whiten_rows(samples[...], radius, mask, twiddle_ref, table_ref, relay, spectra_ref)
+    row = lax.broadcasted_iota(jnp.int32, choice_ref.shape, 0)
+    choice = jnp.zeros(choice_ref.shape, jnp.float32)
+    for t in range(STEPS):
+        apart = (owning[t] + core) % SRC_DEV
+        choice = jnp.where(row == (t * SRC_DEV + apart) * halves + within[t], 1.0, choice)
+    choice_ref[...] = choice
 
     rows = STEPS * windows
     row = lax.broadcasted_iota(jnp.int32, (rows, total), 0)
@@ -238,19 +236,62 @@
     for t in range(STEPS):
         channel = (owning[t] * members + member) * channels + within[t] * SRC_DEV + core
         picks = jnp.where((row // windows == t) & (lane == channel), 1.0, picks)
-    mask_ref[...] = jnp.broadcast_to(at_window(flags_of(picks)), mask_ref.shape)
-
-    row = lax.broadcasted_iota(jnp.int32, choice_ref.shape, 0)
-    choice = jnp.zeros(choice_ref.shape, jnp.float32)
-    for t in range(STEPS):
-        picked = (t * groups + (owning[t] ^ group)) * halves + within[t]
-        choice = jnp.where(row == picked, 1.0, choice)
-    choice_ref[...] = choice
+    mask_ref[...] = jnp.broadcast_to(at_window(flags_of(picks, flags)), mask_ref.shape)
+
+    row = lax.broadcasted_iota(jnp.int32, take_ref.shape[1:], 0)
+    for index in range(take_ref.shape[0]):
+        take = jnp.zeros(take_ref.shape[1:], jnp.float32)
+        for t in range(STEPS):
+            differs = ((owning[t] // SRC_DEV) ^ plane) >> index & 1
+            take = jnp.where(row // windows == t, differs.astype(jnp.float32), take)
+        take_ref[index] = take
+
+
+def pick_kernel(flip, choice_ref, own_ref, other_ref, out_ref, samples):
+    channels, windows, length = own_ref.shape
+    halves = channels // SRC_DEV
+    half = (lax.axis_index("grp") + flip) % SRC_DEV
+    points = length // RADIX
+    for step in range(STEPS):
+        held = [jnp.zeros((windows, points), jnp.float32)] * RADIX
+        for k, raw_ref in enumerate((own_ref, other_ref)):
+            for h in range(halves):
+                index = (step * SRC_DEV + k) * halves + h
+                here = jnp.broadcast_to(choice_ref[index : index + 1, :], (windows, points)) > 0.0
+                row = raw_ref[h * SRC_DEV + half].astype(jnp.float32)
+                for n in range(RADIX):
+                    held[n] = jnp.where(here, row[:, n * points : (n + 1) * points], held[n])
+        for n in range(RADIX):
+            samples[step * windows : (step + 1) * windows, n * points : (n + 1) * points] = held[n]
+    out_ref[...] = samples[...].astype(out_ref.dtype)
+
+
+def receiver_kernel(radius, order, ids_ref, usable_ref, raw_ref, twiddle_ref, table_ref, *rest):
+    spectra_ref, inverse_ref, samples, relay = rest
+    channels, windows, _ = raw_ref.shape
+    halves = channels // SRC_DEV
+    members = lax.axis_size("dev")
+    group, member = lax.axis_index("grp"), lax.axis_index("dev")
+    core = group % SRC_DEV
+    first = (group * members + member) * channels
+    flags = usable_ref[...].astype(jnp.float32).astype(jnp.bfloat16)
+    total = flags.shape[1]
+    owning = [ids_ref[t] // halves for t in range(STEPS)]
+    within = [ids_ref[t] % halves for t in range(STEPS)]
+
+    for r in range(channels):
+        samples[r * windows : (r + 1) * windows, :] = raw_ref[r].astype(jnp.float32)
+    rows = channels * windows
+    row = lax.broadcasted_iota(jnp.int32, (rows, total), 0)
+    lane = lax.broadcasted_iota(jnp.int32, (rows, total), 1)
+    own = jnp.where(lane == first + row // windows, 1.0, 0.0)
+    mask = at_window(flags_of(own, flags))
+    whiten_rows(samples[...], radius, mask, twiddle_ref, table_ref, relay, spectra_ref)
 
     rows = STEPS * channels
     row = lax.broadcasted_iota(jnp.int32, (rows, total), 0)
     lane = lax.broadcasted_iota(jnp.int32, (rows, total), 1)
-    received = flags_of(jnp.where(lane == first + row % channels, 1.0, 0.0))
+    received = flags_of(jnp.where(lane == first + row % channels, 1.0, 0.0), flags)
     blocks = []
     for k, odd in order:
         picks = jnp.zeros((rows, total), jnp.float32)
@@ -262,32 +303,22 @@
             )
             picks = jnp.where((row // channels == t) & (lane == channel), 1.0, picks)
         blocks.append(picks)
-    sent = flags_of(jnp.concatenate(blocks, axis=0))
+    sent = flags_of(jnp.concatenate(blocks, axis=0), flags)
     both = sent * jnp.concatenate([received] * len(order), axis=0)
     counts = jnp.sum(both, axis=1, keepdims=True)
     inverse_ref[...] = jnp.broadcast_to(1.0 / jnp.maximum(counts, 1.0), inverse_ref.shape)
 
 
 def source_kernel(radius, *refs):
-    choice_ref, mask_ref = refs[:2]
-    twiddle_ref, table_ref, out_ref, samples, relay = refs[-5:]
-    raws = refs[2:-5]
-    channels, windows, length = raws[0].shape
-    halves = channels // SRC_DEV
-    core = lax.axis_index("grp") % SRC_DEV
+    take_ref, mask_ref, kept_ref, came_ref, twiddle_ref, table_ref = refs[:6]
+    out_ref, relay = refs[-2:]
+    rows, length = kept_ref.shape
     points = length // RADIX
-    for step in range(STEPS):
-        held = [jnp.zeros((windows, points), jnp.float32)] * RADIX
-        for k, raw_ref in enumerate(raws):
-            for h in range(halves):
-                index = (step * len(raws) + k) * halves + h
-                here = jnp.broadcast_to(choice_ref[index : index + 1, :], (windows, points)) > 0.0
-                row = raw_ref[h * SRC_DEV + core].astype(jnp.float32)
-                for n in range(RADIX):
-                    held[n] = jnp.where(here, row[:, n * points : (n + 1) * points], held[n])
-        for n in range(RADIX):
-            samples[step * windows : (step + 1) * windows, n * points : (n + 1) * points] = held[n]
-    whiten_rows(samples[...], radius, mask_ref[:, :1], twiddle_ref, table_ref, relay, out_ref)
+    here = take_ref[...] > 0.0
+    kept, came = kept_ref[...].astype(jnp.float32), came_ref[...].astype(jnp.float32)
+    here = jnp.concatenate([here] * RADIX, axis=1)
+    samples = jnp.where(here, came, kept)
+    whiten_rows(samples, radius, mask_ref[:, :1], twiddle_ref, table_ref, relay, out_ref)
 
 
 def lagged_rows(windows, pieces, recv_ref, inverse, table_ref, products, stacked):
@@ -403,26 +434,52 @@
         bit //= 2
     order = panel_order(member_bits)
 
-    raws = {0: records}
-    bit = groups // 2
-    while bit > 1:
-        raws.update({k ^ bit ^ 1: exchange(v, bit ^ 1, 0) for k, v in raws.items()})
-        bit //= 2
-    raws.update({k ^ 1: exchange(v, 1, 0) for k, v in raws.items()})
-    raws = [raws[k] for k in range(groups)]
+    usable_rows = usable.T
+    planes = groups // SRC_DEV
+    source_rows = STEPS * windows
+    plane_bits = planes.bit_length() - 1
+
+    records_other = exchange(records, 1, 0)
+    choice, mask, take = pl.pallas_call(
+        functools.partial(choice_kernel, halves, channels),
+        out_shape=[
+            jax.ShapeDtypeStruct((STEPS * SRC_DEV * halves, width), jnp.float32),
+            jax.ShapeDtypeStruct((source_rows, width), jnp.float32),
+            jax.ShapeDtypeStruct((plane_bits, source_rows, width), jnp.float32),
+        ],
+        in_specs=[SMEM] + [VMEM] * 2,
+        out_specs=[VMEM] * 3,
+        compiler_params=PARAMS,
+        name="choose_rows",
+    )(panel_ids, usable_rows, twiddle)
+
+    def pick(flip):
+        return pl.pallas_call(
+            functools.partial(pick_kernel, flip),
+            out_shape=jax.ShapeDtypeStruct((source_rows, length), records.dtype),
+            in_specs=[VMEM] * 3,
+            out_specs=VMEM,
+            scratch_shapes=[pltpu.VMEM((source_rows, length), jnp.float32)],
+            compiler_params=PARAMS,
+            name="pick_rows",
+        )(choice, records, records_other)
+
+    came = exchange(pick(1), SRC_DEV * (planes // 2) + 1, 0)
+    kept = pick(0)
+    for index in range(plane_bits - 2, -1, -1):
+        kept = jnp.where(take[index + 1][:, :1] > 0.0, came, kept)
+        came = exchange(kept, SRC_DEV << index, 0)
 
     row_count = channels * windows
     pairs = len(order) * STEPS * channels
-    receivers, inverse, choice, mask = pl.pallas_call(
-        functools.partial(prepare_kernel, radius, order),
+    receivers, inverse = pl.pallas_call(
+        functools.partial(receiver_kernel, radius, order),
         out_shape=[
             jax.ShapeDtypeStruct((2 * row_count * blocks, width), jnp.bfloat16),
             jax.ShapeDtypeStruct((pairs, width), jnp.float32),
-            jax.ShapeDtypeStruct((STEPS * groups * halves, width), jnp.float32),
-            jax.ShapeDtypeStruct((STEPS * windows, width), jnp.float32),
         ],
         in_specs=[SMEM] + [VMEM] * 4,
-        out_specs=[VMEM] * 4,
+        out_specs=[VMEM] * 2,
         scratch_shapes=[
             pltpu.VMEM((row_count, length), jnp.float32),
             pltpu.VMEM((2 * row_count * blocks, width), jnp.float32),
@@ -430,21 +487,17 @@
         compiler_params=PARAMS,
         cost_estimate=AHEAD,
         name="receiver_spectra",
-    )(panel_ids, usable.T, records, twiddle, table)
-
-    source_rows = STEPS * windows
+    )(panel_ids, usable_rows, records, twiddle, table)
+
     piece = pl.pallas_call(
         functools.partial(source_kernel, radius),
         out_shape=jax.ShapeDtypeStruct((2 * source_rows * blocks, width), jnp.bfloat16),
-        in_specs=[VMEM] * (groups + 4),
+        in_specs=[VMEM] * 7,
         out_specs=VMEM,
-        scratch_shapes=[
-            pltpu.VMEM((source_rows, length), jnp.float32),
-            pltpu.VMEM((2 * source_rows * blocks, width), jnp.float32),
-        ],
+        scratch_shapes=[pltpu.VMEM((2 * source_rows * blocks, width), jnp.float32)],
         compiler_params=PARAMS,
         name="source_spectra",
-    )(choice, mask, *raws, twiddle, table)
+    )(take[0], mask, kept, came, twiddle, table, inverse)
 
     held = piece
     for bit in member_bits[:-1]:
@@ -453,7 +506,7 @@
     held_other = exchange(held, 1, 0)
     brought_other = exchange(brought, 1, 0)
 
-    def part(first, *buffers):
+    def part(first, cost, *buffers):
         rows = sum(b.shape[0] for b in buffers) // (2 * windows * blocks) * channels
         return pl.pallas_call(
             functools.partial(part_kernel, windows, first),
@@ -465,11 +518,12 @@
                 pltpu.VMEM((rows, 2 * bin_count), jnp.bfloat16),
             ],
             compiler_params=PARAMS,
+            cost_estimate=cost,
             name="correlate_part",
         )(inverse, receivers, ltable, *buffers)
 
-    early = part(0, held, held_other)
-    middle = part(pairs // 2, brought)
+    early = part(0, BESIDE, held, held_other)
+    middle = part(pairs // 2, BESIDE, brought)
     rows = pairs // 4
     return pl.pallas_call(
         functools.partial(last_kernel, windows, order),

time: 24.4 us -> 23.5 us (0.963)
  waiting for transfers between devices: 15.2 us -> 13.5 us
  Pallas kernels: 4.43 us -> 5.22 us
    ppermute x8 -> x7, waiting for transfers between devices: 15.2 us -> 13.5 us  [exchange(): return lax.ppermute(value, AXES, pairs)]
    pallas_call x1 -> x4, Pallas kernels: 1.17 us -> 2.01 us  [the longest x1 1.15 us: on_device(): pl.pallas_call(functools.partial(receiver_kernel, radius, order), out_sha...]
    ppermute x8 -> x7, starting transfers between devices: 4.52 us -> 4.58 us  [exchange(): return lax.ppermute(value, AXES, pairs)]
  transfers between devices with their start and end apart: 8 -> 7, of which waited for: 4 -> 4; matrix products, arithmetic and copies ran while one was open for 0% -> 0% of each run, Pallas kernels for 11% -> 15%
where the time goes in v2:
time: 23.5 us; the launch traced here: 23.4 us
  waiting for transfers between devices  13.5 us (57%)
  Pallas kernels  5.22 us (22%)
  starting transfers between devices  4.58 us (19%)
    ppermute x7, waiting for transfers between devices, exchange(): return lax.ppermute(value, AXES, pairs)  13.5 us
    ppermute x7, starting transfers between devices, exchange(): return lax.ppermute(value, AXES, pairs)  4.58 us
    pallas_call x2, Pallas kernels, part(): pl.pallas_call(functools.partial(part_kernel, windows, first), out_shape=...  1.23 us
    pallas_call x1, Pallas kernels, on_device(): pl.pallas_call(functools.partial(last_kernel, windows, order), out_shape=...  1.19 us
    pallas_call x1, Pallas kernels, on_device(): pl.pallas_call(functools.partial(receiver_kernel, radius, order), out_sha...  1.15 us
    pallas_call x1, Pallas kernels, on_device(): pl.pallas_call(functools.partial(choice_kernel, halves, channels), out_sh...  0.77 us
  transfers between devices with their start and end apart: 7, of which 4 were waited for; matrix products, arithmetic and copies ran while one was open for 0% of the time, Pallas kernels for 15%

profile of v2, /device:TPU:25, one launch (start us, length us, event | category | flops | bytes accessed | tf_op | source)
XLA Modules:
  0.0 23.4 jit_solution(3246846933129538969)
XLA Ops:
  0.0 0.0 copy-start.1
  0.0 0.0 copy-start.3
  0.0 0.0 copy-start.2
  0.0 0.7 %collective-permute-start = (bf16[4,4,2048]{2,1,0:T(4,128)(2,1)}, bf16[4,4,2048]{2,1,0:T(4,128)(2,1)S(1)}, u32[]{:S(2)}, u32[]{:S(2)}) collective-permute-start(bf16[4,4,2048]{2,1,0:T(4,128)(2,1)} %own_ref.3), channel_id=1, source_target_pairs={{0,8},{1,9},{2,10},{3,11},{4,12},{5,13},{6,14},{7,15},{8,0},{9,1},... | collective-permute-start | bytes 196616 | tf_op jit(solution)/shard_map/ppermute | solution.py:414
  0.8 0.4 %short_tables.1 = (bf16[2,512,256]{2,1,0:T(8,128)(2,1)S(1)}, f32[2,16,128]{2,1,0:T(8,128)S(1)}) custom-call(), custom_call_target="tpu_custom_call" | custom-call | flops 5000000000 | bytes 1000000 | tf_op jit(solution)/shard_map/short_tables/pallas_call | solution.py:417
  1.1 0.0 copy-done.3
  1.1 0.0 copy-done.2
  1.2 0.8 %choose_rows.1 = (f32[8,128]{1,0:T(8,128)S(1)}, f32[8,128]{1,0:T(8,128)S(1)}, f32[1,8,128]{2,1,0:T(8,128)S(1)}) custom-call(s32[2]{0:T(128)S(1)} %copy-done.3, s32[4,128]{1,0:T(4,128)S(1)} %bitcast.3, f32[2,16,128]{2,1,0:T(8,128)S(1)} %get-tuple-element.12.twiddle_ref.after_ref.refs_4_), custom_call_target="tpu_custom_call" | custom-call | tf_op jit(solution)/shard_map/choose_rows/pallas_call | solution.py:443
  1.9 0.0 collective-permute-done.other_ref
  1.9 0.0 copy-done.1
  2.0 1.5 %collective-permute-start.1 = (bf16[8,2048]{1,0:T(8,128)(2,1)S(1)}, bf16[8,2048]{1,0:T(8,128)(2,1)S(1)}, u32[]{:S(2)}, u32[]{:S(2)}) collective-permute-start(bf16[8,2048]{1,0:T(8,128)(2,1)S(1)} %pick_rows.3), channel_id=1, source_target_pairs={{0,24},{1,25},{2,26},{3,27},{4,28},{5,29},{6,30},{7,31},{8,16},{9,... | collective-permute-start | bytes 98312 | tf_op jit(solution)/shard_map/ppermute | solution.py:414
  3.4 0.0 copy-start
  3.4 1.1 %receiver_spectra.1 = (bf16[256,128]{1,0:T(8,128)(2,1)S(1)}, f32[128,128]{1,0:T(8,128)S(1)}) custom-call(s32[2]{0:T(128)S(1)} %copy-done.3, s32[4,128]{1,0:T(4,128)S(1)} %bitcast.4, bf16[4,4,2048]{2,1,0:T(4,128)(2,1)S(1)} %copy-done.1, f32[2,16,128]{2,1,0:T(8,128)S(1)} %get-tuple-element.12.twiddle_ref.after_ref.refs_4_, ...), custom_call_target="tpu_custom_call" | custom-call | flops 5000000000 | bytes 1000000 | tf_op jit(solution)/shard_map/receiver_spectra/pallas_call | solution.py:475
  4.6 0.1 pick_rows.2.refs_2_
  4.6 0.7 %collective-permute-done.1.refs_3_ = bf16[8,2048]{1,0:T(8,128)(2,1)S(1)} collective-permute-done((bf16[8,2048]{1,0:T(8,128)(2,1)S(1)}, bf16[8,2048]{1,0:T(8,128)(2,1)S(1)}, u32[]{:S(2)}, u32[]{:S(2)}) %collective-permute-start.1) | collective-permute-done | bytes 32800 | tf_op jit(solution)/shard_map/ppermute | solution.py:414
  5.4 0.4 %source_spectra.1 = bf16[128,128]{1,0:T(8,128)(2,1)S(1)} custom-call(f32[8,128]{1,0:T(8,128)S(1)} %bitcast.2, f32[8,128]{1,0:T(8,128)S(1)} %get-tuple-element.17.refs_1_, bf16[8,2048]{1,0:T(8,128)(2,1)S(1)} %pick_rows.2.refs_2_, bf16[8,2048]{1,0:T(8,128)(2,1)S(1)} %collective-permute-done.1.refs_3_, ...), custom_call_target="tpu_custom_call" | custom-call | tf_op jit(solution)/shard_map/source_spectra/pallas_call | solution.py:492
  5.8 0.3 %collective-permute-start.2 = (bf16[128,128]{1,0:T(8,128)(2,1)S(1)}, bf16[128,128]{1,0:T(8,128)(2,1)S(1)}, u32[]{:S(2)}, u32[]{:S(2)}) collective-permute-start(bf16[128,128]{1,0:T(8,128)(2,1)S(1)} %source_spectra.1), channel_id=1, source_target_pairs={{0,12},{1,13},{2,14},{3,15},{4,8},{5,9},{6,10},{7,11},{8,4},{9,5},... | collective-permute-start | bytes 98312 | tf_op jit(solution)/shard_map/ppermute | solution.py:414
  6.1 4.8 %collective-permute-done.2 = bf16[128,128]{1,0:T(8,128)(2,1)S(1)} collective-permute-done((bf16[128,128]{1,0:T(8,128)(2,1)S(1)}, bf16[128,128]{1,0:T(8,128)(2,1)S(1)}, u32[]{:S(2)}, u32[]{:S(2)}) %collective-permute-start.2) | collective-permute-done | bytes 32800 | tf_op jit(solution)/shard_map/ppermute | solution.py:414
  10.9 0.0 collective-permute-start.3
  10.9 4.1 %collective-permute-done.3 = bf16[256,128]{1,0:T(8,128)(2,1)S(1)} collective-permute-done((bf16[256,128]{1,0:T(8,128)(2,1)S(1)}, bf16[256,128]{1,0:T(8,128)(2,1)S(1)}, u32[]{:S(2)}, u32[]{:S(2)}) %collective-permute-start.3) | collective-permute-done | bytes 65568 | tf_op jit(solution)/shard_map/ppermute | solution.py:414
  15.0 1.6 %collective-permute-start.4 = (bf16[512,128]{1,0:T(8,128)(2,1)S(1)}, bf16[512,128]{1,0:T(8,128)(2,1)S(1)}, u32[]{:S(2)}, u32[]{:S(2)}) collective-permute-start(bf16[512,128]{1,0:T(8,128)(2,1)S(1)} %pad_maximum_fusion.refs_0_), channel_id=1, source_target_pairs={{0,9},{1,8},{2,11},{3,10},{4,13},{5,12},{6,15},{7,14},{8,1},{9,0},... | collective-permute-start | bytes 393224 | tf_op jit(solution)/shard_map/ppermute | solution.py:414
  16.6 0.1 collective-permute-start.6
  16.7 3.9 %collective-permute-done.4.refs_0_ = bf16[512,128]{1,0:T(8,128)(2,1)S(1)} collective-permute-done((bf16[512,128]{1,0:T(8,128)(2,1)S(1)}, bf16[512,128]{1,0:T(8,128)(2,1)S(1)}, u32[]{:S(2)}, u32[]{:S(2)}) %collective-permute-start.4) | collective-permute-done | bytes 131104 | tf_op jit(solution)/shard_map/ppermute | solution.py:414
  20.6 0.4 %collective-permute-start.5 = (bf16[512,128]{1,0:T(8,128)(2,1)S(1)}, bf16[512,128]{1,0:T(8,128)(2,1)S(1)}, u32[]{:S(2)}, u32[]{:S(2)}) collective-permute-start(bf16[512,128]{1,0:T(8,128)(2,1)S(1)} %collective-permute-done.4.refs_0_), channel_id=1, source_target_pairs={{0,8},{1,9},{2,10},{3,11},{4,12},{5,13},{6,14},{7,15},{8,0},{9,1},... | collective-permute-start | bytes 393224 | tf_op jit(solution)/shard_map/ppermute | solution.py:414
  20.9 0.0 copy-done
  20.9 0.5 %correlate_part.3.refs_1_ = f32[32,512]{1,0:T(8,128)S(1)} custom-call(f32[128,128]{1,0:T(8,128)S(1)} %get-tuple-element.14.refs_6_.inverse_ref, bf16[256,128]{1,0:T(8,128)(2,1)S(1)} %get-tuple-element.15.recv_ref, bf16[2048,512]{1,0:T(8,128)(2,1)S(1)} %copy-done, bf16[512,128]{1,0:T(8,128)(2,1)S(1)} %collective-permute-done.4.refs_0_), custom_call_target="tpu_custom_call" | custom-call | flops 1000000000 | bytes 1000000 | tf_op jit(solution)/shard_map/correlate_part/pallas_call | solution.py:511
  21.5 0.0 collective-permute-done.6.refs_1_
  21.5 0.7 %correlate_part.2.refs_0_ = f32[64,512]{1,0:T(8,128)S(1)} custom-call(f32[128,128]{1,0:T(8,128)S(1)} %get-tuple-element.14.refs_6_.inverse_ref, bf16[256,128]{1,0:T(8,128)(2,1)S(1)} %get-tuple-element.15.recv_ref, bf16[2048,512]{1,0:T(8,128)(2,1)S(1)} %copy-done, bf16[512,128]{1,0:T(8,128)(2,1)S(1)} %pad_maximum_fusion.refs_0_, ...), custom_call_target="tpu_custom_call" | custom-call | flops 1000000000 | bytes 1000000 | tf_op jit(solution)/shard_map/correlate_part/pallas_call | solution.py:511
  22.2 0.0 collective-permute-done.5.piece_ref
  22.2 1.2 %correlate_last.1 = bf16[2,16,4,512]{3,2,1,0:T(4,128)(2,1)} custom-call(f32[128,128]{1,0:T(8,128)S(1)} %get-tuple-element.14.refs_6_.inverse_ref, bf16[256,128]{1,0:T(8,128)(2,1)S(1)} %get-tuple-element.15.recv_ref, bf16[2048,512]{1,0:T(8,128)(2,1)S(1)} %copy-done, bf16[512,128]{1,0:T(8,128)(2,1)S(1)} %collective-permute-done.5.piece_ref, ...), custom_call_target="tpu_custom_call" | custom-call | tf_op jit(solution)/shard_map/correlate_last/pallas_call | solution.py:528
  (3 shorter events, 0.1 us)
Async XLA Ops:
  0.0 1.9 %copy-start.1 = (bf16[4,4,2048]{2,1,0:T(4,128)(2,1)S(1)}, bf16[4,4,2048]{2,1,0:T(4,128)(2,1)}, u32[]{:S(2)}) copy-start(bf16[4,4,2048]{2,1,0:T(4,128)(2,1)} %own_ref.3) | copy-start | bytes 196612
  0.0 1.1 %copy-start.3 = (s32[2]{0:T(128)S(1)}, s32[2]{0:T(128)}, u32[]{:S(2)}) copy-start(s32[2]{0:T(128)} %ids_ref.3) | copy-start | bytes 28
  0.0 1.1 %copy-start.2 = (s32[128,4]{0,1:T(4,128)S(1)}, s32[128,4]{0,1:T(4,128)}, u32[]{:S(2)}) copy-start(s32[128,4]{0,1:T(4,128)} %param.5) | copy-start | bytes 6148
  0.0 1.9 %collective-permute-start = (bf16[4,4,2048]{2,1,0:T(4,128)(2,1)}, bf16[4,4,2048]{2,1,0:T(4,128)(2,1)S(1)}, u32[]{:S(2)}, u32[]{:S(2)}) collective-permute-start(bf16[4,4,2048]{2,1,0:T(4,128)(2,1)} %own_ref.3), channel_id=1, source_target_pairs={{0,8},{1,9},{2,10},{3,11},{4,12},{5,13},{6,14},{7,15},{8,0},{9,1},... | collective-permute-start | bytes 196616 | tf_op jit(solution)/shard_map/ppermute | solution.py:414
  2.0 3.4 %collective-permute-start.1 = (bf16[8,2048]{1,0:T(8,128)(2,1)S(1)}, bf16[8,2048]{1,0:T(8,128)(2,1)S(1)}, u32[]{:S(2)}, u32[]{:S(2)}) collective-permute-start(bf16[8,2048]{1,0:T(8,128)(2,1)S(1)} %pick_rows.3), channel_id=1, source_target_pairs={{0,24},{1,25},{2,26},{3,27},{4,28},{5,29},{6,30},{7,31},{8,16},{9,... | collective-permute-start | bytes 98312 | tf_op jit(solution)/shard_map/ppermute | solution.py:414
  3.4 17.5 %copy-start = (bf16[2048,512]{1,0:T(8,128)(2,1)S(1)}, bf16[2048,512]{1,0:T(8,128)(2,1)}, u32[]{:S(2)}) copy-start(bf16[2048,512]{1,0:T(8,128)(2,1)} %constant.2.clone.table_ref) | copy-start | bytes 6291460
  5.8 5.1 %collective-permute-start.2 = (bf16[128,128]{1,0:T(8,128)(2,1)S(1)}, bf16[128,128]{1,0:T(8,128)(2,1)S(1)}, u32[]{:S(2)}, u32[]{:S(2)}) collective-permute-start(bf16[128,128]{1,0:T(8,128)(2,1)S(1)} %source_spectra.1), channel_id=1, source_target_pairs={{0,12},{1,13},{2,14},{3,15},{4,8},{5,9},{6,10},{7,11},{8,4},{9,5},... | collective-permute-start | bytes 98312 | tf_op jit(solution)/shard_map/ppermute | solution.py:414
  10.9 4.1 %collective-permute-start.3 = (bf16[256,128]{1,0:T(8,128)(2,1)S(1)}, bf16[256,128]{1,0:T(8,128)(2,1)S(1)}, u32[]{:S(2)}, u32[]{:S(2)}) collective-permute-start(bf16[256,128]{1,0:T(8,128)(2,1)S(1)} %pad_maximum_fusion.1), channel_id=1, source_target_pairs={{0,10},{1,11},{2,8},{3,9},{4,14},{5,15},{6,12},{7,13},{8,2},{9,3},... | collective-permute-start | bytes 196616 | tf_op jit(solution)/shard_map/ppermute | solution.py:414
  15.0 5.6 %collective-permute-start.4 = (bf16[512,128]{1,0:T(8,128)(2,1)S(1)}, bf16[512,128]{1,0:T(8,128)(2,1)S(1)}, u32[]{:S(2)}, u32[]{:S(2)}) collective-permute-start(bf16[512,128]{1,0:T(8,128)(2,1)S(1)} %pad_maximum_fusion.refs_0_), channel_id=1, source_target_pairs={{0,9},{1,8},{2,11},{3,10},{4,13},{5,12},{6,15},{7,14},{8,1},{9,0},... | collective-permute-start | bytes 393224 | tf_op jit(solution)/shard_map/ppermute | solution.py:414
  16.6 4.9 %collective-permute-start.6 = (bf16[512,128]{1,0:T(8,128)(2,1)S(1)}, bf16[512,128]{1,0:T(8,128)(2,1)S(1)}, u32[]{:S(2)}, u32[]{:S(2)}) collective-permute-start(bf16[512,128]{1,0:T(8,128)(2,1)S(1)} %pad_maximum_fusion.refs_0_), channel_id=1, source_target_pairs={{0,8},{1,9},{2,10},{3,11},{4,12},{5,13},{6,14},{7,15},{8,0},{9,1},... | collective-permute-start | bytes 393224 | tf_op jit(solution)/shard_map/ppermute | solution.py:414
  20.6 1.6 %collective-permute-start.5 = (bf16[512,128]{1,0:T(8,128)(2,1)S(1)}, bf16[512,128]{1,0:T(8,128)(2,1)S(1)}, u32[]{:S(2)}, u32[]{:S(2)}) collective-permute-start(bf16[512,128]{1,0:T(8,128)(2,1)S(1)} %collective-permute-done.4.refs_0_), channel_id=1, source_target_pairs={{0,8},{1,9},{2,10},{3,11},{4,12},{5,13},{6,14},{7,15},{8,0},{9,1},... | collective-permute-start | bytes 393224 | tf_op jit(solution)/shard_map/ppermute | solution.py:414

commit v3 on v2

--- a/solution.py
+++ b/solution.py
@@ -267,7 +267,7 @@
 
 
 def receiver_kernel(radius, order, ids_ref, usable_ref, raw_ref, twiddle_ref, table_ref, *rest):
-    spectra_ref, inverse_ref, samples, relay = rest
+    spectra_ref, inverse_ref, other_ref, samples, relay = rest
     channels, windows, _ = raw_ref.shape
     halves = channels // SRC_DEV
     members = lax.axis_size("dev")
@@ -291,7 +291,6 @@
     rows = STEPS * channels
     row = lax.broadcasted_iota(jnp.int32, (rows, total), 0)
     lane = lax.broadcasted_iota(jnp.int32, (rows, total), 1)
-    received = flags_of(jnp.where(lane == first + row % channels, 1.0, 0.0), flags)
     blocks = []
     for k, odd in order:
         picks = jnp.zeros((rows, total), jnp.float32)
@@ -304,14 +303,18 @@
             picks = jnp.where((row // channels == t) & (lane == channel), 1.0, picks)
         blocks.append(picks)
     sent = flags_of(jnp.concatenate(blocks, axis=0), flags)
-    both = sent * jnp.concatenate([received] * len(order), axis=0)
-    counts = jnp.sum(both, axis=1, keepdims=True)
-    inverse_ref[...] = jnp.broadcast_to(1.0 / jnp.maximum(counts, 1.0), inverse_ref.shape)
+    theirs = ((group ^ 1) * members + (member ^ 1)) * channels
+    for ref, start in ((inverse_ref, first), (other_ref, theirs)):
+        received = flags_of(jnp.where(lane == start + row % channels, 1.0, 0.0), flags)
+        both = sent * jnp.concatenate([received] * len(order), axis=0)
+        counts = jnp.sum(both, axis=1, keepdims=True)
+        ref[...] = jnp.broadcast_to(1.0 / jnp.maximum(counts, 1.0), ref.shape)
 
 
 def source_kernel(radius, *refs):
-    take_ref, mask_ref, kept_ref, came_ref, twiddle_ref, table_ref = refs[:6]
-    out_ref, relay = refs[-2:]
+    take_ref, mask_ref, kept_ref, came_ref, twiddle_ref, table_ref, spectra_ref = refs[:7]
+    out_ref, passed_ref, relay = refs[7:]
+    passed_ref[...] = spectra_ref[...]
     rows, length = kept_ref.shape
     points = length // RADIX
     here = take_ref[...] > 0.0
@@ -321,9 +324,8 @@
     whiten_rows(samples, radius, mask_ref[:, :1], twiddle_ref, table_ref, relay, out_ref)
 
 
-def lagged_rows(windows, pieces, recv_ref, inverse, table_ref, products, stacked):
+def lagged_rows(windows, pieces, sets, table_ref, products, stacked):
     blocks = RADIX // 2
-    receivers = recv_ref.shape[0] // (2 * windows * blocks)
 
     def row_set(ref, base, first, rows):
         out = []
@@ -336,27 +338,30 @@
             out.append(held)
         return out
 
-    own = [row_set(recv_ref, 0, r * windows, receivers * windows) for r in range(receivers)]
-    pairs = len(pieces) * STEPS * receivers
-    for p, (ref, base) in enumerate(pieces):
-        for step in range(STEPS):
-            a, b = row_set(ref, base, step * windows, STEPS * windows)
-            for r in range(receivers):
-                c, e = own[r]
-                re = im = None
-                for w in range(windows):
-                    re_w = a[w] * c[w] + b[w] * e[w]
-                    im_w = b[w] * c[w] - a[w] * e[w]
-                    re = re_w if re is None else re + re_w
-                    im = im_w if im is None else im + im_w
-                pair = (p * STEPS + step) * receivers + r
-                products[0, pair * blocks : (pair + 1) * blocks, :] = re
-                products[1, pair * blocks : (pair + 1) * blocks, :] = im
+    pair = 0
+    for recv_ref, _ in sets:
+        receivers = recv_ref.shape[0] // (2 * windows * blocks)
+        own = [row_set(recv_ref, 0, r * windows, receivers * windows) for r in range(receivers)]
+        for ref, base in pieces:
+            for step in range(STEPS):
+                a, b = row_set(ref, base, step * windows, STEPS * windows)
+                for r in range(receivers):
+                    c, e = own[r]
+                    re = im = None
+                    for w in range(windows):
+                        re_w = a[w] * c[w] + b[w] * e[w]
+                        im_w = b[w] * c[w] - a[w] * e[w]
+                        re = re_w if re is None else re + re_w
+                        im = im_w if im is None else im + im_w
+                    products[0, pair * blocks : (pair + 1) * blocks, :] = re
+                    products[1, pair * blocks : (pair + 1) * blocks, :] = im
+                    pair += 1
     width = products.shape[2]
+    inverse = jnp.concatenate([factors for _, factors in sets], axis=0)
     for part in range(2):
         for q in range(blocks):
             column = (part * blocks + q) * width
-            values = products[part, pl.ds(q, pairs, stride=blocks), :] * inverse
+            values = products[part, pl.ds(q, pair, stride=blocks), :] * inverse
             stacked[:, column : column + width] = values.astype(jnp.bfloat16)
     return jnp.dot(stacked[...], table_ref[...], preferred_element_type=jnp.float32)
 
@@ -366,36 +371,41 @@
     return [(ref, base) for base in range(0, ref.shape[0], rows)]
 
 
-def part_kernel(windows, first, inverse_ref, recv_ref, table_ref, *refs):
-    out_ref, products, stacked = refs[-3:]
-    pieces = [piece for ref in refs[:-3] for piece in pieces_of(ref, windows)]
-    inverse = inverse_ref[first : first + out_ref.shape[0], :]
-    out_ref[...] = lagged_rows(windows, pieces, recv_ref, inverse, table_ref, products, stacked)
-
-
-def last_kernel(windows, order, inverse_ref, recv_ref, table_ref, piece_ref, *refs):
-    out_ref, products, stacked = refs[-3:]
-    pieces = pieces_of(piece_ref, windows)
-    rows = stacked.shape[0]
-    inverse = inverse_ref[inverse_ref.shape[0] - rows :, :]
+def part_kernel(windows, first, n_sets, *refs):
+    table_ref, set_refs, refs = refs[0], refs[1 : 1 + 2 * n_sets], refs[1 + 2 * n_sets :]
+    products, stacked = refs[-2:]
+    buffers, outs = refs[: -2 - n_sets], refs[-2 - n_sets : -2]
+    pieces = [piece for ref in buffers for piece in pieces_of(ref, windows)]
+    rows = outs[0].shape[0]
+    sets = [
+        (set_refs[2 * i], set_refs[2 * i + 1][first : first + rows, :]) for i in range(n_sets)
+    ]
+    lagged = lagged_rows(windows, pieces, sets, table_ref, products, stacked)
+    for i, out_ref in enumerate(outs):
+        out_ref[...] = lagged[i * rows : (i + 1) * rows].astype(jnp.bfloat16)
+
+
+def pass_kernel(value_ref, after_ref, out_ref):
+    del after_ref
+    out_ref[...] = value_ref[...]
+
+
+def place_kernel(order, *refs):
+    out_ref = refs[-1]
     member = lax.axis_index("dev")
     core = lax.axis_index("grp") % SRC_DEV
     receivers = out_ref.shape[2]
-
-    def place(rows_ref, some):
-        for p, (k, odd) in enumerate(some):
+    whole = order + [(k ^ 1, 1 - odd) for k, odd in order]
+    block = STEPS * receivers
+    done = 0
+    for ref in refs[:-1]:
+        for p in range(ref.shape[0] // block):
+            k, odd = whole[done]
             source = (member ^ k) * SRC_DEV + (core + odd) % SRC_DEV
             for step in range(STEPS):
-                pair = (p * STEPS + step) * receivers
-                out_ref[step, source] = rows_ref[pair : pair + receivers, :].astype(jnp.bfloat16)
-
-    done = 0
-    for ref in refs[:-3]:
-        count = ref.shape[0] // (STEPS * receivers)
-        place(ref, order[done : done + count])
-        done += count
-    lagged = lagged_rows(windows, pieces, recv_ref, inverse, table_ref, products, stacked)
-    place(lagged, order[done:])
+                row = p * block + step * receivers
+                out_ref[step, source] = ref[row : row + receivers, :]
+            done += 1
 
 
 def on_device(records, usable, panel_ids):
@@ -432,7 +442,7 @@
     while bit:
         member_bits.append(bit)
         bit //= 2
-    order = panel_order(member_bits)
+    order = panel_order(member_bits[:-1])
 
     usable_rows = usable.T
     planes = groups // SRC_DEV
@@ -472,14 +482,15 @@
 
     row_count = channels * windows
     pairs = len(order) * STEPS * channels
-    receivers, inverse = pl.pallas_call(
+    receivers, inverse, inverse_theirs = pl.pallas_call(
         functools.partial(receiver_kernel, radius, order),
         out_shape=[
             jax.ShapeDtypeStruct((2 * row_count * blocks, width), jnp.bfloat16),
             jax.ShapeDtypeStruct((pairs, width), jnp.float32),
+            jax.ShapeDtypeStruct((pairs, width), jnp.float32),
         ],
         in_specs=[SMEM] + [VMEM] * 4,
-        out_specs=[VMEM] * 2,
+        out_specs=[VMEM] * 3,
         scratch_shapes=[
             pltpu.VMEM((row_count, length), jnp.float32),
             pltpu.VMEM((2 * row_count * blocks, width), jnp.float32),
@@ -489,56 +500,68 @@
         name="receiver_spectra",
     )(panel_ids, usable_rows, records, twiddle, table)
 
-    piece = pl.pallas_call(
+    piece, passed = pl.pallas_call(
         functools.partial(source_kernel, radius),
-        out_shape=jax.ShapeDtypeStruct((2 * source_rows * blocks, width), jnp.bfloat16),
+        out_shape=[
+            jax.ShapeDtypeStruct((2 * source_rows * blocks, width), jnp.bfloat16),
+            jax.ShapeDtypeStruct(receivers.shape, receivers.dtype),
+        ],
         in_specs=[VMEM] * 7,
-        out_specs=VMEM,
+        out_specs=[VMEM] * 2,
         scratch_shapes=[pltpu.VMEM((2 * source_rows * blocks, width), jnp.float32)],
         compiler_params=PARAMS,
         name="source_spectra",
-    )(take[0], mask, kept, came, twiddle, table, inverse)
+    )(take[0], mask, kept, came, twiddle, table, receivers)
 
     held = piece
-    for bit in member_bits[:-1]:
+    for bit in member_bits[:-2]:
         held = jnp.concatenate([held, exchange(held, 1, bit)], axis=0)
-    brought = exchange(held, 1, member_bits[-1])
+    theirs = exchange(passed, 1, 1)
     held_other = exchange(held, 1, 0)
-    brought_other = exchange(brought, 1, 0)
-
-    def part(first, cost, *buffers):
+
+    def part(first, sets, *buffers):
         rows = sum(b.shape[0] for b in buffers) // (2 * windows * blocks) * channels
+        total = rows * len(sets)
         return pl.pallas_call(
-            functools.partial(part_kernel, windows, first),
-            out_shape=jax.ShapeDtypeStruct((rows, NLAG), jnp.float32),
-            in_specs=[VMEM] * (3 + len(buffers)),
-            out_specs=VMEM,
+            functools.partial(part_kernel, windows, first, len(sets)),
+            out_shape=[jax.ShapeDtypeStruct((rows, NLAG), jnp.bfloat16)] * len(sets),
+            in_specs=[VMEM] * (1 + 2 * len(sets) + len(buffers)),
+            out_specs=[VMEM] * len(sets),
             scratch_shapes=[
-                pltpu.VMEM((2, rows * blocks, width), jnp.float32),
-                pltpu.VMEM((rows, 2 * bin_count), jnp.bfloat16),
+                pltpu.VMEM((2, total * blocks, width), jnp.float32),
+                pltpu.VMEM((total, 2 * bin_count), jnp.bfloat16),
             ],
             compiler_params=PARAMS,
-            cost_estimate=cost,
+            cost_estimate=BESIDE,
             name="correlate_part",
-        )(inverse, receivers, ltable, *buffers)
-
-    early = part(0, BESIDE, held, held_other)
-    middle = part(pairs // 2, BESIDE, brought)
-    rows = pairs // 4
+        )(ltable, *[array for pair in sets for array in pair], *buffers)
+
+    mine, other = (receivers, inverse), (theirs, inverse_theirs)
+    early_theirs, early = part(0, [other, mine], held, held_other)
+    brought = exchange(held, 1, member_bits[-2])
+    brought = pl.pallas_call(
+        pass_kernel,
+        out_shape=jax.ShapeDtypeStruct(brought.shape, brought.dtype),
+        in_specs=[VMEM] * 2,
+        out_specs=VMEM,
+        compiler_params=PARAMS,
+        name="pass_on",
+    )(brought, early_theirs)
+    brought_other = exchange(brought, 1, 0)
+    (middle_theirs,) = part(pairs // 2, [other], brought)
+    (late_theirs,) = part(pairs // 4 * 3, [other], brought_other)
+    (late,) = part(pairs // 2, [mine], brought, brought_other)
+    back = exchange(jnp.concatenate([early_theirs, middle_theirs, late_theirs], axis=0), 1, 1)
     return pl.pallas_call(
-        functools.partial(last_kernel, windows, order),
+        functools.partial(place_kernel, order),
         out_shape=jax.ShapeDtypeStruct(
             (STEPS, members * SRC_DEV, channels, NLAG), jnp.bfloat16
         ),
-        in_specs=[VMEM] * 6,
+        in_specs=[VMEM] * 3,
         out_specs=VMEM,
-        scratch_shapes=[
-            pltpu.VMEM((2, rows * blocks, width), jnp.float32),
-            pltpu.VMEM((rows, 2 * bin_count), jnp.bfloat16),
-        ],
         compiler_params=PARAMS,
-        name="correlate_last",
-    )(inverse, receivers, ltable, brought_other, early, middle)
+        name="place_rows",
+    )(early, late, back)
 
 
 def solution(mesh):

time: 23.5 us -> 22 us (0.936)
  the two profiles are of different devices: /device:TPU:25 before, /device:TPU:0 now
where the time goes in v3:
time: 22 us; the launch traced here: 21.8 us
  starting transfers between devices  11.2 us (51%)
  Pallas kernels  5.51 us (25%)
  waiting for transfers between devices  5.07 us (23%)
    ppermute x8, starting transfers between devices, exchange(): return lax.ppermute(value, AXES, pairs)  11.2 us
    ppermute x8, waiting for transfers between devices, exchange(): return lax.ppermute(value, AXES, pairs)  5.07 us
    pallas_call x4, Pallas kernels, part(): pl.pallas_call(functools.partial(part_kernel, windows, first, len(sets)),...  2.05 us
    pallas_call x1, Pallas kernels, on_device(): pl.pallas_call(functools.partial(receiver_kernel, radius, order), out_sha...  1.1 us
    pallas_call x1, Pallas kernels, on_device(): pl.pallas_call(functools.partial(choice_kernel, halves, channels), out_sh...  0.77 us
    pallas_call x1, Pallas kernels, on_device(): pl.pallas_call(functools.partial(place_kernel, order), out_shape=jax.Shap...  0.69 us
  transfers between devices with their start and end apart: 8, of which 6 were waited for; matrix products, arithmetic and copies ran while one was open for 0% of the time, Pallas kernels for 18%

profile of v3, /device:TPU:0, one launch (start us, length us, event | category | flops | bytes accessed | tf_op | source)
XLA Modules:
  0.0 21.8 jit_solution(11022596663345482596)
XLA Ops:
  0.0 0.0 copy-start
  0.0 0.0 copy-start.2
  0.0 0.5 %collective-permute-start = (bf16[4,4,2048]{2,1,0:T(4,128)(2,1)}, bf16[4,4,2048]{2,1,0:T(4,128)(2,1)S(1)}, u32[]{:S(2)}, u32[]{:S(2)}) collective-permute-start(bf16[4,4,2048]{2,1,0:T(4,128)(2,1)} %raw_ref.1), channel_id=1, source_target_pairs={{0,8},{1,9},{2,10},{3,11},{4,12},{5,13},{6,14},{7,15},{8,0},{9,1},... | collective-permute-start | bytes 196616 | tf_op jit(solution)/shard_map/ppermute | solution.py:424
  0.5 0.4 %short_tables.1 = (bf16[2,512,256]{2,1,0:T(8,128)(2,1)S(1)}, f32[2,16,128]{2,1,0:T(8,128)S(1)}) custom-call(), custom_call_target="tpu_custom_call" | custom-call | flops 5000000000 | bytes 1000000 | tf_op jit(solution)/shard_map/short_tables/pallas_call | solution.py:427
  0.9 0.0 copy-done.2
  0.9 0.0 copy-done.1
  0.9 0.8 %choose_rows.1 = (f32[8,128]{1,0:T(8,128)S(1)}, f32[8,128]{1,0:T(8,128)S(1)}, f32[1,8,128]{2,1,0:T(8,128)S(1)}) custom-call(s32[2]{0:T(128)S(1)} %copy-done.2, s32[4,128]{1,0:T(4,128)S(1)} %bitcast.3, f32[2,16,128]{2,1,0:T(8,128)S(1)} %get-tuple-element.17.after_ref.twiddle_ref.refs_4_), custom_call_target="tpu_custom_call" | custom-call | tf_op jit(solution)/shard_map/choose_rows/pallas_call | solution.py:453
  1.7 0.0 collective-permute-done.other_ref
  1.7 0.0 copy-done
  1.7 2.7 %collective-permute-start.1 = (bf16[8,2048]{1,0:T(8,128)(2,1)S(1)}, bf16[8,2048]{1,0:T(8,128)(2,1)S(1)}, u32[]{:S(2)}, u32[]{:S(2)}) collective-permute-start(bf16[8,2048]{1,0:T(8,128)(2,1)S(1)} %pick_rows.3), channel_id=1, source_target_pairs={{0,24},{1,25},{2,26},{3,27},{4,28},{5,29},{6,30},{7,31},{8,16},{9,... | collective-permute-start | bytes 98312 | tf_op jit(solution)/shard_map/ppermute | solution.py:424
  4.4 1.1 %receiver_spectra.1 = (bf16[256,128]{1,0:T(8,128)(2,1)S(1)}, f32[64,128]{1,0:T(8,128)S(1)}, f32[64,128]{1,0:T(8,128)S(1)}) custom-call(s32[2]{0:T(128)S(1)} %copy-done.2, s32[4,128]{1,0:T(4,128)S(1)} %bitcast.4, bf16[4,4,2048]{2,1,0:T(4,128)(2,1)S(1)} %copy-done, f32[2,16,128]{2,1,0:T(8,128)S(1)} %get-tuple-element.17.after_ref.twiddle_ref.refs_4_, ...), custom_call_target="tpu_custom_call" | custom-call | flops 5000000000 | bytes 1000000 | tf_op jit(solution)/shard_map/receiver_spectra/pallas_call | solution.py:485
  5.5 0.1 pick_rows.2.refs_2_
  5.6 0.4 %collective-permute-done.1.refs_3_ = bf16[8,2048]{1,0:T(8,128)(2,1)S(1)} collective-permute-done((bf16[8,2048]{1,0:T(8,128)(2,1)S(1)}, bf16[8,2048]{1,0:T(8,128)(2,1)S(1)}, u32[]{:S(2)}, u32[]{:S(2)}) %collective-permute-start.1) | collective-permute-done | bytes 32800 | tf_op jit(solution)/shard_map/ppermute | solution.py:424
  6.0 0.4 %source_spectra.1 = (bf16[128,128]{1,0:T(8,128)(2,1)S(1)}, bf16[256,128]{1,0:T(8,128)(2,1)S(1)}) custom-call(f32[8,128]{1,0:T(8,128)S(1)} %bitcast.2, f32[8,128]{1,0:T(8,128)S(1)} %get-tuple-element.19.refs_1_, bf16[8,2048]{1,0:T(8,128)(2,1)S(1)} %pick_rows.2.refs_2_, bf16[8,2048]{1,0:T(8,128)(2,1)S(1)} %collective-permute-done.1.refs_3_, ...), custom_call_target="tpu_custom_call" | custom-call | tf_op jit(solution)/shard_map/source_spectra/pallas_call | solution.py:503
  6.4 2.9 %collective-permute-start.3 = (bf16[128,128]{1,0:T(8,128)(2,1)S(1)}, bf16[128,128]{1,0:T(8,128)(2,1)S(1)}, u32[]{:S(2)}, u32[]{:S(2)}) collective-permute-start(bf16[128,128]{1,0:T(8,128)(2,1)S(1)} %get-tuple-element.26), channel_id=1, source_target_pairs={{0,12},{1,13},{2,14},{3,15},{4,8},{5,9},{6,10},{7,11},{8,4},{9,5},... | collective-permute-start | bytes 98312 | tf_op jit(solution)/shard_map/ppermute | solution.py:424
  9.3 1.4 %collective-permute-start.2 = (bf16[256,128]{1,0:T(8,128)(2,1)S(1)}, bf16[256,128]{1,0:T(8,128)(2,1)S(1)}, u32[]{:S(2)}, u32[]{:S(2)}) collective-permute-start(bf16[256,128]{1,0:T(8,128)(2,1)S(1)} %get-tuple-element.23), channel_id=1, source_target_pairs={{0,9},{1,8},{2,11},{3,10},{4,13},{5,12},{6,15},{7,14},{8,1},{9,0},... | collective-permute-start | bytes 196616 | tf_op jit(solution)/shard_map/ppermute | solution.py:424
  10.8 0.2 collective-permute-done.3
  10.9 0.3 %collective-permute-start.4 = (bf16[256,128]{1,0:T(8,128)(2,1)S(1)}, bf16[256,128]{1,0:T(8,128)(2,1)S(1)}, u32[]{:S(2)}, u32[]{:S(2)}) collective-permute-start(bf16[256,128]{1,0:T(8,128)(2,1)S(1)} %constant_dynamic-update-slice_fusion.refs_5_), channel_id=1, source_target_pairs={{0,8},{1,9},{2,10},{3,11},{4,12},{5,13},{6,14},{7,15},{8,0},{9,1},... | collective-permute-start | bytes 196616 | tf_op jit(solution)/shard_map/ppermute | solution.py:424
  11.2 1.8 %collective-permute-start.5 = (bf16[256,128]{1,0:T(8,128)(2,1)S(1)}, bf16[256,128]{1,0:T(8,128)(2,1)S(1)}, u32[]{:S(2)}, u32[]{:S(2)}) collective-permute-start(bf16[256,128]{1,0:T(8,128)(2,1)S(1)} %constant_dynamic-update-slice_fusion.refs_5_), channel_id=1, source_target_pairs={{0,10},{1,11},{2,8},{3,9},{4,14},{5,15},{6,12},{7,13},{8,2},{9,3},... | collective-permute-start | bytes 196616 | tf_op jit(solution)/shard_map/ppermute | solution.py:424
  13.0 0.3 %collective-permute-done.2.refs_1_ = bf16[256,128]{1,0:T(8,128)(2,1)S(1)} collective-permute-done((bf16[256,128]{1,0:T(8,128)(2,1)S(1)}, bf16[256,128]{1,0:T(8,128)(2,1)S(1)}, u32[]{:S(2)}, u32[]{:S(2)}) %collective-permute-start.2) | collective-permute-done | bytes 65568 | tf_op jit(solution)/shard_map/ppermute | solution.py:424
  13.3 0.0 collective-permute-done.4.refs_6_
  13.3 0.0 copy-done.3
  13.3 0.7 %correlate_part.4 = (bf16[32,512]{1,0:T(8,128)(2,1)S(1)}, bf16[32,512]{1,0:T(8,128)(2,1)S(1)}) custom-call(bf16[2048,512]{1,0:T(8,128)(2,1)S(1)} %copy-done.3, bf16[256,128]{1,0:T(8,128)(2,1)S(1)} %collective-permute-done.2.refs_1_, f32[64,128]{1,0:T(8,128)S(1)} %get-tuple-element.24.refs_2_, bf16[256,128]{1,0:T(8,128)(2,1)S(1)} %get-tuple-element.22.refs_6_.refs_3_.refs_1_, ...), custom_call_target="tpu_custom_call" | custom-call | flops 1000000000 | bytes 1000000 | tf_op jit(solution)/shard_map/correlate_part/pallas_call | solution.py:525
  14.0 1.3 %collective-permute-done.5.value_ref = bf16[256,128]{1,0:T(8,128)(2,1)S(1)} collective-permute-done((bf16[256,128]{1,0:T(8,128)(2,1)S(1)}, bf16[256,128]{1,0:T(8,128)(2,1)S(1)}, u32[]{:S(2)}, u32[]{:S(2)}) %collective-permute-start.5) | collective-permute-done | bytes 65568 | tf_op jit(solution)/shard_map/ppermute | solution.py:424
  15.4 0.2 collective-permute-start.6
  15.5 0.4 %correlate_part.6 = bf16[16,512]{1,0:T(8,128)(2,1)S(1)} custom-call(bf16[2048,512]{1,0:T(8,128)(2,1)S(1)} %copy-done.3, bf16[256,128]{1,0:T(8,128)(2,1)S(1)} %collective-permute-done.2.refs_1_, f32[64,128]{1,0:T(8,128)S(1)} %get-tuple-element.24.refs_2_, bf16[256,128]{1,0:T(8,128)(2,1)S(1)} %pass_on.1.refs_3_), custom_call_target="tpu_custom_call" | custom-call | flops 1000000000 | bytes 1000000 | tf_op jit(solution)/shard_map/correlate_part/pallas_call | solution.py:525
  15.9 0.7 %collective-permute-done.6.refs_4_.refs_3_ = bf16[256,128]{1,0:T(8,128)(2,1)S(1)} collective-permute-done((bf16[256,128]{1,0:T(8,128)(2,1)S(1)}, bf16[256,128]{1,0:T(8,128)(2,1)S(1)}, u32[]{:S(2)}, u32[]{:S(2)}) %collective-permute-start.6) | collective-permute-done | bytes 65568 | tf_op jit(solution)/shard_map/ppermute | solution.py:424
  16.6 0.4 %correlate_part.7 = bf16[16,512]{1,0:T(8,128)(2,1)S(1)} custom-call(bf16[2048,512]{1,0:T(8,128)(2,1)S(1)} %copy-done.3, bf16[256,128]{1,0:T(8,128)(2,1)S(1)} %collective-permute-done.2.refs_1_, f32[64,128]{1,0:T(8,128)S(1)} %get-tuple-element.24.refs_2_, bf16[256,128]{1,0:T(8,128)(2,1)S(1)} %collective-permute-done.6.refs_4_.refs_3_), custom_call_target="tpu_custom_call" | custom-call | flops 1000000000 | bytes 1000000 | tf_op jit(solution)/shard_map/correlate_part/pallas_call | solution.py:525
  17.0 1.4 %collective-permute-start.7 = (bf16[64,512]{1,0:T(8,128)(2,1)S(1)}, bf16[64,512]{1,0:T(8,128)(2,1)S(1)}, u32[]{:S(2)}, u32[]{:S(2)}) collective-permute-start(bf16[64,512]{1,0:T(8,128)(2,1)S(1)} %pad_maximum_fusion), channel_id=1, source_target_pairs={{0,9},{1,8},{2,11},{3,10},{4,13},{5,12},{6,15},{7,14},{8,1},{9,0},... | collective-permute-start | bytes 196616 | tf_op jit(solution)/shard_map/ppermute | solution.py:424
  18.5 0.5 %correlate_part.5.refs_1_ = bf16[32,512]{1,0:T(8,128)(2,1)S(1)} custom-call(bf16[2048,512]{1,0:T(8,128)(2,1)S(1)} %copy-done.3, bf16[256,128]{1,0:T(8,128)(2,1)S(1)} %get-tuple-element.22.refs_6_.refs_3_.refs_1_, f32[64,128]{1,0:T(8,128)S(1)} %get-tuple-element.25.refs_4_.refs_2_, bf16[256,128]{1,0:T(8,128)(2,1)S(1)} %pass_on.1.refs_3_, ...), custom_call_target="tpu_custom_call" | custom-call | flops 1000000000 | bytes 1000000 | tf_op jit(solution)/shard_map/correlate_part/pallas_call | solution.py:525
  19.0 2.2 %collective-permute-done.7.refs_2_ = bf16[64,512]{1,0:T(8,128)(2,1)S(1)} collective-permute-done((bf16[64,512]{1,0:T(8,128)(2,1)S(1)}, bf16[64,512]{1,0:T(8,128)(2,1)S(1)}, u32[]{:S(2)}, u32[]{:S(2)}) %collective-permute-start.7) | collective-permute-done | bytes 65568 | tf_op jit(solution)/shard_map/ppermute | solution.py:424
  21.1 0.7 %place_rows.1 = bf16[2,16,4,512]{3,2,1,0:T(4,128)(2,1)} custom-call(bf16[32,512]{1,0:T(8,128)(2,1)S(1)} %get-tuple-element.27.refs_0_, bf16[32,512]{1,0:T(8,128)(2,1)S(1)} %correlate_part.5.refs_1_, bf16[64,512]{1,0:T(8,128)(2,1)S(1)} %collective-permute-done.7.refs_2_), custom_call_target="tpu_custom_call" | custom-call | tf_op jit(solution)/shard_map/place_rows/pallas_call | solution.py:555
  (7 shorter events, 0.1 us)
Async XLA Ops:
  0.0 1.7 %copy-start = (bf16[4,4,2048]{2,1,0:T(4,128)(2,1)S(1)}, bf16[4,4,2048]{2,1,0:T(4,128)(2,1)}, u32[]{:S(2)}) copy-start(bf16[4,4,2048]{2,1,0:T(4,128)(2,1)} %raw_ref.1) | copy-start | bytes 196612
  0.0 0.9 %copy-start.2 = (s32[2]{0:T(128)S(1)}, s32[2]{0:T(128)}, u32[]{:S(2)}) copy-start(s32[2]{0:T(128)} %ids_ref.3) | copy-start | bytes 28
  0.0 0.9 %copy-start.1 = (s32[128,4]{0,1:T(4,128)S(1)}, s32[128,4]{0,1:T(4,128)}, u32[]{:S(2)}) copy-start(s32[128,4]{0,1:T(4,128)} %param.5) | copy-start | bytes 6148
  0.0 1.7 %collective-permute-start = (bf16[4,4,2048]{2,1,0:T(4,128)(2,1)}, bf16[4,4,2048]{2,1,0:T(4,128)(2,1)S(1)}, u32[]{:S(2)}, u32[]{:S(2)}) collective-permute-start(bf16[4,4,2048]{2,1,0:T(4,128)(2,1)} %raw_ref.1), channel_id=1, source_target_pairs={{0,8},{1,9},{2,10},{3,11},{4,12},{5,13},{6,14},{7,15},{8,0},{9,1},... | collective-permute-start | bytes 196616 | tf_op jit(solution)/shard_map/ppermute | solution.py:424
  1.7 4.3 %collective-permute-start.1 = (bf16[8,2048]{1,0:T(8,128)(2,1)S(1)}, bf16[8,2048]{1,0:T(8,128)(2,1)S(1)}, u32[]{:S(2)}, u32[]{:S(2)}) collective-permute-start(bf16[8,2048]{1,0:T(8,128)(2,1)S(1)} %pick_rows.3), channel_id=1, source_target_pairs={{0,24},{1,25},{2,26},{3,27},{4,28},{5,29},{6,30},{7,31},{8,16},{9,... | collective-permute-start | bytes 98312 | tf_op jit(solution)/shard_map/ppermute | solution.py:424
  4.4 8.9 %copy-start.3 = (bf16[2048,512]{1,0:T(8,128)(2,1)S(1)}, bf16[2048,512]{1,0:T(8,128)(2,1)}, u32[]{:S(2)}) copy-start(bf16[2048,512]{1,0:T(8,128)(2,1)} %constant.2.clone.refs_0_) | copy-start | bytes 6291460
  6.4 4.5 %collective-permute-start.3 = (bf16[128,128]{1,0:T(8,128)(2,1)S(1)}, bf16[128,128]{1,0:T(8,128)(2,1)S(1)}, u32[]{:S(2)}, u32[]{:S(2)}) collective-permute-start(bf16[128,128]{1,0:T(8,128)(2,1)S(1)} %get-tuple-element.26), channel_id=1, source_target_pairs={{0,12},{1,13},{2,14},{3,15},{4,8},{5,9},{6,10},{7,11},{8,4},{9,5},... | collective-permute-start | bytes 98312 | tf_op jit(solution)/shard_map/ppermute | solution.py:424
  9.3 4.0 %collective-permute-start.2 = (bf16[256,128]{1,0:T(8,128)(2,1)S(1)}, bf16[256,128]{1,0:T(8,128)(2,1)S(1)}, u32[]{:S(2)}, u32[]{:S(2)}) collective-permute-start(bf16[256,128]{1,0:T(8,128)(2,1)S(1)} %get-tuple-element.23), channel_id=1, source_target_pairs={{0,9},{1,8},{2,11},{3,10},{4,13},{5,12},{6,15},{7,14},{8,1},{9,0},... | collective-permute-start | bytes 196616 | tf_op jit(solution)/shard_map/ppermute | solution.py:424
  10.9 2.4 %collective-permute-start.4 = (bf16[256,128]{1,0:T(8,128)(2,1)S(1)}, bf16[256,128]{1,0:T(8,128)(2,1)S(1)}, u32[]{:S(2)}, u32[]{:S(2)}) collective-permute-start(bf16[256,128]{1,0:T(8,128)(2,1)S(1)} %constant_dynamic-update-slice_fusion.refs_5_), channel_id=1, source_target_pairs={{0,8},{1,9},{2,10},{3,11},{4,12},{5,13},{6,14},{7,15},{8,0},{9,1},... | collective-permute-start | bytes 196616 | tf_op jit(solution)/shard_map/ppermute | solution.py:424
  11.2 4.1 %collective-permute-start.5 = (bf16[256,128]{1,0:T(8,128)(2,1)S(1)}, bf16[256,128]{1,0:T(8,128)(2,1)S(1)}, u32[]{:S(2)}, u32[]{:S(2)}) collective-permute-start(bf16[256,128]{1,0:T(8,128)(2,1)S(1)} %constant_dynamic-update-slice_fusion.refs_5_), channel_id=1, source_target_pairs={{0,10},{1,11},{2,8},{3,9},{4,14},{5,15},{6,12},{7,13},{8,2},{9,3},... | collective-permute-start | bytes 196616 | tf_op jit(solution)/shard_map/ppermute | solution.py:424
  15.4 1.3 %collective-permute-start.6 = (bf16[256,128]{1,0:T(8,128)(2,1)S(1)}, bf16[256,128]{1,0:T(8,128)(2,1)S(1)}, u32[]{:S(2)}, u32[]{:S(2)}) collective-permute-start(bf16[256,128]{1,0:T(8,128)(2,1)S(1)} %pass_on.1.refs_3_), channel_id=1, source_target_pairs={{0,8},{1,9},{2,10},{3,11},{4,12},{5,13},{6,14},{7,15},{8,0},{9,1},... | collective-permute-start | bytes 196616 | tf_op jit(solution)/shard_map/ppermute | solution.py:424
  17.0 4.1 %collective-permute-start.7 = (bf16[64,512]{1,0:T(8,128)(2,1)S(1)}, bf16[64,512]{1,0:T(8,128)(2,1)S(1)}, u32[]{:S(2)}, u32[]{:S(2)}) collective-permute-start(bf16[64,512]{1,0:T(8,128)(2,1)S(1)} %pad_maximum_fusion), channel_id=1, source_target_pairs={{0,9},{1,8},{2,11},{3,10},{4,13},{5,12},{6,15},{7,14},{8,1},{9,0},... | collective-permute-start | bytes 196616 | tf_op jit(solution)/shard_map/ppermute | solution.py:424

commit v4 on v3

--- a/solution.py
+++ b/solution.py
@@ -31,7 +31,8 @@
     return np.concatenate(order)
 
 
-def tables_kernel(length, table_ref, twiddle_ref):
+def tables_kernel(length, after_ref, table_ref, twiddle_ref):
+    del after_ref
     points = length // RADIX
     per = points // 2
     row = lax.broadcasted_iota(jnp.int32, (points, points), 0)
@@ -212,8 +213,13 @@
     return jnp.sum(kept, axis=1, keepdims=True)
 
 
-def choice_kernel(halves, channels, ids_ref, usable_ref, after_ref, choice_ref, mask_ref, take_ref):
+def first_kernel(out_ref):
+    out_ref[...] = jnp.zeros_like(out_ref)
+
+
+def choice_kernel(halves, channels, ids_ref, usable_ref, after_ref, *outs):
     del after_ref
+    choice_ref, mask_ref, take_ref, info_ref = outs
     windows, total = usable_ref.shape
     members = lax.axis_size("dev")
     group, member = lax.axis_index("grp"), lax.axis_index("dev")
@@ -228,6 +234,13 @@
         apart = (owning[t] + core) % SRC_DEV
         choice = jnp.where(row == (t * SRC_DEV + apart) * halves + within[t], 1.0, choice)
     choice_ref[...] = choice
+
+    row = lax.broadcasted_iota(jnp.int32, info_ref.shape, 0)
+    info = jnp.zeros(info_ref.shape, jnp.int32)
+    for t in range(STEPS):
+        start = owning[t] * members * channels + within[t] * SRC_DEV
+        info = jnp.where(row == t, start, info)
+    info_ref[...] = info
 
     rows = STEPS * windows
     row = lax.broadcasted_iota(jnp.int32, (rows, total), 0)
@@ -266,18 +279,15 @@
     out_ref[...] = samples[...].astype(out_ref.dtype)
 
 
-def receiver_kernel(radius, order, ids_ref, usable_ref, raw_ref, twiddle_ref, table_ref, *rest):
+def receiver_kernel(radius, order, info_ref, usable_ref, raw_ref, twiddle_ref, table_ref, *rest):
     spectra_ref, inverse_ref, other_ref, samples, relay = rest
     channels, windows, _ = raw_ref.shape
-    halves = channels // SRC_DEV
     members = lax.axis_size("dev")
     group, member = lax.axis_index("grp"), lax.axis_index("dev")
     core = group % SRC_DEV
     first = (group * members + member) * channels
     flags = usable_ref[...].astype(jnp.float32).astype(jnp.bfloat16)
     total = flags.shape[1]
-    owning = [ids_ref[t] // halves for t in range(STEPS)]
-    within = [ids_ref[t] % halves for t in range(STEPS)]
 
     for r in range(channels):
         samples[r * windows : (r + 1) * windows, :] = raw_ref[r].astype(jnp.float32)
@@ -291,17 +301,14 @@
     rows = STEPS * channels
     row = lax.broadcasted_iota(jnp.int32, (rows, total), 0)
     lane = lax.broadcasted_iota(jnp.int32, (rows, total), 1)
+    start = jnp.zeros((rows, total), jnp.int32)
+    for t in range(STEPS):
+        here = jnp.broadcast_to(info_ref[t : t + 1, :1], (rows, total))
+        start = jnp.where(row // channels == t, here, start)
     blocks = []
     for k, odd in order:
-        picks = jnp.zeros((rows, total), jnp.float32)
-        for t in range(STEPS):
-            channel = (
-                (owning[t] * members + (member ^ k)) * channels
-                + within[t] * SRC_DEV
-                + (core + odd) % SRC_DEV
-            )
-            picks = jnp.where((row // channels == t) & (lane == channel), 1.0, picks)
-        blocks.append(picks)
+        offset = (member ^ k) * channels + (core + odd) % SRC_DEV
+        blocks.append(jnp.where(lane == start + offset, 1.0, 0.0))
     sent = flags_of(jnp.concatenate(blocks, axis=0), flags)
     theirs = ((group ^ 1) * members + (member ^ 1)) * channels
     for ref, start in ((inverse_ref, first), (other_ref, theirs)):
@@ -423,19 +430,6 @@
         pairs = [(i, i ^ flip) for i in range(groups * members)]
         return lax.ppermute(value, AXES, pairs)
 
-    points = length // RADIX
-    table, twiddle = pl.pallas_call(
-        functools.partial(tables_kernel, length),
-        out_shape=[
-            jax.ShapeDtypeStruct((2, 4 * points, 2 * points), jnp.bfloat16),
-            jax.ShapeDtypeStruct((2, RADIX, points), jnp.float32),
-        ],
-        in_specs=[],
-        out_specs=[VMEM] * 2,
-        compiler_params=PARAMS,
-        cost_estimate=AHEAD,
-        name="short_tables",
-    )()
     ltable = jnp.asarray(lag_table(length, bin_count, NLAG))
     member_bits = []
     bit = members // 2
@@ -450,18 +444,28 @@
     plane_bits = planes.bit_length() - 1
 
     records_other = exchange(records, 1, 0)
-    choice, mask, take = pl.pallas_call(
+    ahead = pl.pallas_call(
+        first_kernel,
+        out_shape=jax.ShapeDtypeStruct((8, width), jnp.float32),
+        in_specs=[],
+        out_specs=VMEM,
+        compiler_params=PARAMS,
+        cost_estimate=AHEAD,
+        name="ahead",
+    )()
+    choice, mask, take, info = pl.pallas_call(
         functools.partial(choice_kernel, halves, channels),
         out_shape=[
             jax.ShapeDtypeStruct((STEPS * SRC_DEV * halves, width), jnp.float32),
             jax.ShapeDtypeStruct((source_rows, width), jnp.float32),
             jax.ShapeDtypeStruct((plane_bits, source_rows, width), jnp.float32),
+            jax.ShapeDtypeStruct((8, width), jnp.int32),
         ],
         in_specs=[SMEM] + [VMEM] * 2,
-        out_specs=[VMEM] * 3,
+        out_specs=[VMEM] * 4,
         compiler_params=PARAMS,
         name="choose_rows",
-    )(panel_ids, usable_rows, twiddle)
+    )(panel_ids, usable_rows, ahead)
 
     def pick(flip):
         return pl.pallas_call(
@@ -474,11 +478,26 @@
             name="pick_rows",
         )(choice, records, records_other)
 
-    came = exchange(pick(1), SRC_DEV * (planes // 2) + 1, 0)
+    sent = pick(1)
+    came = exchange(sent, SRC_DEV * (planes // 2) + 1, 0)
     kept = pick(0)
     for index in range(plane_bits - 2, -1, -1):
         kept = jnp.where(take[index + 1][:, :1] > 0.0, came, kept)
         came = exchange(kept, SRC_DEV << index, 0)
+
+    points = length // RADIX
+    table, twiddle = pl.pallas_call(
+        functools.partial(tables_kernel, length),
+        out_shape=[
+            jax.ShapeDtypeStruct((2, 4 * points, 2 * points), jnp.bfloat16),
+            jax.ShapeDtypeStruct((2, RADIX, points), jnp.float32),
+        ],
+        in_specs=[VMEM],
+        out_specs=[VMEM] * 2,
+        compiler_params=PARAMS,
+        cost_estimate=AHEAD,
+        name="short_tables",
+    )(sent)
 
     row_count = channels * windows
     pairs = len(order) * STEPS * channels
@@ -489,7 +508,7 @@
             jax.ShapeDtypeStruct((pairs, width), jnp.float32),
             jax.ShapeDtypeStruct((pairs, width), jnp.float32),
         ],
-        in_specs=[SMEM] + [VMEM] * 4,
+        in_specs=[VMEM] * 5,
         out_specs=[VMEM] * 3,
         scratch_shapes=[
             pltpu.VMEM((row_count, length), jnp.float32),
@@ -498,7 +517,7 @@
         compiler_params=PARAMS,
         cost_estimate=AHEAD,
         name="receiver_spectra",
-    )(panel_ids, usable_rows, records, twiddle, table)
+    )(info, usable_rows, records, twiddle, table)
 
     piece, passed = pl.pallas_call(
         functools.partial(source_kernel, radius),
@@ -517,7 +536,16 @@
     for bit in member_bits[:-2]:
         held = jnp.concatenate([held, exchange(held, 1, bit)], axis=0)
     theirs = exchange(passed, 1, 1)
-    held_other = exchange(held, 1, 0)
+
+    def pass_on(value, after):
+        return pl.pallas_call(
+            pass_kernel,
+            out_shape=jax.ShapeDtypeStruct(value.shape, value.dtype),
+            in_specs=[VMEM] * 2,
+            out_specs=VMEM,
+            compiler_params=PARAMS,
+            name="pass_on",
+        )(value, after)
 
     def part(first, sets, *buffers):
         rows = sum(b.shape[0] for b in buffers) // (2 * windows * blocks) * channels
@@ -537,21 +565,17 @@
         )(ltable, *[array for pair in sets for array in pair], *buffers)
 
     mine, other = (receivers, inverse), (theirs, inverse_theirs)
-    early_theirs, early = part(0, [other, mine], held, held_other)
     brought = exchange(held, 1, member_bits[-2])
-    brought = pl.pallas_call(
-        pass_kernel,
-        out_shape=jax.ShapeDtypeStruct(brought.shape, brought.dtype),
-        in_specs=[VMEM] * 2,
-        out_specs=VMEM,
-        compiler_params=PARAMS,
-        name="pass_on",
-    )(brought, early_theirs)
+    held_other = exchange(pass_on(held, theirs), 1, 0)
+    early_theirs, early = part(0, [other, mine], held)
+    (next_theirs,) = part(pairs // 4, [other], held_other)
+    brought = pass_on(brought, next_theirs)
     brought_other = exchange(brought, 1, 0)
     (middle_theirs,) = part(pairs // 2, [other], brought)
     (late_theirs,) = part(pairs // 4 * 3, [other], brought_other)
-    (late,) = part(pairs // 2, [mine], brought, brought_other)
-    back = exchange(jnp.concatenate([early_theirs, middle_theirs, late_theirs], axis=0), 1, 1)
+    (late,) = part(pairs // 4, [mine], held_other, brought, brought_other)
+    lag_rows = [early_theirs, next_theirs, middle_theirs, late_theirs]
+    back = exchange(jnp.concatenate(lag_rows, axis=0), 1, 1)
     return pl.pallas_call(
         functools.partial(place_kernel, order),
         out_shape=jax.ShapeDtypeStruct(

time: 22 us -> 21.7 us (0.986)
  the two profiles are of different devices: /device:TPU:0 before, /device:TPU:25 now
where the time goes in v4:
time: 21.7 us; the launch traced here: 21.5 us
  waiting for transfers between devices  9.88 us (46%)
  starting transfers between devices  6.28 us (29%)
  Pallas kernels  5.27 us (24%)
    ppermute x8, waiting for transfers between devices, exchange(): return lax.ppermute(value, AXES, pairs)  9.88 us
    ppermute x8, starting transfers between devices, exchange(): return lax.ppermute(value, AXES, pairs)  6.28 us
    pallas_call x5, Pallas kernels, part(): pl.pallas_call(functools.partial(part_kernel, windows, first, len(sets)),...  2.34 us
    pallas_call x1, Pallas kernels, on_device(): pl.pallas_call(functools.partial(choice_kernel, halves, channels), out_sh...  0.77 us
    pallas_call x1, Pallas kernels, on_device(): pl.pallas_call(functools.partial(place_kernel, order), out_shape=jax.Shap...  0.69 us
    pallas_call x1, Pallas kernels, on_device(): pl.pallas_call(functools.partial(receiver_kernel, radius, order), out_sha...  0.57 us
  transfers between devices with their start and end apart: 8, of which 7 were waited for; matrix products, arithmetic and copies ran while one was open for 0% of the time, Pallas kernels for 17%

profile of v4, /device:TPU:25, one launch (start us, length us, event | category | flops | bytes accessed | tf_op | source)
XLA Modules:
  0.0 21.5 jit_solution(9494351153612360510)
XLA Ops:
  0.0 0.7 %collective-permute-start = (bf16[4,4,2048]{2,1,0:T(4,128)(2,1)}, bf16[4,4,2048]{2,1,0:T(4,128)(2,1)S(1)}, u32[]{:S(2)}, u32[]{:S(2)}) collective-permute-start(bf16[4,4,2048]{2,1,0:T(4,128)(2,1)} %raw_ref.1), channel_id=1, source_target_pairs={{0,8},{1,9},{2,10},{3,11},{4,12},{5,13},{6,14},{7,15},{8,0},{9,1},... | collective-permute-start | bytes 196616 | tf_op jit(solution)/shard_map/ppermute | solution.py:431
  0.8 0.0 copy-done.2
  0.8 0.0 copy-done.1
  0.8 0.8 %choose_rows.1 = (f32[8,128]{1,0:T(8,128)S(1)}, f32[8,128]{1,0:T(8,128)S(1)}, f32[1,8,128]{2,1,0:T(8,128)S(1)}, s32[8,128]{1,0:T(8,128)S(1)}) custom-call(s32[2]{0:T(128)S(1)} %copy-done.2, s32[4,128]{1,0:T(4,128)S(1)} %bitcast.3, f32[8,128]{1,0:T(8,128)S(1)} %ahead.1.after_ref), custom_call_target="tpu_custom_call" | custom-call | tf_op jit(solution)/shard_map/choose_rows/pallas_call | solution.py:456
  1.5 0.3 %collective-permute-done.other_ref = bf16[4,4,2048]{2,1,0:T(4,128)(2,1)S(1)} collective-permute-done((bf16[4,4,2048]{2,1,0:T(4,128)(2,1)}, bf16[4,4,2048]{2,1,0:T(4,128)(2,1)S(1)}, u32[]{:S(2)}, u32[]{:S(2)}) %collective-permute-start) | collective-permute-done | bytes 65568 | tf_op jit(solution)/shard_map/ppermute | solution.py:431
  1.9 0.0 copy-done
  1.9 1.5 %collective-permute-start.1 = (bf16[8,2048]{1,0:T(8,128)(2,1)S(1)}, bf16[8,2048]{1,0:T(8,128)(2,1)S(1)}, u32[]{:S(2)}, u32[]{:S(2)}) collective-permute-start(bf16[8,2048]{1,0:T(8,128)(2,1)S(1)} %pick_rows.3.after_ref), channel_id=1, source_target_pairs={{0,24},{1,25},{2,26},{3,27},{4,28},{5,29},{6,30},{7,31},{8,16},{9,... | collective-permute-start | bytes 98312 | tf_op jit(solution)/shard_map/ppermute | solution.py:431
  3.4 0.4 %short_tables.1 = (bf16[2,512,256]{2,1,0:T(8,128)(2,1)S(1)}, f32[2,16,128]{2,1,0:T(8,128)S(1)}) custom-call(bf16[8,2048]{1,0:T(8,128)(2,1)S(1)} %pick_rows.3.after_ref), custom_call_target="tpu_custom_call" | custom-call | flops 5000000000 | bytes 1000000 | tf_op jit(solution)/shard_map/short_tables/pallas_call | solution.py:489
  3.8 0.0 copy-start.3
  3.8 0.6 %receiver_spectra.1 = (bf16[256,128]{1,0:T(8,128)(2,1)S(1)}, f32[64,128]{1,0:T(8,128)S(1)}, f32[64,128]{1,0:T(8,128)S(1)}) custom-call(s32[8,128]{1,0:T(8,128)S(1)} %get-tuple-element.23.info_ref, s32[4,128]{1,0:T(4,128)S(1)} %bitcast.4, bf16[4,4,2048]{2,1,0:T(4,128)(2,1)S(1)} %copy-done, f32[2,16,128]{2,1,0:T(8,128)S(1)} %get-tuple-element.21.twiddle_ref.refs_4_, ...), custom_call_target="tpu_custom_call" | custom-call | flops 5000000000 | bytes 1000000 | tf_op jit(solution)/shard_map/receiver_spectra/pallas_call | solution.py:504
  4.4 0.1 pick_rows.2.refs_2_
  4.5 0.9 %collective-permute-done.1.refs_3_ = bf16[8,2048]{1,0:T(8,128)(2,1)S(1)} collective-permute-done((bf16[8,2048]{1,0:T(8,128)(2,1)S(1)}, bf16[8,2048]{1,0:T(8,128)(2,1)S(1)}, u32[]{:S(2)}, u32[]{:S(2)}) %collective-permute-start.1) | collective-permute-done | bytes 32800 | tf_op jit(solution)/shard_map/ppermute | solution.py:431
  5.3 0.4 %source_spectra.1 = (bf16[128,128]{1,0:T(8,128)(2,1)S(1)}, bf16[256,128]{1,0:T(8,128)(2,1)S(1)}) custom-call(f32[8,128]{1,0:T(8,128)S(1)} %bitcast.2, f32[8,128]{1,0:T(8,128)S(1)} %get-tuple-element.19.refs_1_, bf16[8,2048]{1,0:T(8,128)(2,1)S(1)} %pick_rows.2.refs_2_, bf16[8,2048]{1,0:T(8,128)(2,1)S(1)} %collective-permute-done.1.refs_3_, ...), custom_call_target="tpu_custom_call" | custom-call | tf_op jit(solution)/shard_map/source_spectra/pallas_call | solution.py:522
  5.7 0.4 %collective-permute-start.3 = (bf16[128,128]{1,0:T(8,128)(2,1)S(1)}, bf16[128,128]{1,0:T(8,128)(2,1)S(1)}, u32[]{:S(2)}, u32[]{:S(2)}) collective-permute-start(bf16[128,128]{1,0:T(8,128)(2,1)S(1)} %get-tuple-element.28), channel_id=1, source_target_pairs={{0,12},{1,13},{2,14},{3,15},{4,8},{5,9},{6,10},{7,11},{8,4},{9,5},... | collective-permute-start | bytes 98312 | tf_op jit(solution)/shard_map/ppermute | solution.py:431
  6.1 1.3 %collective-permute-start.2 = (bf16[256,128]{1,0:T(8,128)(2,1)S(1)}, bf16[256,128]{1,0:T(8,128)(2,1)S(1)}, u32[]{:S(2)}, u32[]{:S(2)}) collective-permute-start(bf16[256,128]{1,0:T(8,128)(2,1)S(1)} %get-tuple-element.25), channel_id=1, source_target_pairs={{0,9},{1,8},{2,11},{3,10},{4,13},{5,12},{6,15},{7,14},{8,1},{9,0},... | collective-permute-start | bytes 196616 | tf_op jit(solution)/shard_map/ppermute | solution.py:431
  7.4 3.5 %collective-permute-done.3 = bf16[128,128]{1,0:T(8,128)(2,1)S(1)} collective-permute-done((bf16[128,128]{1,0:T(8,128)(2,1)S(1)}, bf16[128,128]{1,0:T(8,128)(2,1)S(1)}, u32[]{:S(2)}, u32[]{:S(2)}) %collective-permute-start.3) | collective-permute-done | bytes 32800 | tf_op jit(solution)/shard_map/ppermute | solution.py:431
  10.9 0.0 collective-permute-start.5
  10.9 0.0 collective-permute-done.2.refs_1_.after_ref
  10.9 0.5 %collective-permute-start.4 = (bf16[256,128]{1,0:T(8,128)(2,1)S(1)}, bf16[256,128]{1,0:T(8,128)(2,1)S(1)}, u32[]{:S(2)}, u32[]{:S(2)}) collective-permute-start(bf16[256,128]{1,0:T(8,128)(2,1)S(1)} %pass_on.2), channel_id=1, source_target_pairs={{0,8},{1,9},{2,10},{3,11},{4,12},{5,13},{6,14},{7,15},{8,0},{9,1},... | collective-permute-start | bytes 196616 | tf_op jit(solution)/shard_map/ppermute | solution.py:431
  11.4 0.0 copy-done.3
  11.4 0.5 %correlate_part.5 = (bf16[16,512]{1,0:T(8,128)(2,1)S(1)}, bf16[16,512]{1,0:T(8,128)(2,1)S(1)}) custom-call(bf16[2048,512]{1,0:T(8,128)(2,1)S(1)} %copy-done.3, bf16[256,128]{1,0:T(8,128)(2,1)S(1)} %collective-permute-done.2.refs_1_.after_ref, f32[64,128]{1,0:T(8,128)S(1)} %get-tuple-element.26.refs_2_, ...), custom_call_target="tpu_custom_call" | custom-call | flops 1000000000 | bytes 1000000 | tf_op jit(solution)/shard_map/correlate_part/pallas_call | solution.py:553
  11.9 0.4 %collective-permute-done.4.refs_3_ = bf16[256,128]{1,0:T(8,128)(2,1)S(1)} collective-permute-done((bf16[256,128]{1,0:T(8,128)(2,1)S(1)}, bf16[256,128]{1,0:T(8,128)(2,1)S(1)}, u32[]{:S(2)}, u32[]{:S(2)}) %collective-permute-start.4) | collective-permute-done | bytes 65568 | tf_op jit(solution)/shard_map/ppermute | solution.py:431
  12.3 0.4 %correlate_part.6.after_ref = bf16[16,512]{1,0:T(8,128)(2,1)S(1)} custom-call(bf16[2048,512]{1,0:T(8,128)(2,1)S(1)} %copy-done.3, bf16[256,128]{1,0:T(8,128)(2,1)S(1)} %collective-permute-done.2.refs_1_.after_ref, f32[64,128]{1,0:T(8,128)S(1)} %get-tuple-element.26.refs_2_, bf16[256,128]{1,0:T(8,128)(2,1)S(1)} %collective-permute-done.4.refs_3_), custom_call_target="tpu_custom_call" | custom-call | flops 1000000000 | bytes 1000000 | tf_op jit(solution)/shard_map/correlate_part/pallas_call | solution.py:553
  12.7 2.3 %collective-permute-done.5.value_ref = bf16[256,128]{1,0:T(8,128)(2,1)S(1)} collective-permute-done((bf16[256,128]{1,0:T(8,128)(2,1)S(1)}, bf16[256,128]{1,0:T(8,128)(2,1)S(1)}, u32[]{:S(2)}, u32[]{:S(2)}) %collective-permute-start.5) | collective-permute-done | bytes 65568 | tf_op jit(solution)/shard_map/ppermute | solution.py:431
  15.0 0.4 %collective-permute-start.6 = (bf16[256,128]{1,0:T(8,128)(2,1)S(1)}, bf16[256,128]{1,0:T(8,128)(2,1)S(1)}, u32[]{:S(2)}, u32[]{:S(2)}) collective-permute-start(bf16[256,128]{1,0:T(8,128)(2,1)S(1)} %pass_on.3.refs_4_.refs_3_), channel_id=1, source_target_pairs={{0,8},{1,9},{2,10},{3,11},{4,12},{5,13},{6,14},{7,15},{8,0},{9,1},... | collective-permute-start | bytes 196616 | tf_op jit(solution)/shard_map/ppermute | solution.py:431
  15.4 0.4 %correlate_part.8 = bf16[16,512]{1,0:T(8,128)(2,1)S(1)} custom-call(bf16[2048,512]{1,0:T(8,128)(2,1)S(1)} %copy-done.3, bf16[256,128]{1,0:T(8,128)(2,1)S(1)} %collective-permute-done.2.refs_1_.after_ref, f32[64,128]{1,0:T(8,128)S(1)} %get-tuple-element.26.refs_2_, bf16[256,128]{1,0:T(8,128)(2,1)S(1)} %pass_on.3.refs_4_.refs_3_), custom_call_target="tpu_custom_call" | custom-call | flops 1000000000 | bytes 1000000 | tf_op jit(solution)/shard_map/correlate_part/pallas_call | solution.py:553
  15.8 0.5 %collective-permute-done.6.refs_5_.refs_3_ = bf16[256,128]{1,0:T(8,128)(2,1)S(1)} collective-permute-done((bf16[256,128]{1,0:T(8,128)(2,1)S(1)}, bf16[256,128]{1,0:T(8,128)(2,1)S(1)}, u32[]{:S(2)}, u32[]{:S(2)}) %collective-permute-start.6) | collective-permute-done | bytes 65568 | tf_op jit(solution)/shard_map/ppermute | solution.py:431
  16.3 0.4 %correlate_part.9 = bf16[16,512]{1,0:T(8,128)(2,1)S(1)} custom-call(bf16[2048,512]{1,0:T(8,128)(2,1)S(1)} %copy-done.3, bf16[256,128]{1,0:T(8,128)(2,1)S(1)} %collective-permute-done.2.refs_1_.after_ref, f32[64,128]{1,0:T(8,128)S(1)} %get-tuple-element.26.refs_2_, bf16[256,128]{1,0:T(8,128)(2,1)S(1)} %collective-permute-done.6.refs_5_.refs_3_), custom_call_target="tpu_custom_call" | custom-call | flops 1000000000 | bytes 1000000 | tf_op jit(solution)/shard_map/correlate_part/pallas_call | solution.py:553
  16.7 1.5 %collective-permute-start.7 = (bf16[64,512]{1,0:T(8,128)(2,1)S(1)}, bf16[64,512]{1,0:T(8,128)(2,1)S(1)}, u32[]{:S(2)}, u32[]{:S(2)}) collective-permute-start(bf16[64,512]{1,0:T(8,128)(2,1)S(1)} %pad_maximum_fusion), channel_id=1, source_target_pairs={{0,9},{1,8},{2,11},{3,10},{4,13},{5,12},{6,15},{7,14},{8,1},{9,0},... | collective-permute-start | bytes 196616 | tf_op jit(solution)/shard_map/ppermute | solution.py:431
  18.3 0.6 %correlate_part.7.refs_1_ = bf16[48,512]{1,0:T(8,128)(2,1)S(1)} custom-call(bf16[2048,512]{1,0:T(8,128)(2,1)S(1)} %copy-done.3, bf16[256,128]{1,0:T(8,128)(2,1)S(1)} %get-tuple-element.24.refs_6_.refs_3_.refs_1_, f32[64,128]{1,0:T(8,128)S(1)} %get-tuple-element.27.refs_4_.refs_2_, bf16[256,128]{1,0:T(8,128)(2,1)S(1)} %collective-permute-done.4.refs_3_, ...), custom_call_target="tpu_custom_call" | custom-call | flops 1000000000 | bytes 1000000 | tf_op jit(solution)/shard_map/correlate_part/pallas_call | solution.py:553
  18.9 2.0 %collective-permute-done.7.refs_2_ = bf16[64,512]{1,0:T(8,128)(2,1)S(1)} collective-permute-done((bf16[64,512]{1,0:T(8,128)(2,1)S(1)}, bf16[64,512]{1,0:T(8,128)(2,1)S(1)}, u32[]{:S(2)}, u32[]{:S(2)}) %collective-permute-start.7) | collective-permute-done | bytes 65568 | tf_op jit(solution)/shard_map/ppermute | solution.py:431
  20.9 0.7 %place_rows.1 = bf16[2,16,4,512]{3,2,1,0:T(4,128)(2,1)} custom-call(bf16[16,512]{1,0:T(8,128)(2,1)S(1)} %get-tuple-element.29.refs_0_, bf16[48,512]{1,0:T(8,128)(2,1)S(1)} %correlate_part.7.refs_1_, bf16[64,512]{1,0:T(8,128)(2,1)S(1)} %collective-permute-done.7.refs_2_), custom_call_target="tpu_custom_call" | custom-call | tf_op jit(solution)/shard_map/place_rows/pallas_call | solution.py:579
  (10 shorter events, 0.1 us)
Async XLA Ops:
  0.0 1.9 %copy-start = (bf16[4,4,2048]{2,1,0:T(4,128)(2,1)S(1)}, bf16[4,4,2048]{2,1,0:T(4,128)(2,1)}, u32[]{:S(2)}) copy-start(bf16[4,4,2048]{2,1,0:T(4,128)(2,1)} %raw_ref.1) | copy-start | bytes 196612
  0.0 0.8 %copy-start.2 = (s32[2]{0:T(128)S(1)}, s32[2]{0:T(128)}, u32[]{:S(2)}) copy-start(s32[2]{0:T(128)} %ids_ref.1) | copy-start | bytes 28
  0.0 0.8 %copy-start.1 = (s32[128,4]{0,1:T(4,128)S(1)}, s32[128,4]{0,1:T(4,128)}, u32[]{:S(2)}) copy-start(s32[128,4]{0,1:T(4,128)} %param.5) | copy-start | bytes 6148
  0.0 1.9 %collective-permute-start = (bf16[4,4,2048]{2,1,0:T(4,128)(2,1)}, bf16[4,4,2048]{2,1,0:T(4,128)(2,1)S(1)}, u32[]{:S(2)}, u32[]{:S(2)}) collective-permute-start(bf16[4,4,2048]{2,1,0:T(4,128)(2,1)} %raw_ref.1), channel_id=1, source_target_pairs={{0,8},{1,9},{2,10},{3,11},{4,12},{5,13},{6,14},{7,15},{8,0},{9,1},... | collective-permute-start | bytes 196616 | tf_op jit(solution)/shard_map/ppermute | solution.py:431
  1.9 3.4 %collective-permute-start.1 = (bf16[8,2048]{1,0:T(8,128)(2,1)S(1)}, bf16[8,2048]{1,0:T(8,128)(2,1)S(1)}, u32[]{:S(2)}, u32[]{:S(2)}) collective-permute-start(bf16[8,2048]{1,0:T(8,128)(2,1)S(1)} %pick_rows.3.after_ref), channel_id=1, source_target_pairs={{0,24},{1,25},{2,26},{3,27},{4,28},{5,29},{6,30},{7,31},{8,16},{9,... | collective-permute-start | bytes 98312 | tf_op jit(solution)/shard_map/ppermute | solution.py:431
  3.8 7.6 %copy-start.3 = (bf16[2048,512]{1,0:T(8,128)(2,1)S(1)}, bf16[2048,512]{1,0:T(8,128)(2,1)}, u32[]{:S(2)}) copy-start(bf16[2048,512]{1,0:T(8,128)(2,1)} %constant.2.clone.refs_0_) | copy-start | bytes 6291460
  5.7 5.2 %collective-permute-start.3 = (bf16[128,128]{1,0:T(8,128)(2,1)S(1)}, bf16[128,128]{1,0:T(8,128)(2,1)S(1)}, u32[]{:S(2)}, u32[]{:S(2)}) collective-permute-start(bf16[128,128]{1,0:T(8,128)(2,1)S(1)} %get-tuple-element.28), channel_id=1, source_target_pairs={{0,12},{1,13},{2,14},{3,15},{4,8},{5,9},{6,10},{7,11},{8,4},{9,5},... | collective-permute-start | bytes 98312 | tf_op jit(solution)/shard_map/ppermute | solution.py:431
  6.1 4.8 %collective-permute-start.2 = (bf16[256,128]{1,0:T(8,128)(2,1)S(1)}, bf16[256,128]{1,0:T(8,128)(2,1)S(1)}, u32[]{:S(2)}, u32[]{:S(2)}) collective-permute-start(bf16[256,128]{1,0:T(8,128)(2,1)S(1)} %get-tuple-element.25), channel_id=1, source_target_pairs={{0,9},{1,8},{2,11},{3,10},{4,13},{5,12},{6,15},{7,14},{8,1},{9,0},... | collective-permute-start | bytes 196616 | tf_op jit(solution)/shard_map/ppermute | solution.py:431
  10.9 4.1 %collective-permute-start.5 = (bf16[256,128]{1,0:T(8,128)(2,1)S(1)}, bf16[256,128]{1,0:T(8,128)(2,1)S(1)}, u32[]{:S(2)}, u32[]{:S(2)}) collective-permute-start(bf16[256,128]{1,0:T(8,128)(2,1)S(1)} %constant_dynamic-update-slice_fusion.refs_5_.value_ref), channel_id=1, source_target_pairs={{0,10},{1,11},{2,8},{3,9},{4,14},{5,15},{6,12},{7,13},{8,2},{9,3},... | collective-permute-start | bytes 196616 | tf_op jit(solution)/shard_map/ppermute | solution.py:431
  10.9 1.4 %collective-permute-start.4 = (bf16[256,128]{1,0:T(8,128)(2,1)S(1)}, bf16[256,128]{1,0:T(8,128)(2,1)S(1)}, u32[]{:S(2)}, u32[]{:S(2)}) collective-permute-start(bf16[256,128]{1,0:T(8,128)(2,1)S(1)} %pass_on.2), channel_id=1, source_target_pairs={{0,8},{1,9},{2,10},{3,11},{4,12},{5,13},{6,14},{7,15},{8,0},{9,1},... | collective-permute-start | bytes 196616 | tf_op jit(solution)/shard_map/ppermute | solution.py:431
  15.0 1.3 %collective-permute-start.6 = (bf16[256,128]{1,0:T(8,128)(2,1)S(1)}, bf16[256,128]{1,0:T(8,128)(2,1)S(1)}, u32[]{:S(2)}, u32[]{:S(2)}) collective-permute-start(bf16[256,128]{1,0:T(8,128)(2,1)S(1)} %pass_on.3.refs_4_.refs_3_), channel_id=1, source_target_pairs={{0,8},{1,9},{2,10},{3,11},{4,12},{5,13},{6,14},{7,15},{8,0},{9,1},... | collective-permute-start | bytes 196616 | tf_op jit(solution)/shard_map/ppermute | solution.py:431
  16.7 4.1 %collective-permute-start.7 = (bf16[64,512]{1,0:T(8,128)(2,1)S(1)}, bf16[64,512]{1,0:T(8,128)(2,1)S(1)}, u32[]{:S(2)}, u32[]{:S(2)}) collective-permute-start(bf16[64,512]{1,0:T(8,128)(2,1)S(1)} %pad_maximum_fusion), channel_id=1, source_target_pairs={{0,9},{1,8},{2,11},{3,10},{4,13},{5,12},{6,15},{7,14},{8,1},{9,0},... | collective-permute-start | bytes 196616 | tf_op jit(solution)/shard_map/ppermute | solution.py:431

commit v5 on v4

--- a/solution.py
+++ b/solution.py
@@ -183,18 +183,14 @@
     out_ref[...] = relay_ref[...].astype(jnp.bfloat16)
 
 
-def holdings(member_bits):
+def panel_order(member_bits):
     held = [(0, 0)]
-    for bit in member_bits[:-1]:
+    for bit in member_bits:
         held += [(k ^ bit, 1 - odd) for k, odd in held]
-    brought = [(k ^ member_bits[-1], 1 - odd) for k, odd in held]
-    return held, brought
-
-
-def panel_order(member_bits):
-    held, brought = holdings(member_bits)
-    flip = lambda pieces: [(k, 1 - odd) for k, odd in pieces]
-    return held + flip(held) + brought + flip(brought)
+    return held
+
+
+MINE, MATE, CROSS, SAME = (0, 0), (1, 0), (1, 1), (0, 1)
 
 
 def flags_of(picks, flags):
@@ -280,7 +276,8 @@
 
 
 def receiver_kernel(radius, order, info_ref, usable_ref, raw_ref, twiddle_ref, table_ref, *rest):
-    spectra_ref, inverse_ref, other_ref, samples, relay = rest
+    spectra_ref, samples, relay = rest[0], rest[-2], rest[-1]
+    factor_refs = rest[1:-2]
     channels, windows, _ = raw_ref.shape
     members = lax.axis_size("dev")
     group, member = lax.axis_index("grp"), lax.axis_index("dev")
@@ -310,9 +307,9 @@
         offset = (member ^ k) * channels + (core + odd) % SRC_DEV
         blocks.append(jnp.where(lane == start + offset, 1.0, 0.0))
     sent = flags_of(jnp.concatenate(blocks, axis=0), flags)
-    theirs = ((group ^ 1) * members + (member ^ 1)) * channels
-    for ref, start in ((inverse_ref, first), (other_ref, theirs)):
-        received = flags_of(jnp.where(lane == start + row % channels, 1.0, 0.0), flags)
+    for ref, (core_flip, member_flip) in zip(factor_refs, (MINE, MATE, CROSS, SAME)):
+        whose = ((group ^ core_flip) * members + (member ^ member_flip)) * channels
+        received = flags_of(jnp.where(lane == whose + row % channels, 1.0, 0.0), flags)
         both = sent * jnp.concatenate([received] * len(order), axis=0)
         counts = jnp.sum(both, axis=1, keepdims=True)
         ref[...] = jnp.broadcast_to(1.0 / jnp.maximum(counts, 1.0), ref.shape)
@@ -402,7 +399,9 @@
     member = lax.axis_index("dev")
     core = lax.axis_index("grp") % SRC_DEV
     receivers = out_ref.shape[2]
-    whole = order + [(k ^ 1, 1 - odd) for k, odd in order]
+    whole = []
+    for core_flip, member_flip in (MINE, MATE, CROSS, SAME):
+        whole += [(k ^ member_flip, odd ^ core_flip) for k, odd in order]
     block = STEPS * receivers
     done = 0
     for ref in refs[:-1]:
@@ -501,15 +500,14 @@
 
     row_count = channels * windows
     pairs = len(order) * STEPS * channels
-    receivers, inverse, inverse_theirs = pl.pallas_call(
+    receivers, *factors = pl.pallas_call(
         functools.partial(receiver_kernel, radius, order),
         out_shape=[
             jax.ShapeDtypeStruct((2 * row_count * blocks, width), jnp.bfloat16),
-            jax.ShapeDtypeStruct((pairs, width), jnp.float32),
-            jax.ShapeDtypeStruct((pairs, width), jnp.float32),
-        ],
+        ]
+        + [jax.ShapeDtypeStruct((pairs, width), jnp.float32)] * 4,
         in_specs=[VMEM] * 5,
-        out_specs=[VMEM] * 3,
+        out_specs=[VMEM] * 5,
         scratch_shapes=[
             pltpu.VMEM((row_count, length), jnp.float32),
             pltpu.VMEM((2 * row_count * blocks, width), jnp.float32),
@@ -535,7 +533,8 @@
     held = piece
     for bit in member_bits[:-2]:
         held = jnp.concatenate([held, exchange(held, 1, bit)], axis=0)
-    theirs = exchange(passed, 1, 1)
+    cross = exchange(passed, *CROSS)
+    brought = exchange(held, 1, member_bits[-2])
 
     def pass_on(value, after):
         return pl.pallas_call(
@@ -564,28 +563,28 @@
             name="correlate_part",
         )(ltable, *[array for pair in sets for array in pair], *buffers)
 
-    mine, other = (receivers, inverse), (theirs, inverse_theirs)
-    brought = exchange(held, 1, member_bits[-2])
-    held_other = exchange(pass_on(held, theirs), 1, 0)
-    early_theirs, early = part(0, [other, mine], held)
-    (next_theirs,) = part(pairs // 4, [other], held_other)
-    brought = pass_on(brought, next_theirs)
-    brought_other = exchange(brought, 1, 0)
-    (middle_theirs,) = part(pairs // 2, [other], brought)
-    (late_theirs,) = part(pairs // 4 * 3, [other], brought_other)
-    (late,) = part(pairs // 4, [mine], held_other, brought, brought_other)
-    lag_rows = [early_theirs, next_theirs, middle_theirs, late_theirs]
-    back = exchange(jnp.concatenate(lag_rows, axis=0), 1, 1)
+    same = exchange(pass_on(cross, receivers), *MATE)
+    mate = exchange(pass_on(receivers, same), *MATE)
+    sets = list(zip((receivers, mate, cross, same), factors))
+    early = part(0, sets[2:3], held) + part(0, sets[3:], held)
+    later = part(pairs // 2, sets[2:], brought)
+    back_cross, back_same = [
+        exchange(jnp.concatenate([a, b], axis=0), *which)
+        for a, b, which in zip(early, later, (CROSS, SAME))
+    ]
+    (mate_rows,) = part(0, sets[1:2], held, brought)
+    back_mate = exchange(mate_rows, *MATE)
+    (rows,) = part(0, sets[:1], held, brought)
     return pl.pallas_call(
         functools.partial(place_kernel, order),
         out_shape=jax.ShapeDtypeStruct(
             (STEPS, members * SRC_DEV, channels, NLAG), jnp.bfloat16
         ),
-        in_specs=[VMEM] * 3,
+        in_specs=[VMEM] * 4,
         out_specs=VMEM,
         compiler_params=PARAMS,
         name="place_rows",
-    )(early, late, back)
+    )(rows, back_mate, back_cross, back_same)
 
 
 def solution(mesh):

time: 21.7 us -> 21.8 us (level)
  waiting for transfers between devices: 9.88 us -> 9.21 us
  starting transfers between devices: 6.28 us -> 6.9 us
    ppermute x8 -> x10, waiting for transfers between devices: 9.88 us -> 9.21 us  [exchange(): return lax.ppermute(value, AXES, pairs)]
    ppermute x8 -> x10, starting transfers between devices: 6.28 us -> 6.9 us  [exchange(): return lax.ppermute(value, AXES, pairs)]
  transfers between devices with their start and end apart: 8 -> 10, of which waited for: 7 -> 7; matrix products, arithmetic and copies ran while one was open for 0% -> 0% of each run, Pallas kernels for 17% -> 17%
where the time goes in v5:
time: 21.8 us; the launch traced here: 21.6 us
  waiting for transfers between devices  9.21 us (42%)
  starting transfers between devices  6.9 us (32%)
  Pallas kernels  5.35 us (25%)
    ppermute x10, waiting for transfers between devices, exchange(): return lax.ppermute(value, AXES, pairs)  9.21 us
    ppermute x10, starting transfers between devices, exchange(): return lax.ppermute(value, AXES, pairs)  6.9 us
    pallas_call x5, Pallas kernels, part(): pl.pallas_call(functools.partial(part_kernel, windows, first, len(sets)),...  2.38 us
    pallas_call x1, Pallas kernels, on_device(): pl.pallas_call(functools.partial(choice_kernel, halves, channels), out_sh...  0.77 us
    pallas_call x1, Pallas kernels, on_device(): pl.pallas_call(functools.partial(place_kernel, order), out_shape=jax.Shap...  0.69 us
    pallas_call x1, Pallas kernels, on_device(): pl.pallas_call(functools.partial(receiver_kernel, radius, order), out_sha...  0.61 us
  transfers between devices with their start and end apart: 10, of which 7 were waited for; matrix products, arithmetic and copies ran while one was open for 0% of the time, Pallas kernels for 17%

profile of v5, /device:TPU:25, one launch (start us, length us, event | category | flops | bytes accessed | tf_op | source)
XLA Modules:
  0.0 21.6 jit_solution(11620388950770854370)
XLA Ops:
  0.0 0.7 %collective-permute-start = (bf16[4,4,2048]{2,1,0:T(4,128)(2,1)}, bf16[4,4,2048]{2,1,0:T(4,128)(2,1)S(1)}, u32[]{:S(2)}, u32[]{:S(2)}) collective-permute-start(bf16[4,4,2048]{2,1,0:T(4,128)(2,1)} %own_ref.3), channel_id=1, source_target_pairs={{0,8},{1,9},{2,10},{3,11},{4,12},{5,13},{6,14},{7,15},{8,0},{9,1},... | collective-permute-start | bytes 196616 | tf_op jit(solution)/shard_map/ppermute | solution.py:430
  0.8 0.8 %choose_rows.1 = (f32[8,128]{1,0:T(8,128)S(1)}, f32[8,128]{1,0:T(8,128)S(1)}, f32[1,8,128]{2,1,0:T(8,128)S(1)}, s32[8,128]{1,0:T(8,128)S(1)}) custom-call(s32[2]{0:T(128)S(1)} %copy-done.2, s32[4,128]{1,0:T(4,128)S(1)} %bitcast.3, f32[8,128]{1,0:T(8,128)S(1)} %ahead.1.after_ref), custom_call_target="tpu_custom_call" | custom-call | tf_op jit(solution)/shard_map/choose_rows/pallas_call | solution.py:455
  1.5 0.3 %collective-permute-done.other_ref = bf16[4,4,2048]{2,1,0:T(4,128)(2,1)S(1)} collective-permute-done((bf16[4,4,2048]{2,1,0:T(4,128)(2,1)}, bf16[4,4,2048]{2,1,0:T(4,128)(2,1)S(1)}, u32[]{:S(2)}, u32[]{:S(2)}) %collective-permute-start) | collective-permute-done | bytes 65568 | tf_op jit(solution)/shard_map/ppermute | solution.py:430
  1.9 1.5 %collective-permute-start.1 = (bf16[8,2048]{1,0:T(8,128)(2,1)S(1)}, bf16[8,2048]{1,0:T(8,128)(2,1)S(1)}, u32[]{:S(2)}, u32[]{:S(2)}) collective-permute-start(bf16[8,2048]{1,0:T(8,128)(2,1)S(1)} %pick_rows.2.after_ref), channel_id=1, source_target_pairs={{0,24},{1,25},{2,26},{3,27},{4,28},{5,29},{6,30},{7,31},{8,16},{9,... | collective-permute-start | bytes 98312 | tf_op jit(solution)/shard_map/ppermute | solution.py:430
  3.4 0.4 %short_tables.1 = (bf16[2,512,256]{2,1,0:T(8,128)(2,1)S(1)}, f32[2,16,128]{2,1,0:T(8,128)S(1)}) custom-call(bf16[8,2048]{1,0:T(8,128)(2,1)S(1)} %pick_rows.2.after_ref), custom_call_target="tpu_custom_call" | custom-call | flops 5000000000 | bytes 1000000 | tf_op jit(solution)/shard_map/short_tables/pallas_call | solution.py:488
  3.8 0.0 copy-start.3
  3.8 0.6 %receiver_spectra.1 = (bf16[256,128]{1,0:T(8,128)(2,1)S(1)}, f32[32,128]{1,0:T(8,128)S(1)}, f32[32,128]{1,0:T(8,128)S(1)}, f32[32,128]{1,0:T(8,128)S(1)}, f32[32,128]{1,0:T(8,128)S(1)}) custom-call(s32[8,128]{1,0:T(8,128)S(1)} %get-tuple-element.20.info_ref, s32[4,128]{1,0:T(4,128)S(1)} %bitcast.4, bf16[4,4,2048]{2,1,0:T(4,128)(2,1)S(1)} %copy-done, ...), custom_call_target="tpu_custom_call" | custom-call | flops 5000000000 | bytes 1000000 | tf_op jit(solution)/shard_map/receiver_spectra/pallas_call | solution.py:503
  4.4 0.1 pick_rows.3.refs_2_
  4.5 0.8 %collective-permute-done.1.refs_3_ = bf16[8,2048]{1,0:T(8,128)(2,1)S(1)} collective-permute-done((bf16[8,2048]{1,0:T(8,128)(2,1)S(1)}, bf16[8,2048]{1,0:T(8,128)(2,1)S(1)}, u32[]{:S(2)}, u32[]{:S(2)}) %collective-permute-start.1) | collective-permute-done | bytes 32800 | tf_op jit(solution)/shard_map/ppermute | solution.py:430
  5.3 0.4 %source_spectra.1 = (bf16[128,128]{1,0:T(8,128)(2,1)S(1)}, bf16[256,128]{1,0:T(8,128)(2,1)S(1)}) custom-call(f32[8,128]{1,0:T(8,128)S(1)} %bitcast.2, f32[8,128]{1,0:T(8,128)S(1)} %get-tuple-element.27.refs_1_, bf16[8,2048]{1,0:T(8,128)(2,1)S(1)} %pick_rows.3.refs_2_, bf16[8,2048]{1,0:T(8,128)(2,1)S(1)} %collective-permute-done.1.refs_3_, ...), custom_call_target="tpu_custom_call" | custom-call | tf_op jit(solution)/shard_map/source_spectra/pallas_call | solution.py:520
  5.7 0.4 %collective-permute-start.2 = (bf16[128,128]{1,0:T(8,128)(2,1)S(1)}, bf16[128,128]{1,0:T(8,128)(2,1)S(1)}, u32[]{:S(2)}, u32[]{:S(2)}) collective-permute-start(bf16[128,128]{1,0:T(8,128)(2,1)S(1)} %get-tuple-element.28), channel_id=1, source_target_pairs={{0,12},{1,13},{2,14},{3,15},{4,8},{5,9},{6,10},{7,11},{8,4},{9,5},... | collective-permute-start | bytes 98312 | tf_op jit(solution)/shard_map/ppermute | solution.py:430
  6.1 1.3 %collective-permute-start.4 = (bf16[256,128]{1,0:T(8,128)(2,1)S(1)}, bf16[256,128]{1,0:T(8,128)(2,1)S(1)}, u32[]{:S(2)}, u32[]{:S(2)}) collective-permute-start(bf16[256,128]{1,0:T(8,128)(2,1)S(1)} %get-tuple-element.29), channel_id=1, source_target_pairs={{0,9},{1,8},{2,11},{3,10},{4,13},{5,12},{6,15},{7,14},{8,1},{9,0},... | collective-permute-start | bytes 196616 | tf_op jit(solution)/shard_map/ppermute | solution.py:430
  7.4 3.5 %collective-permute-done.2 = bf16[128,128]{1,0:T(8,128)(2,1)S(1)} collective-permute-done((bf16[128,128]{1,0:T(8,128)(2,1)S(1)}, bf16[128,128]{1,0:T(8,128)(2,1)S(1)}, u32[]{:S(2)}, u32[]{:S(2)}) %collective-permute-start.2) | collective-permute-done | bytes 32800 | tf_op jit(solution)/shard_map/ppermute | solution.py:430
  10.9 0.0 collective-permute-start.3
  10.9 0.0 collective-permute-done.4.value_ref.refs_1_
  11.0 0.5 %collective-permute-start.5 = (bf16[256,128]{1,0:T(8,128)(2,1)S(1)}, bf16[256,128]{1,0:T(8,128)(2,1)S(1)}, u32[]{:S(2)}, u32[]{:S(2)}) collective-permute-start(bf16[256,128]{1,0:T(8,128)(2,1)S(1)} %pass_on.2), channel_id=1, source_target_pairs={{0,8},{1,9},{2,10},{3,11},{4,12},{5,13},{6,14},{7,15},{8,0},{9,1},... | collective-permute-start | bytes 196616 | tf_op jit(solution)/shard_map/ppermute | solution.py:430
  11.4 0.4 %correlate_part.7 = bf16[16,512]{1,0:T(8,128)(2,1)S(1)} custom-call(bf16[2048,512]{1,0:T(8,128)(2,1)S(1)} %copy-done.3, bf16[256,128]{1,0:T(8,128)(2,1)S(1)} %collective-permute-done.4.value_ref.refs_1_, f32[32,128]{1,0:T(8,128)S(1)} %get-tuple-element.31.refs_2_, bf16[256,128]{1,0:T(8,128)(2,1)S(1)} %constant_dynamic-update-slice_fusion.refs_3_), custom_call_target="tpu_custom_call" | custom-call | flops 1000000000 | bytes 1000000 | tf_op jit(solution)/shard_map/correlate_part/pallas_call | solution.py:552
  11.8 0.5 %collective-permute-done.5.after_ref.refs_3_.refs_1_ = bf16[256,128]{1,0:T(8,128)(2,1)S(1)} collective-permute-done((bf16[256,128]{1,0:T(8,128)(2,1)S(1)}, bf16[256,128]{1,0:T(8,128)(2,1)S(1)}, u32[]{:S(2)}, u32[]{:S(2)}) %collective-permute-start.5) | collective-permute-done | bytes 65568 | tf_op jit(solution)/shard_map/ppermute | solution.py:430
  12.3 0.4 %correlate_part.9 = bf16[16,512]{1,0:T(8,128)(2,1)S(1)} custom-call(bf16[2048,512]{1,0:T(8,128)(2,1)S(1)} %copy-done.3, bf16[256,128]{1,0:T(8,128)(2,1)S(1)} %collective-permute-done.5.after_ref.refs_3_.refs_1_, f32[32,128]{1,0:T(8,128)S(1)} %get-tuple-element.32.refs_4_.refs_2_, bf16[256,128]{1,0:T(8,128)(2,1)S(1)} %constant_dynamic-update-slice_fusion.refs_3_), custom_call_target="tpu_custom_call" | custom-call | flops 1000000000 | bytes 1000000 | tf_op jit(solution)/shard_map/correlate_part/pallas_call | solution.py:552
  12.7 2.3 %collective-permute-done.3.refs_4_.refs_5_ = bf16[256,128]{1,0:T(8,128)(2,1)S(1)} collective-permute-done((bf16[256,128]{1,0:T(8,128)(2,1)S(1)}, bf16[256,128]{1,0:T(8,128)(2,1)S(1)}, u32[]{:S(2)}, u32[]{:S(2)}) %collective-permute-start.3) | collective-permute-done | bytes 65568 | tf_op jit(solution)/shard_map/ppermute | solution.py:430
  15.0 0.5 %correlate_part.8 = (bf16[16,512]{1,0:T(8,128)(2,1)S(1)}, bf16[16,512]{1,0:T(8,128)(2,1)S(1)}) custom-call(bf16[2048,512]{1,0:T(8,128)(2,1)S(1)} %copy-done.3, bf16[256,128]{1,0:T(8,128)(2,1)S(1)} %collective-permute-done.4.value_ref.refs_1_, f32[32,128]{1,0:T(8,128)S(1)} %get-tuple-element.31.refs_2_, ...), custom_call_target="tpu_custom_call" | custom-call | flops 1000000000 | bytes 1000000 | tf_op jit(solution)/shard_map/correlate_part/pallas_call | solution.py:552
  15.6 1.3 %collective-permute-start.9 = (bf16[32,512]{1,0:T(8,128)(2,1)S(1)}, bf16[32,512]{1,0:T(8,128)(2,1)S(1)}, u32[]{:S(2)}, u32[]{:S(2)}) collective-permute-start(bf16[32,512]{1,0:T(8,128)(2,1)S(1)} %pad_maximum_fusion.1), channel_id=1, source_target_pairs={{0,1},{1,0},{2,3},{3,2},{4,5},{5,4},{6,7},{7,6},{8,9},{9,8},{10,11... | collective-permute-start | bytes 98312 | tf_op jit(solution)/shard_map/ppermute | solution.py:430
  16.9 0.7 %collective-permute-start.6 = (bf16[256,128]{1,0:T(8,128)(2,1)S(1)}, bf16[256,128]{1,0:T(8,128)(2,1)S(1)}, u32[]{:S(2)}, u32[]{:S(2)}) collective-permute-start(bf16[256,128]{1,0:T(8,128)(2,1)S(1)} %pass_on.3), channel_id=1, source_target_pairs={{0,8},{1,9},{2,10},{3,11},{4,12},{5,13},{6,14},{7,15},{8,0},{9,1},... | collective-permute-start | bytes 196616 | tf_op jit(solution)/shard_map/ppermute | solution.py:430
  17.5 0.2 collective-permute-start.8
  17.7 0.7 %collective-permute-done.6.refs_1_ = bf16[256,128]{1,0:T(8,128)(2,1)S(1)} collective-permute-done((bf16[256,128]{1,0:T(8,128)(2,1)S(1)}, bf16[256,128]{1,0:T(8,128)(2,1)S(1)}, u32[]{:S(2)}, u32[]{:S(2)}) %collective-permute-start.6) | collective-permute-done | bytes 65568 | tf_op jit(solution)/shard_map/ppermute | solution.py:430
  18.4 0.5 %correlate_part.6 = bf16[32,512]{1,0:T(8,128)(2,1)S(1)} custom-call(bf16[2048,512]{1,0:T(8,128)(2,1)S(1)} %copy-done.3, bf16[256,128]{1,0:T(8,128)(2,1)S(1)} %collective-permute-done.6.refs_1_, f32[32,128]{1,0:T(8,128)S(1)} %get-tuple-element.30.refs_2_, bf16[256,128]{1,0:T(8,128)(2,1)S(1)} %constant_dynamic-update-slice_fusion.refs_3_, ...), custom_call_target="tpu_custom_call" | custom-call | flops 1000000000 | bytes 1000000 | tf_op jit(solution)/shard_map/correlate_part/pallas_call | solution.py:552
  19.0 0.4 %collective-permute-start.7 = (bf16[32,512]{1,0:T(8,128)(2,1)S(1)}, bf16[32,512]{1,0:T(8,128)(2,1)S(1)}, u32[]{:S(2)}, u32[]{:S(2)}) collective-permute-start(bf16[32,512]{1,0:T(8,128)(2,1)S(1)} %correlate_part.6), channel_id=1, source_target_pairs={{0,8},{1,9},{2,10},{3,11},{4,12},{5,13},{6,14},{7,15},{8,0},{9,1},... | collective-permute-start | bytes 98312 | tf_op jit(solution)/shard_map/ppermute | solution.py:430
  19.3 0.5 %correlate_part.5.refs_0_ = bf16[32,512]{1,0:T(8,128)(2,1)S(1)} custom-call(bf16[2048,512]{1,0:T(8,128)(2,1)S(1)} %copy-done.3, bf16[256,128]{1,0:T(8,128)(2,1)S(1)} %get-tuple-element.24.refs_6_.refs_1_.after_ref.value_ref, f32[32,128]{1,0:T(8,128)S(1)} %get-tuple-element.25.refs_2_, bf16[256,128]{1,0:T(8,128)(2,1)S(1)} %constant_dynamic-update-slice_fusion.refs_3_, ...), custom_call_target="tpu_custom_call" | custom-call | flops 1000000000 | bytes 1000000 | tf_op jit(solution)/shard_map/correlate_part/pallas_call | solution.py:552
  19.8 0.0 collective-permute-done.9.refs_3_
  19.9 1.0 %collective-permute-done.8.refs_2_ = bf16[32,512]{1,0:T(8,128)(2,1)S(1)} collective-permute-done((bf16[32,512]{1,0:T(8,128)(2,1)S(1)}, bf16[32,512]{1,0:T(8,128)(2,1)S(1)}, u32[]{:S(2)}, u32[]{:S(2)}) %collective-permute-start.8) | collective-permute-done | bytes 32800 | tf_op jit(solution)/shard_map/ppermute | solution.py:430
  20.9 0.0 collective-permute-done.7.refs_1_
  20.9 0.7 %place_rows.1 = bf16[2,16,4,512]{3,2,1,0:T(4,128)(2,1)} custom-call(bf16[32,512]{1,0:T(8,128)(2,1)S(1)} %correlate_part.5.refs_0_, bf16[32,512]{1,0:T(8,128)(2,1)S(1)} %collective-permute-done.7.refs_1_, bf16[32,512]{1,0:T(8,128)(2,1)S(1)} %collective-permute-done.8.refs_2_, bf16[32,512]{1,0:T(8,128)(2,1)S(1)} %collective-permute-done.9.refs_3_), custom_call_target="tpu_custom_call" | custom-call | tf_op jit(solution)/shard_map/place_rows/pallas_call | solution.py:578
  (15 shorter events, 0.1 us)
Async XLA Ops:
  0.0 1.9 %copy-start = (bf16[4,4,2048]{2,1,0:T(4,128)(2,1)S(1)}, bf16[4,4,2048]{2,1,0:T(4,128)(2,1)}, u32[]{:S(2)}) copy-start(bf16[4,4,2048]{2,1,0:T(4,128)(2,1)} %own_ref.3) | copy-start | bytes 196612
  0.0 0.8 %copy-start.2 = (s32[2]{0:T(128)S(1)}, s32[2]{0:T(128)}, u32[]{:S(2)}) copy-start(s32[2]{0:T(128)} %ids_ref.1) | copy-start | bytes 28
  0.0 0.8 %copy-start.1 = (s32[128,4]{0,1:T(4,128)S(1)}, s32[128,4]{0,1:T(4,128)}, u32[]{:S(2)}) copy-start(s32[128,4]{0,1:T(4,128)} %param.5) | copy-start | bytes 6148
  0.0 1.9 %collective-permute-start = (bf16[4,4,2048]{2,1,0:T(4,128)(2,1)}, bf16[4,4,2048]{2,1,0:T(4,128)(2,1)S(1)}, u32[]{:S(2)}, u32[]{:S(2)}) collective-permute-start(bf16[4,4,2048]{2,1,0:T(4,128)(2,1)} %own_ref.3), channel_id=1, source_target_pairs={{0,8},{1,9},{2,10},{3,11},{4,12},{5,13},{6,14},{7,15},{8,0},{9,1},... | collective-permute-start | bytes 196616 | tf_op jit(solution)/shard_map/ppermute | solution.py:430
  1.9 3.4 %collective-permute-start.1 = (bf16[8,2048]{1,0:T(8,128)(2,1)S(1)}, bf16[8,2048]{1,0:T(8,128)(2,1)S(1)}, u32[]{:S(2)}, u32[]{:S(2)}) collective-permute-start(bf16[8,2048]{1,0:T(8,128)(2,1)S(1)} %pick_rows.2.after_ref), channel_id=1, source_target_pairs={{0,24},{1,25},{2,26},{3,27},{4,28},{5,29},{6,30},{7,31},{8,16},{9,... | collective-permute-start | bytes 98312 | tf_op jit(solution)/shard_map/ppermute | solution.py:430
  3.8 7.6 %copy-start.3 = (bf16[2048,512]{1,0:T(8,128)(2,1)S(1)}, bf16[2048,512]{1,0:T(8,128)(2,1)}, u32[]{:S(2)}) copy-start(bf16[2048,512]{1,0:T(8,128)(2,1)} %constant.2.clone.refs_0_) | copy-start | bytes 6291460
  5.7 5.2 %collective-permute-start.2 = (bf16[128,128]{1,0:T(8,128)(2,1)S(1)}, bf16[128,128]{1,0:T(8,128)(2,1)S(1)}, u32[]{:S(2)}, u32[]{:S(2)}) collective-permute-start(bf16[128,128]{1,0:T(8,128)(2,1)S(1)} %get-tuple-element.28), channel_id=1, source_target_pairs={{0,12},{1,13},{2,14},{3,15},{4,8},{5,9},{6,10},{7,11},{8,4},{9,5},... | collective-permute-start | bytes 98312 | tf_op jit(solution)/shard_map/ppermute | solution.py:430
  6.1 4.8 %collective-permute-start.4 = (bf16[256,128]{1,0:T(8,128)(2,1)S(1)}, bf16[256,128]{1,0:T(8,128)(2,1)S(1)}, u32[]{:S(2)}, u32[]{:S(2)}) collective-permute-start(bf16[256,128]{1,0:T(8,128)(2,1)S(1)} %get-tuple-element.29), channel_id=1, source_target_pairs={{0,9},{1,8},{2,11},{3,10},{4,13},{5,12},{6,15},{7,14},{8,1},{9,0},... | collective-permute-start | bytes 196616 | tf_op jit(solution)/shard_map/ppermute | solution.py:430
  10.9 4.1 %collective-permute-start.3 = (bf16[256,128]{1,0:T(8,128)(2,1)S(1)}, bf16[256,128]{1,0:T(8,128)(2,1)S(1)}, u32[]{:S(2)}, u32[]{:S(2)}) collective-permute-start(bf16[256,128]{1,0:T(8,128)(2,1)S(1)} %constant_dynamic-update-slice_fusion.refs_3_), channel_id=1, source_target_pairs={{0,10},{1,11},{2,8},{3,9},{4,14},{5,15},{6,12},{7,13},{8,2},{9,3},... | collective-permute-start | bytes 196616 | tf_op jit(solution)/shard_map/ppermute | solution.py:430
  11.0 1.4 %collective-permute-start.5 = (bf16[256,128]{1,0:T(8,128)(2,1)S(1)}, bf16[256,128]{1,0:T(8,128)(2,1)S(1)}, u32[]{:S(2)}, u32[]{:S(2)}) collective-permute-start(bf16[256,128]{1,0:T(8,128)(2,1)S(1)} %pass_on.2), channel_id=1, source_target_pairs={{0,8},{1,9},{2,10},{3,11},{4,12},{5,13},{6,14},{7,15},{8,0},{9,1},... | collective-permute-start | bytes 196616 | tf_op jit(solution)/shard_map/ppermute | solution.py:430
  15.6 4.3 %collective-permute-start.9 = (bf16[32,512]{1,0:T(8,128)(2,1)S(1)}, bf16[32,512]{1,0:T(8,128)(2,1)S(1)}, u32[]{:S(2)}, u32[]{:S(2)}) collective-permute-start(bf16[32,512]{1,0:T(8,128)(2,1)S(1)} %pad_maximum_fusion.1), channel_id=1, source_target_pairs={{0,1},{1,0},{2,3},{3,2},{4,5},{5,4},{6,7},{7,6},{8,9},{9,8},{10,11... | collective-permute-start | bytes 98312 | tf_op jit(solution)/shard_map/ppermute | solution.py:430
  16.9 1.6 %collective-permute-start.6 = (bf16[256,128]{1,0:T(8,128)(2,1)S(1)}, bf16[256,128]{1,0:T(8,128)(2,1)S(1)}, u32[]{:S(2)}, u32[]{:S(2)}) collective-permute-start(bf16[256,128]{1,0:T(8,128)(2,1)S(1)} %pass_on.3), channel_id=1, source_target_pairs={{0,8},{1,9},{2,10},{3,11},{4,12},{5,13},{6,14},{7,15},{8,0},{9,1},... | collective-permute-start | bytes 196616 | tf_op jit(solution)/shard_map/ppermute | solution.py:430
  17.5 3.4 %collective-permute-start.8 = (bf16[32,512]{1,0:T(8,128)(2,1)S(1)}, bf16[32,512]{1,0:T(8,128)(2,1)S(1)}, u32[]{:S(2)}, u32[]{:S(2)}) collective-permute-start(bf16[32,512]{1,0:T(8,128)(2,1)S(1)} %pad_maximum_fusion), channel_id=1, source_target_pairs={{0,9},{1,8},{2,11},{3,10},{4,13},{5,12},{6,15},{7,14},{8,1},{9,0},... | collective-permute-start | bytes 98312 | tf_op jit(solution)/shard_map/ppermute | solution.py:430
  19.0 1.9 %collective-permute-start.7 = (bf16[32,512]{1,0:T(8,128)(2,1)S(1)}, bf16[32,512]{1,0:T(8,128)(2,1)S(1)}, u32[]{:S(2)}, u32[]{:S(2)}) collective-permute-start(bf16[32,512]{1,0:T(8,128)(2,1)S(1)} %correlate_part.6), channel_id=1, source_target_pairs={{0,8},{1,9},{2,10},{3,11},{4,12},{5,13},{6,14},{7,15},{8,0},{9,1},... | collective-permute-start | bytes 98312 | tf_op jit(solution)/shard_map/ppermute | solution.py:430

commit v6 on v4

--- a/solution.py
+++ b/solution.py
@@ -15,6 +15,8 @@
 STEPS = 2
 RADIX = 16
 AXES = ("grp", "dev")
+TURN_PLANE, TURN_GATHER, TURN_LAST = 1, (1, 1), 1
+BIT_ORDER = (2, 1, 0)
 SMEM = pl.BlockSpec(memory_space=pltpu.SMEM)
 VMEM = pl.BlockSpec(memory_space=pltpu.VMEM)
 AHEAD = pl.CostEstimate(flops=5_000_000_000, bytes_accessed=1_000_000, transcendentals=0)
@@ -183,16 +185,16 @@
     out_ref[...] = relay_ref[...].astype(jnp.bfloat16)
 
 
-def holdings(member_bits):
+def turn(index):
+    return TURN_GATHER[min(index, len(TURN_GATHER) - 1)]
+
+
+def panel_order(bits):
     held = [(0, 0)]
-    for bit in member_bits[:-1]:
-        held += [(k ^ bit, 1 - odd) for k, odd in held]
-    brought = [(k ^ member_bits[-1], 1 - odd) for k, odd in held]
-    return held, brought
-
-
-def panel_order(member_bits):
-    held, brought = holdings(member_bits)
+    for index, bit in enumerate(bits):
+        brought = [(k ^ bit, odd ^ turn(index)) for k, odd in held]
+        if index < len(bits) - 1:
+            held = held + brought
     flip = lambda pieces: [(k, 1 - odd) for k, odd in pieces]
     return held + flip(held) + brought + flip(brought)
 
@@ -279,7 +281,7 @@
     out_ref[...] = samples[...].astype(out_ref.dtype)
 
 
-def receiver_kernel(radius, order, info_ref, usable_ref, raw_ref, twiddle_ref, table_ref, *rest):
+def receiver_kernel(radius, order, last_bit, info_ref, usable_ref, raw_ref, twiddle_ref, table_ref, *rest):
     spectra_ref, inverse_ref, other_ref, samples, relay = rest
     channels, windows, _ = raw_ref.shape
     members = lax.axis_size("dev")
@@ -310,7 +312,7 @@
         offset = (member ^ k) * channels + (core + odd) % SRC_DEV
         blocks.append(jnp.where(lane == start + offset, 1.0, 0.0))
     sent = flags_of(jnp.concatenate(blocks, axis=0), flags)
-    theirs = ((group ^ 1) * members + (member ^ 1)) * channels
+    theirs = ((group ^ TURN_LAST) * members + (member ^ last_bit)) * channels
     for ref, start in ((inverse_ref, first), (other_ref, theirs)):
         received = flags_of(jnp.where(lane == start + row % channels, 1.0, 0.0), flags)
         both = sent * jnp.concatenate([received] * len(order), axis=0)
@@ -397,12 +399,12 @@
     out_ref[...] = value_ref[...]
 
 
-def place_kernel(order, *refs):
+def place_kernel(order, last_bit, *refs):
     out_ref = refs[-1]
     member = lax.axis_index("dev")
     core = lax.axis_index("grp") % SRC_DEV
     receivers = out_ref.shape[2]
-    whole = order + [(k ^ 1, 1 - odd) for k, odd in order]
+    whole = order + [(k ^ last_bit, odd ^ TURN_LAST) for k, odd in order]
     block = STEPS * receivers
     done = 0
     for ref in refs[:-1]:
@@ -431,12 +433,10 @@
         return lax.ppermute(value, AXES, pairs)
 
     ltable = jnp.asarray(lag_table(length, bin_count, NLAG))
-    member_bits = []
-    bit = members // 2
-    while bit:
-        member_bits.append(bit)
-        bit //= 2
-    order = panel_order(member_bits[:-1])
+    all_bits = [1 << i for i in range(members.bit_length() - 1)]
+    chosen = [all_bits[i] for i in BIT_ORDER]
+    *gather_bits, last_bit = [b for b in all_bits[::-1] if b not in chosen] + chosen
+    order = panel_order(gather_bits)
 
     usable_rows = usable.T
     planes = groups // SRC_DEV
@@ -478,9 +478,9 @@
             name="pick_rows",
         )(choice, records, records_other)
 
-    sent = pick(1)
-    came = exchange(sent, SRC_DEV * (planes // 2) + 1, 0)
-    kept = pick(0)
+    sent = pick(TURN_PLANE)
+    came = exchange(sent, SRC_DEV * (planes // 2) + TURN_PLANE, 0)
+    kept = pick(0) if TURN_PLANE else sent
     for index in range(plane_bits - 2, -1, -1):
         kept = jnp.where(take[index + 1][:, :1] > 0.0, came, kept)
         came = exchange(kept, SRC_DEV << index, 0)
@@ -502,7 +502,7 @@
     row_count = channels * windows
     pairs = len(order) * STEPS * channels
     receivers, inverse, inverse_theirs = pl.pallas_call(
-        functools.partial(receiver_kernel, radius, order),
+        functools.partial(receiver_kernel, radius, order, last_bit),
         out_shape=[
             jax.ShapeDtypeStruct((2 * row_count * blocks, width), jnp.bfloat16),
             jax.ShapeDtypeStruct((pairs, width), jnp.float32),
@@ -533,9 +533,9 @@
     )(take[0], mask, kept, came, twiddle, table, receivers)
 
     held = piece
-    for bit in member_bits[:-2]:
-        held = jnp.concatenate([held, exchange(held, 1, bit)], axis=0)
-    theirs = exchange(passed, 1, 1)
+    for index, bit in enumerate(gather_bits[:-1]):
+        held = jnp.concatenate([held, exchange(held, turn(index), bit)], axis=0)
+    theirs = exchange(passed, TURN_LAST, last_bit)
 
     def pass_on(value, after):
         return pl.pallas_call(
@@ -565,19 +565,18 @@
         )(ltable, *[array for pair in sets for array in pair], *buffers)
 
     mine, other = (receivers, inverse), (theirs, inverse_theirs)
-    brought = exchange(held, 1, member_bits[-2])
+    brought = exchange(held, turn(len(gather_bits) - 1), gather_bits[-1])
     held_other = exchange(pass_on(held, theirs), 1, 0)
     early_theirs, early = part(0, [other, mine], held)
-    (next_theirs,) = part(pairs // 4, [other], held_other)
-    brought = pass_on(brought, next_theirs)
+    brought = pass_on(brought, early_theirs)
     brought_other = exchange(brought, 1, 0)
-    (middle_theirs,) = part(pairs // 2, [other], brought)
+    (middle_theirs,) = part(pairs // 4, [other], held_other, brought)
     (late_theirs,) = part(pairs // 4 * 3, [other], brought_other)
     (late,) = part(pairs // 4, [mine], held_other, brought, brought_other)
-    lag_rows = [early_theirs, next_theirs, middle_theirs, late_theirs]
-    back = exchange(jnp.concatenate(lag_rows, axis=0), 1, 1)
+    lag_rows = [early_theirs, middle_theirs, late_theirs]
+    back = exchange(jnp.concatenate(lag_rows, axis=0), TURN_LAST, last_bit)
     return pl.pallas_call(
-        functools.partial(place_kernel, order),
+        functools.partial(place_kernel, order, last_bit),
         out_shape=jax.ShapeDtypeStruct(
             (STEPS, members * SRC_DEV, channels, NLAG), jnp.bfloat16
         ),

time: 21.7 us -> 21.7 us (level)
  Pallas kernels: 5.27 us -> 4.95 us
  waiting for transfers between devices: 9.88 us -> 10.2 us
    ppermute x8, waiting for transfers between devices: 9.88 us -> 10.2 us  [exchange(): return lax.ppermute(value, AXES, pairs)]
    pallas_call x5 -> x4, Pallas kernels: 2.34 us -> 2.02 us  [part(): pl.pallas_call(functools.partial(part_kernel, windows, first, len(sets)),...]
  transfers between devices with their start and end apart: 8 -> 8, of which waited for: 7 -> 6; matrix products, arithmetic and copies ran while one was open for 0% -> 0% of each run, Pallas kernels for 17% -> 16%
where the time goes in v6:
time: 21.7 us; the launch traced here: 21.5 us
  waiting for transfers between devices  10.2 us (47%)
  starting transfers between devices  6.28 us (29%)
  Pallas kernels  4.95 us (23%)
    ppermute x8, waiting for transfers between devices, exchange(): return lax.ppermute(value, AXES, pairs)  10.2 us
    ppermute x8, starting transfers between devices, exchange(): return lax.ppermute(value, AXES, pairs)  6.28 us
    pallas_call x4, Pallas kernels, part(): pl.pallas_call(functools.partial(part_kernel, windows, first, len(sets)),...  2.02 us
    pallas_call x1, Pallas kernels, on_device(): pl.pallas_call(functools.partial(choice_kernel, halves, channels), out_sh...  0.77 us
    pallas_call x1, Pallas kernels, on_device(): pl.pallas_call(functools.partial(place_kernel, order, last_bit), out_shap...  0.69 us
    pallas_call x1, Pallas kernels, on_device(): pl.pallas_call(functools.partial(receiver_kernel, radius, order, last_bit...  0.57 us
  transfers between devices with their start and end apart: 8, of which 6 were waited for; matrix products, arithmetic and copies ran while one was open for 0% of the time, Pallas kernels for 16%

profile of v6, /device:TPU:25, one launch (start us, length us, event | category | flops | bytes accessed | tf_op | source)
XLA Modules:
  0.0 21.5 jit_solution(7743189403545520720)
XLA Ops:
  0.0 0.0 copy-start
  0.0 0.7 %collective-permute-start = (bf16[4,4,2048]{2,1,0:T(4,128)(2,1)}, bf16[4,4,2048]{2,1,0:T(4,128)(2,1)S(1)}, u32[]{:S(2)}, u32[]{:S(2)}) collective-permute-start(bf16[4,4,2048]{2,1,0:T(4,128)(2,1)} %raw_ref.1), channel_id=1, source_target_pairs={{0,8},{1,9},{2,10},{3,11},{4,12},{5,13},{6,14},{7,15},{8,0},{9,1},... | collective-permute-start | bytes 196616 | tf_op jit(solution)/shard_map/ppermute | solution.py:433
  0.8 0.0 copy-done.2
  0.8 0.0 copy-done.1
  0.8 0.8 %choose_rows.1 = (f32[8,128]{1,0:T(8,128)S(1)}, f32[8,128]{1,0:T(8,128)S(1)}, f32[1,8,128]{2,1,0:T(8,128)S(1)}, s32[8,128]{1,0:T(8,128)S(1)}) custom-call(s32[2]{0:T(128)S(1)} %copy-done.2, s32[4,128]{1,0:T(4,128)S(1)} %bitcast.3, f32[8,128]{1,0:T(8,128)S(1)} %ahead.1.after_ref), custom_call_target="tpu_custom_call" | custom-call | tf_op jit(solution)/shard_map/choose_rows/pallas_call | solution.py:456
  1.5 0.3 %collective-permute-done.other_ref = bf16[4,4,2048]{2,1,0:T(4,128)(2,1)S(1)} collective-permute-done((bf16[4,4,2048]{2,1,0:T(4,128)(2,1)}, bf16[4,4,2048]{2,1,0:T(4,128)(2,1)S(1)}, u32[]{:S(2)}, u32[]{:S(2)}) %collective-permute-start) | collective-permute-done | bytes 65568 | tf_op jit(solution)/shard_map/ppermute | solution.py:433
  1.9 0.0 copy-done
  1.9 1.5 %collective-permute-start.1 = (bf16[8,2048]{1,0:T(8,128)(2,1)S(1)}, bf16[8,2048]{1,0:T(8,128)(2,1)S(1)}, u32[]{:S(2)}, u32[]{:S(2)}) collective-permute-start(bf16[8,2048]{1,0:T(8,128)(2,1)S(1)} %pick_rows.3.after_ref), channel_id=1, source_target_pairs={{0,24},{1,25},{2,26},{3,27},{4,28},{5,29},{6,30},{7,31},{8,16},{9,... | collective-permute-start | bytes 98312 | tf_op jit(solution)/shard_map/ppermute | solution.py:433
  3.4 0.4 %short_tables.1 = (bf16[2,512,256]{2,1,0:T(8,128)(2,1)S(1)}, f32[2,16,128]{2,1,0:T(8,128)S(1)}) custom-call(bf16[8,2048]{1,0:T(8,128)(2,1)S(1)} %pick_rows.3.after_ref), custom_call_target="tpu_custom_call" | custom-call | flops 5000000000 | bytes 1000000 | tf_op jit(solution)/shard_map/short_tables/pallas_call | solution.py:489
  3.8 0.0 copy-start.3
  3.8 0.6 %receiver_spectra.1 = (bf16[256,128]{1,0:T(8,128)(2,1)S(1)}, f32[64,128]{1,0:T(8,128)S(1)}, f32[64,128]{1,0:T(8,128)S(1)}) custom-call(s32[8,128]{1,0:T(8,128)S(1)} %get-tuple-element.23.info_ref, s32[4,128]{1,0:T(4,128)S(1)} %bitcast.4, bf16[4,4,2048]{2,1,0:T(4,128)(2,1)S(1)} %copy-done, f32[2,16,128]{2,1,0:T(8,128)S(1)} %get-tuple-element.21.twiddle_ref.refs_4_, ...), custom_call_target="tpu_custom_call" | custom-call | flops 5000000000 | bytes 1000000 | tf_op jit(solution)/shard_map/receiver_spectra/pallas_call | solution.py:504
  4.4 0.1 pick_rows.2.refs_2_
  4.5 0.9 %collective-permute-done.1.refs_3_ = bf16[8,2048]{1,0:T(8,128)(2,1)S(1)} collective-permute-done((bf16[8,2048]{1,0:T(8,128)(2,1)S(1)}, bf16[8,2048]{1,0:T(8,128)(2,1)S(1)}, u32[]{:S(2)}, u32[]{:S(2)}) %collective-permute-start.1) | collective-permute-done | bytes 32800 | tf_op jit(solution)/shard_map/ppermute | solution.py:433
  5.3 0.4 %source_spectra.1 = (bf16[128,128]{1,0:T(8,128)(2,1)S(1)}, bf16[256,128]{1,0:T(8,128)(2,1)S(1)}) custom-call(f32[8,128]{1,0:T(8,128)S(1)} %bitcast.2, f32[8,128]{1,0:T(8,128)S(1)} %get-tuple-element.19.refs_1_, bf16[8,2048]{1,0:T(8,128)(2,1)S(1)} %pick_rows.2.refs_2_, bf16[8,2048]{1,0:T(8,128)(2,1)S(1)} %collective-permute-done.1.refs_3_, ...), custom_call_target="tpu_custom_call" | custom-call | tf_op jit(solution)/shard_map/source_spectra/pallas_call | solution.py:522
  5.7 0.4 %collective-permute-start.3 = (bf16[128,128]{1,0:T(8,128)(2,1)S(1)}, bf16[128,128]{1,0:T(8,128)(2,1)S(1)}, u32[]{:S(2)}, u32[]{:S(2)}) collective-permute-start(bf16[128,128]{1,0:T(8,128)(2,1)S(1)} %get-tuple-element.28), channel_id=1, source_target_pairs={{0,12},{1,13},{2,14},{3,15},{4,8},{5,9},{6,10},{7,11},{8,4},{9,5},... | collective-permute-start | bytes 98312 | tf_op jit(solution)/shard_map/ppermute | solution.py:433
  6.1 1.3 %collective-permute-start.2 = (bf16[256,128]{1,0:T(8,128)(2,1)S(1)}, bf16[256,128]{1,0:T(8,128)(2,1)S(1)}, u32[]{:S(2)}, u32[]{:S(2)}) collective-permute-start(bf16[256,128]{1,0:T(8,128)(2,1)S(1)} %get-tuple-element.25), channel_id=1, source_target_pairs={{0,9},{1,8},{2,11},{3,10},{4,13},{5,12},{6,15},{7,14},{8,1},{9,0},... | collective-permute-start | bytes 196616 | tf_op jit(solution)/shard_map/ppermute | solution.py:433
  7.4 3.5 %collective-permute-done.3 = bf16[128,128]{1,0:T(8,128)(2,1)S(1)} collective-permute-done((bf16[128,128]{1,0:T(8,128)(2,1)S(1)}, bf16[128,128]{1,0:T(8,128)(2,1)S(1)}, u32[]{:S(2)}, u32[]{:S(2)}) %collective-permute-start.3) | collective-permute-done | bytes 32800 | tf_op jit(solution)/shard_map/ppermute | solution.py:433
  10.9 0.0 collective-permute-start.5
  10.9 0.0 collective-permute-done.2.refs_1_.after_ref
  10.9 0.5 %collective-permute-start.4 = (bf16[256,128]{1,0:T(8,128)(2,1)S(1)}, bf16[256,128]{1,0:T(8,128)(2,1)S(1)}, u32[]{:S(2)}, u32[]{:S(2)}) collective-permute-start(bf16[256,128]{1,0:T(8,128)(2,1)S(1)} %pass_on.2), channel_id=1, source_target_pairs={{0,8},{1,9},{2,10},{3,11},{4,12},{5,13},{6,14},{7,15},{8,0},{9,1},... | collective-permute-start | bytes 196616 | tf_op jit(solution)/shard_map/ppermute | solution.py:433
  11.4 0.0 copy-done.3
  11.4 0.5 %correlate_part.4 = (bf16[16,512]{1,0:T(8,128)(2,1)S(1)}, bf16[16,512]{1,0:T(8,128)(2,1)S(1)}) custom-call(bf16[2048,512]{1,0:T(8,128)(2,1)S(1)} %copy-done.3, bf16[256,128]{1,0:T(8,128)(2,1)S(1)} %collective-permute-done.2.refs_1_.after_ref, f32[64,128]{1,0:T(8,128)S(1)} %get-tuple-element.26.refs_2_, ...), custom_call_target="tpu_custom_call" | custom-call | flops 1000000000 | bytes 1000000 | tf_op jit(solution)/shard_map/correlate_part/pallas_call | solution.py:553
  11.9 3.1 %collective-permute-done.5.value_ref = bf16[256,128]{1,0:T(8,128)(2,1)S(1)} collective-permute-done((bf16[256,128]{1,0:T(8,128)(2,1)S(1)}, bf16[256,128]{1,0:T(8,128)(2,1)S(1)}, u32[]{:S(2)}, u32[]{:S(2)}) %collective-permute-start.5) | collective-permute-done | bytes 65568 | tf_op jit(solution)/shard_map/ppermute | solution.py:433
  15.0 0.4 %collective-permute-start.6 = (bf16[256,128]{1,0:T(8,128)(2,1)S(1)}, bf16[256,128]{1,0:T(8,128)(2,1)S(1)}, u32[]{:S(2)}, u32[]{:S(2)}) collective-permute-start(bf16[256,128]{1,0:T(8,128)(2,1)S(1)} %pass_on.3.refs_4_), channel_id=1, source_target_pairs={{0,8},{1,9},{2,10},{3,11},{4,12},{5,13},{6,14},{7,15},{8,0},{9,1},... | collective-permute-start | bytes 196616 | tf_op jit(solution)/shard_map/ppermute | solution.py:433
  15.4 0.0 collective-permute-done.4.refs_3_
  15.4 0.5 %correlate_part.6 = bf16[32,512]{1,0:T(8,128)(2,1)S(1)} custom-call(bf16[2048,512]{1,0:T(8,128)(2,1)S(1)} %copy-done.3, bf16[256,128]{1,0:T(8,128)(2,1)S(1)} %collective-permute-done.2.refs_1_.after_ref, f32[64,128]{1,0:T(8,128)S(1)} %get-tuple-element.26.refs_2_, bf16[256,128]{1,0:T(8,128)(2,1)S(1)} %collective-permute-done.4.refs_3_, ...), custom_call_target="tpu_custom_call" | custom-call | flops 1000000000 | bytes 1000000 | tf_op jit(solution)/shard_map/correlate_part/pallas_call | solution.py:553
  15.9 0.4 %collective-permute-done.6.refs_5_.refs_3_ = bf16[256,128]{1,0:T(8,128)(2,1)S(1)} collective-permute-done((bf16[256,128]{1,0:T(8,128)(2,1)S(1)}, bf16[256,128]{1,0:T(8,128)(2,1)S(1)}, u32[]{:S(2)}, u32[]{:S(2)}) %collective-permute-start.6) | collective-permute-done | bytes 65568 | tf_op jit(solution)/shard_map/ppermute | solution.py:433
  16.3 0.4 %correlate_part.7 = bf16[16,512]{1,0:T(8,128)(2,1)S(1)} custom-call(bf16[2048,512]{1,0:T(8,128)(2,1)S(1)} %copy-done.3, bf16[256,128]{1,0:T(8,128)(2,1)S(1)} %collective-permute-done.2.refs_1_.after_ref, f32[64,128]{1,0:T(8,128)S(1)} %get-tuple-element.26.refs_2_, bf16[256,128]{1,0:T(8,128)(2,1)S(1)} %collective-permute-done.6.refs_5_.refs_3_), custom_call_target="tpu_custom_call" | custom-call | flops 1000000000 | bytes 1000000 | tf_op jit(solution)/shard_map/correlate_part/pallas_call | solution.py:553
  16.7 1.5 %collective-permute-start.7 = (bf16[64,512]{1,0:T(8,128)(2,1)S(1)}, bf16[64,512]{1,0:T(8,128)(2,1)S(1)}, u32[]{:S(2)}, u32[]{:S(2)}) collective-permute-start(bf16[64,512]{1,0:T(8,128)(2,1)S(1)} %pad_maximum_fusion), channel_id=1, source_target_pairs={{0,9},{1,8},{2,11},{3,10},{4,13},{5,12},{6,15},{7,14},{8,1},{9,0},... | collective-permute-start | bytes 196616 | tf_op jit(solution)/shard_map/ppermute | solution.py:433
  18.3 0.6 %correlate_part.5.refs_1_ = bf16[48,512]{1,0:T(8,128)(2,1)S(1)} custom-call(bf16[2048,512]{1,0:T(8,128)(2,1)S(1)} %copy-done.3, bf16[256,128]{1,0:T(8,128)(2,1)S(1)} %get-tuple-element.24.refs_6_.refs_3_.refs_1_, f32[64,128]{1,0:T(8,128)S(1)} %get-tuple-element.27.refs_4_.refs_2_, bf16[256,128]{1,0:T(8,128)(2,1)S(1)} %collective-permute-done.4.refs_3_, ...), custom_call_target="tpu_custom_call" | custom-call | flops 1000000000 | bytes 1000000 | tf_op jit(solution)/shard_map/correlate_part/pallas_call | solution.py:553
  18.9 2.0 %collective-permute-done.7.refs_2_ = bf16[64,512]{1,0:T(8,128)(2,1)S(1)} collective-permute-done((bf16[64,512]{1,0:T(8,128)(2,1)S(1)}, bf16[64,512]{1,0:T(8,128)(2,1)S(1)}, u32[]{:S(2)}, u32[]{:S(2)}) %collective-permute-start.7) | collective-permute-done | bytes 65568 | tf_op jit(solution)/shard_map/ppermute | solution.py:433
  20.9 0.7 %place_rows.1 = bf16[2,16,4,512]{3,2,1,0:T(4,128)(2,1)} custom-call(bf16[16,512]{1,0:T(8,128)(2,1)S(1)} %get-tuple-element.29.refs_0_, bf16[48,512]{1,0:T(8,128)(2,1)S(1)} %correlate_part.5.refs_1_, bf16[64,512]{1,0:T(8,128)(2,1)S(1)} %collective-permute-done.7.refs_2_), custom_call_target="tpu_custom_call" | custom-call | tf_op jit(solution)/shard_map/place_rows/pallas_call | solution.py:578
  (9 shorter events, 0.1 us)
Async XLA Ops:
  0.0 1.9 %copy-start = (bf16[4,4,2048]{2,1,0:T(4,128)(2,1)S(1)}, bf16[4,4,2048]{2,1,0:T(4,128)(2,1)}, u32[]{:S(2)}) copy-start(bf16[4,4,2048]{2,1,0:T(4,128)(2,1)} %raw_ref.1) | copy-start | bytes 196612
  0.0 0.8 %copy-start.2 = (s32[2]{0:T(128)S(1)}, s32[2]{0:T(128)}, u32[]{:S(2)}) copy-start(s32[2]{0:T(128)} %ids_ref.1) | copy-start | bytes 28
  0.0 0.8 %copy-start.1 = (s32[128,4]{0,1:T(4,128)S(1)}, s32[128,4]{0,1:T(4,128)}, u32[]{:S(2)}) copy-start(s32[128,4]{0,1:T(4,128)} %param.5) | copy-start | bytes 6148
  0.0 1.9 %collective-permute-start = (bf16[4,4,2048]{2,1,0:T(4,128)(2,1)}, bf16[4,4,2048]{2,1,0:T(4,128)(2,1)S(1)}, u32[]{:S(2)}, u32[]{:S(2)}) collective-permute-start(bf16[4,4,2048]{2,1,0:T(4,128)(2,1)} %raw_ref.1), channel_id=1, source_target_pairs={{0,8},{1,9},{2,10},{3,11},{4,12},{5,13},{6,14},{7,15},{8,0},{9,1},... | collective-permute-start | bytes 196616 | tf_op jit(solution)/shard_map/ppermute | solution.py:433
  1.9 3.4 %collective-permute-start.1 = (bf16[8,2048]{1,0:T(8,128)(2,1)S(1)}, bf16[8,2048]{1,0:T(8,128)(2,1)S(1)}, u32[]{:S(2)}, u32[]{:S(2)}) collective-permute-start(bf16[8,2048]{1,0:T(8,128)(2,1)S(1)} %pick_rows.3.after_ref), channel_id=1, source_target_pairs={{0,24},{1,25},{2,26},{3,27},{4,28},{5,29},{6,30},{7,31},{8,16},{9,... | collective-permute-start | bytes 98312 | tf_op jit(solution)/shard_map/ppermute | solution.py:433
  3.8 7.6 %copy-start.3 = (bf16[2048,512]{1,0:T(8,128)(2,1)S(1)}, bf16[2048,512]{1,0:T(8,128)(2,1)}, u32[]{:S(2)}) copy-start(bf16[2048,512]{1,0:T(8,128)(2,1)} %constant.2.clone.refs_0_) | copy-start | bytes 6291460
  5.7 5.2 %collective-permute-start.3 = (bf16[128,128]{1,0:T(8,128)(2,1)S(1)}, bf16[128,128]{1,0:T(8,128)(2,1)S(1)}, u32[]{:S(2)}, u32[]{:S(2)}) collective-permute-start(bf16[128,128]{1,0:T(8,128)(2,1)S(1)} %get-tuple-element.28), channel_id=1, source_target_pairs={{0,12},{1,13},{2,14},{3,15},{4,8},{5,9},{6,10},{7,11},{8,4},{9,5},... | collective-permute-start | bytes 98312 | tf_op jit(solution)/shard_map/ppermute | solution.py:433
  6.1 4.8 %collective-permute-start.2 = (bf16[256,128]{1,0:T(8,128)(2,1)S(1)}, bf16[256,128]{1,0:T(8,128)(2,1)S(1)}, u32[]{:S(2)}, u32[]{:S(2)}) collective-permute-start(bf16[256,128]{1,0:T(8,128)(2,1)S(1)} %get-tuple-element.25), channel_id=1, source_target_pairs={{0,9},{1,8},{2,11},{3,10},{4,13},{5,12},{6,15},{7,14},{8,1},{9,0},... | collective-permute-start | bytes 196616 | tf_op jit(solution)/shard_map/ppermute | solution.py:433
  10.9 4.1 %collective-permute-start.5 = (bf16[256,128]{1,0:T(8,128)(2,1)S(1)}, bf16[256,128]{1,0:T(8,128)(2,1)S(1)}, u32[]{:S(2)}, u32[]{:S(2)}) collective-permute-start(bf16[256,128]{1,0:T(8,128)(2,1)S(1)} %constant_dynamic-update-slice_fusion.refs_5_.value_ref), channel_id=1, source_target_pairs={{0,10},{1,11},{2,8},{3,9},{4,14},{5,15},{6,12},{7,13},{8,2},{9,3},... | collective-permute-start | bytes 196616 | tf_op jit(solution)/shard_map/ppermute | solution.py:433
  10.9 4.5 %collective-permute-start.4 = (bf16[256,128]{1,0:T(8,128)(2,1)S(1)}, bf16[256,128]{1,0:T(8,128)(2,1)S(1)}, u32[]{:S(2)}, u32[]{:S(2)}) collective-permute-start(bf16[256,128]{1,0:T(8,128)(2,1)S(1)} %pass_on.2), channel_id=1, source_target_pairs={{0,8},{1,9},{2,10},{3,11},{4,12},{5,13},{6,14},{7,15},{8,0},{9,1},... | collective-permute-start | bytes 196616 | tf_op jit(solution)/shard_map/ppermute | solution.py:433
  15.0 1.3 %collective-permute-start.6 = (bf16[256,128]{1,0:T(8,128)(2,1)S(1)}, bf16[256,128]{1,0:T(8,128)(2,1)S(1)}, u32[]{:S(2)}, u32[]{:S(2)}) collective-permute-start(bf16[256,128]{1,0:T(8,128)(2,1)S(1)} %pass_on.3.refs_4_), channel_id=1, source_target_pairs={{0,8},{1,9},{2,10},{3,11},{4,12},{5,13},{6,14},{7,15},{8,0},{9,1},... | collective-permute-start | bytes 196616 | tf_op jit(solution)/shard_map/ppermute | solution.py:433
  16.7 4.1 %collective-permute-start.7 = (bf16[64,512]{1,0:T(8,128)(2,1)S(1)}, bf16[64,512]{1,0:T(8,128)(2,1)S(1)}, u32[]{:S(2)}, u32[]{:S(2)}) collective-permute-start(bf16[64,512]{1,0:T(8,128)(2,1)S(1)} %pad_maximum_fusion), channel_id=1, source_target_pairs={{0,9},{1,8},{2,11},{3,10},{4,13},{5,12},{6,15},{7,14},{8,1},{9,0},... | collective-permute-start | bytes 196616 | tf_op jit(solution)/shard_map/ppermute | solution.py:433

commit v7 on v6

--- a/solution.py
+++ b/solution.py
@@ -33,8 +33,7 @@
     return np.concatenate(order)
 
 
-def tables_kernel(length, after_ref, table_ref, twiddle_ref):
-    del after_ref
+def tables_kernel(length, table_ref, twiddle_ref):
     points = length // RADIX
     per = points // 2
     row = lax.broadcasted_iota(jnp.int32, (points, points), 0)
@@ -191,12 +190,14 @@
 
 def panel_order(bits):
     held = [(0, 0)]
-    for index, bit in enumerate(bits):
-        brought = [(k ^ bit, odd ^ turn(index)) for k, odd in held]
-        if index < len(bits) - 1:
-            held = held + brought
-    flip = lambda pieces: [(k, 1 - odd) for k, odd in pieces]
-    return held + flip(held) + brought + flip(brought)
+    for index, bit in enumerate(bits[:-1]):
+        first = len(held)
+        held = held + [(k ^ bit, odd ^ turn(index)) for k, odd in held]
+    last = [(k ^ bits[-1], odd ^ turn(len(bits) - 1)) for k, odd in held]
+    order = []
+    for pieces in (held, last[:first], last[first:]):
+        order += pieces + [(k, 1 - odd) for k, odd in pieces]
+    return order
 
 
 def flags_of(picks, flags):
@@ -213,10 +214,6 @@
     column = lax.broadcasted_iota(jnp.int32, rows_flags.shape, 1)
     kept = jnp.where(row % rows_flags.shape[1] == column, rows_flags, 0.0)
     return jnp.sum(kept, axis=1, keepdims=True)
-
-
-def first_kernel(out_ref):
-    out_ref[...] = jnp.zeros_like(out_ref)
 
 
 def choice_kernel(halves, channels, ids_ref, usable_ref, after_ref, *outs):
@@ -321,9 +318,8 @@
 
 
 def source_kernel(radius, *refs):
-    take_ref, mask_ref, kept_ref, came_ref, twiddle_ref, table_ref, spectra_ref = refs[:7]
-    out_ref, passed_ref, relay = refs[7:]
-    passed_ref[...] = spectra_ref[...]
+    take_ref, mask_ref, kept_ref, came_ref, twiddle_ref, table_ref = refs[:6]
+    out_ref, relay = refs[-2:]
     rows, length = kept_ref.shape
     points = length // RADIX
     here = take_ref[...] > 0.0
@@ -444,15 +440,20 @@
     plane_bits = planes.bit_length() - 1
 
     records_other = exchange(records, 1, 0)
-    ahead = pl.pallas_call(
-        first_kernel,
-        out_shape=jax.ShapeDtypeStruct((8, width), jnp.float32),
+    points = length // RADIX
+    table, twiddle = pl.pallas_call(
+        functools.partial(tables_kernel, length),
+        out_shape=[
+            jax.ShapeDtypeStruct((2, 4 * points, 2 * points), jnp.bfloat16),
+            jax.ShapeDtypeStruct((2, RADIX, points), jnp.float32),
+        ],
         in_specs=[],
-        out_specs=VMEM,
+        out_specs=[VMEM] * 2,
         compiler_params=PARAMS,
         cost_estimate=AHEAD,
-        name="ahead",
+        name="short_tables",
     )()
+
     choice, mask, take, info = pl.pallas_call(
         functools.partial(choice_kernel, halves, channels),
         out_shape=[
@@ -465,7 +466,7 @@
         out_specs=[VMEM] * 4,
         compiler_params=PARAMS,
         name="choose_rows",
-    )(panel_ids, usable_rows, ahead)
+    )(panel_ids, usable_rows, twiddle)
 
     def pick(flip):
         return pl.pallas_call(
@@ -484,20 +485,6 @@
     for index in range(plane_bits - 2, -1, -1):
         kept = jnp.where(take[index + 1][:, :1] > 0.0, came, kept)
         came = exchange(kept, SRC_DEV << index, 0)
-
-    points = length // RADIX
-    table, twiddle = pl.pallas_call(
-        functools.partial(tables_kernel, length),
-        out_shape=[
-            jax.ShapeDtypeStruct((2, 4 * points, 2 * points), jnp.bfloat16),
-            jax.ShapeDtypeStruct((2, RADIX, points), jnp.float32),
-        ],
-        in_specs=[VMEM],
-        out_specs=[VMEM] * 2,
-        compiler_params=PARAMS,
-        cost_estimate=AHEAD,
-        name="short_tables",
-    )(sent)
 
     row_count = channels * windows
     pairs = len(order) * STEPS * channels
@@ -519,35 +506,17 @@
         name="receiver_spectra",
     )(info, usable_rows, records, twiddle, table)
 
-    piece, passed = pl.pallas_call(
+    piece = pl.pallas_call(
         functools.partial(source_kernel, radius),
-        out_shape=[
-            jax.ShapeDtypeStruct((2 * source_rows * blocks, width), jnp.bfloat16),
-            jax.ShapeDtypeStruct(receivers.shape, receivers.dtype),
-        ],
+        out_shape=jax.ShapeDtypeStruct((2 * source_rows * blocks, width), jnp.bfloat16),
         in_specs=[VMEM] * 7,
-        out_specs=[VMEM] * 2,
+        out_specs=VMEM,
         scratch_shapes=[pltpu.VMEM((2 * source_rows * blocks, width), jnp.float32)],
         compiler_params=PARAMS,
         name="source_spectra",
     )(take[0], mask, kept, came, twiddle, table, receivers)
 
-    held = piece
-    for index, bit in enumerate(gather_bits[:-1]):
-        held = jnp.concatenate([held, exchange(held, turn(index), bit)], axis=0)
-    theirs = exchange(passed, TURN_LAST, last_bit)
-
-    def pass_on(value, after):
-        return pl.pallas_call(
-            pass_kernel,
-            out_shape=jax.ShapeDtypeStruct(value.shape, value.dtype),
-            in_specs=[VMEM] * 2,
-            out_specs=VMEM,
-            compiler_params=PARAMS,
-            name="pass_on",
-        )(value, after)
-
-    def part(first, sets, *buffers):
+    def part(first, sets, *buffers, cost=BESIDE):
         rows = sum(b.shape[0] for b in buffers) // (2 * windows * blocks) * channels
         total = rows * len(sets)
         return pl.pallas_call(
@@ -560,21 +529,37 @@
                 pltpu.VMEM((total, 2 * bin_count), jnp.bfloat16),
             ],
             compiler_params=PARAMS,
-            cost_estimate=BESIDE,
+            cost_estimate=cost,
             name="correlate_part",
         )(ltable, *[array for pair in sets for array in pair], *buffers)
 
+    def pass_on(value, after):
+        return pl.pallas_call(
+            pass_kernel,
+            out_shape=jax.ShapeDtypeStruct(value.shape, value.dtype),
+            in_specs=[VMEM] * 2,
+            out_specs=VMEM,
+            compiler_params=PARAMS,
+            name="pass_on",
+        )(value, after)
+
+    held = piece
+    for index, bit in enumerate(gather_bits[:-2]):
+        held = jnp.concatenate([held, exchange(held, turn(index), bit)], axis=0)
+    rounds = len(gather_bits)
+    theirs = exchange(receivers, TURN_LAST, last_bit)
+    fresh = pass_on(exchange(held, turn(rounds - 2), gather_bits[-2]), theirs)
+    first = exchange(held, turn(rounds - 1), gather_bits[-1])
+    second = exchange(fresh, turn(rounds - 1), gather_bits[-1])
+    held = jnp.concatenate([held, fresh], axis=0)
+    pieces = [held, exchange(held, 1, 0), first, exchange(first, 1, 0)]
+    pieces += [second, exchange(second, 1, 0)]
     mine, other = (receivers, inverse), (theirs, inverse_theirs)
-    brought = exchange(held, turn(len(gather_bits) - 1), gather_bits[-1])
-    held_other = exchange(pass_on(held, theirs), 1, 0)
     early_theirs, early = part(0, [other, mine], held)
-    brought = pass_on(brought, early_theirs)
-    brought_other = exchange(brought, 1, 0)
-    (middle_theirs,) = part(pairs // 4, [other], held_other, brought)
-    (late_theirs,) = part(pairs // 4 * 3, [other], brought_other)
-    (late,) = part(pairs // 4, [mine], held_other, brought, brought_other)
-    lag_rows = [early_theirs, middle_theirs, late_theirs]
-    back = exchange(jnp.concatenate(lag_rows, axis=0), TURN_LAST, last_bit)
+    (next_theirs,) = part(pairs // 4, [other], *pieces[1:4])
+    (late_theirs,) = part(pairs // 4 * 3, [other], *pieces[4:])
+    (late,) = part(pairs // 4, [mine], *pieces[1:])
+    back = exchange(jnp.concatenate([early_theirs, next_theirs, late_theirs], axis=0), TURN_LAST, last_bit)
     return pl.pallas_call(
         functools.partial(place_kernel, order, last_bit),
         out_shape=jax.ShapeDtypeStruct(

time: 21.7 us -> 21.3 us (0.982); the launches traced: 21.5 us -> 20.9 us
  waiting for transfers between devices: 10.2 us -> 9.23 us
  starting transfers between devices: 6.28 us -> 6.64 us
    ppermute x8 -> x10, waiting for transfers between devices: 10.2 us -> 9.23 us  [exchange(): return lax.ppermute(value, AXES, pairs)]
    ppermute x8 -> x10, starting transfers between devices: 6.28 us -> 6.64 us  [exchange(): return lax.ppermute(value, AXES, pairs)]
  transfers between devices with their start and end apart: 8 -> 10, of which waited for: 6 -> 5; matrix products, arithmetic and copies ran while one was open for 0% -> 0% of each run, Pallas kernels for 16% -> 18%
where the time goes in v7:
time: 21.3 us; the launch traced here: 20.9 us
  waiting for transfers between devices  9.23 us (43%)
  starting transfers between devices  6.64 us (31%)
  Pallas kernels  4.93 us (23%)
    ppermute x10, waiting for transfers between devices, exchange(): return lax.ppermute(value, AXES, pairs)  9.23 us
    ppermute x10, starting transfers between devices, exchange(): return lax.ppermute(value, AXES, pairs)  6.64 us
    pallas_call x4, Pallas kernels, part(): pl.pallas_call(functools.partial(part_kernel, windows, first, len(sets)),...  2.02 us
    pallas_call x1, Pallas kernels, on_device(): pl.pallas_call(functools.partial(choice_kernel, halves, channels), out_sh...  0.77 us
    pallas_call x1, Pallas kernels, on_device(): pl.pallas_call(functools.partial(place_kernel, order, last_bit), out_shap...  0.69 us
    pallas_call x1, Pallas kernels, on_device(): pl.pallas_call(functools.partial(receiver_kernel, radius, order, last_bit...  0.56 us
  transfers between devices with their start and end apart: 10, of which 5 were waited for; matrix products, arithmetic and copies ran while one was open for 0% of the time, Pallas kernels for 18%

profile of v7, /device:TPU:25, one launch (start us, length us, event | category | flops | bytes accessed | tf_op | source)
XLA Modules:
  0.0 20.9 jit_solution(9305569206111659629)
XLA Ops:
  0.0 0.7 %collective-permute-start.1 = (bf16[4,4,2048]{2,1,0:T(4,128)(2,1)}, bf16[4,4,2048]{2,1,0:T(4,128)(2,1)S(1)}, u32[]{:S(2)}, u32[]{:S(2)}) collective-permute-start(bf16[4,4,2048]{2,1,0:T(4,128)(2,1)} %own_ref.3), channel_id=1, source_target_pairs={{0,8},{1,9},{2,10},{3,11},{4,12},{5,13},{6,14},{7,15},{8,0},{9,1},... | collective-permute-start | bytes 196616 | tf_op jit(solution)/shard_map/ppermute | solution.py:429
  0.8 0.4 %short_tables.1 = (bf16[2,512,256]{2,1,0:T(8,128)(2,1)S(1)}, f32[2,16,128]{2,1,0:T(8,128)S(1)}) custom-call(), custom_call_target="tpu_custom_call" | custom-call | flops 5000000000 | bytes 1000000 | tf_op jit(solution)/shard_map/short_tables/pallas_call | solution.py:444
  1.1 0.0 copy-done.2
  1.1 0.0 copy-done.1
  1.2 0.8 %choose_rows.1 = (f32[8,128]{1,0:T(8,128)S(1)}, f32[8,128]{1,0:T(8,128)S(1)}, f32[1,8,128]{2,1,0:T(8,128)S(1)}, s32[8,128]{1,0:T(8,128)S(1)}) custom-call(s32[2]{0:T(128)S(1)} %copy-done.2, s32[4,128]{1,0:T(4,128)S(1)} %bitcast.3, f32[2,16,128]{2,1,0:T(8,128)S(1)} %get-tuple-element.16.after_ref.twiddle_ref.refs_4_), custom_call_target="tpu_custom_call" | custom-call | tf_op jit(solution)/shard_map/choose_rows/pallas_call | solution.py:457
  1.9 0.0 collective-permute-done.1.other_ref
  1.9 0.0 copy-done
  2.0 1.5 %collective-permute-start.2 = (bf16[8,2048]{1,0:T(8,128)(2,1)S(1)}, bf16[8,2048]{1,0:T(8,128)(2,1)S(1)}, u32[]{:S(2)}, u32[]{:S(2)}) collective-permute-start(bf16[8,2048]{1,0:T(8,128)(2,1)S(1)} %pick_rows.3), channel_id=1, source_target_pairs={{0,24},{1,25},{2,26},{3,27},{4,28},{5,29},{6,30},{7,31},{8,16},{9,... | collective-permute-start | bytes 98312 | tf_op jit(solution)/shard_map/ppermute | solution.py:429
  3.4 0.6 %receiver_spectra.1 = (bf16[256,128]{1,0:T(8,128)(2,1)S(1)}, f32[64,128]{1,0:T(8,128)S(1)}, f32[64,128]{1,0:T(8,128)S(1)}) custom-call(s32[8,128]{1,0:T(8,128)S(1)} %get-tuple-element.17.info_ref, s32[4,128]{1,0:T(4,128)S(1)} %bitcast.4, bf16[4,4,2048]{2,1,0:T(4,128)(2,1)S(1)} %copy-done, f32[2,16,128]{2,1,0:T(8,128)S(1)} %get-tuple-element.16.after_ref.twiddle_ref.refs_4_, ...), custom_call_target="tpu_custom_call" | custom-call | flops 5000000000 | bytes 1000000 | tf_op jit(solution)/shard_map/receiver_spectra/pallas_call | solution.py:491
  4.0 1.4 %collective-permute-start = (bf16[256,128]{1,0:T(8,128)(2,1)S(1)}, bf16[256,128]{1,0:T(8,128)(2,1)S(1)}, u32[]{:S(2)}, u32[]{:S(2)}) collective-permute-start(bf16[256,128]{1,0:T(8,128)(2,1)S(1)} %get-tuple-element.19.refs_6_.refs_3_.refs_1_), channel_id=1, source_target_pairs={{0,9},{1,8},{2,11},{3,10},{4,13},{5,12},{6,15},{7,14},{8,1},{9,0},... | collective-permute-start | bytes 196616 | tf_op jit(solution)/shard_map/ppermute | solution.py:429
  5.5 0.0 collective-permute-done.2.refs_3_
  5.5 0.4 %source_spectra.1 = bf16[128,128]{1,0:T(8,128)(2,1)S(1)} custom-call(f32[8,128]{1,0:T(8,128)S(1)} %bitcast.2, f32[8,128]{1,0:T(8,128)S(1)} %get-tuple-element.23.refs_1_, bf16[8,2048]{1,0:T(8,128)(2,1)S(1)} %pick_rows.2.refs_2_, bf16[8,2048]{1,0:T(8,128)(2,1)S(1)} %collective-permute-done.2.refs_3_, ...), custom_call_target="tpu_custom_call" | custom-call | tf_op jit(solution)/shard_map/source_spectra/pallas_call | solution.py:509
  5.9 0.3 %collective-permute-start.3 = (bf16[128,128]{1,0:T(8,128)(2,1)S(1)}, bf16[128,128]{1,0:T(8,128)(2,1)S(1)}, u32[]{:S(2)}, u32[]{:S(2)}) collective-permute-start(bf16[128,128]{1,0:T(8,128)(2,1)S(1)} %source_spectra.1), channel_id=1, source_target_pairs={{0,12},{1,13},{2,14},{3,15},{4,8},{5,9},{6,10},{7,11},{8,4},{9,5},... | collective-permute-start | bytes 98312 | tf_op jit(solution)/shard_map/ppermute | solution.py:429
  6.2 0.3 %collective-permute-start.5 = (bf16[128,128]{1,0:T(8,128)(2,1)S(1)}, bf16[128,128]{1,0:T(8,128)(2,1)S(1)}, u32[]{:S(2)}, u32[]{:S(2)}) collective-permute-start(bf16[128,128]{1,0:T(8,128)(2,1)S(1)} %source_spectra.1), channel_id=1, source_target_pairs={{0,10},{1,11},{2,8},{3,9},{4,14},{5,15},{6,12},{7,13},{8,2},{9,3},... | collective-permute-start | bytes 98312 | tf_op jit(solution)/shard_map/ppermute | solution.py:429
  6.5 1.5 %collective-permute-done.after_ref.refs_1_ = bf16[256,128]{1,0:T(8,128)(2,1)S(1)} collective-permute-done((bf16[256,128]{1,0:T(8,128)(2,1)S(1)}, bf16[256,128]{1,0:T(8,128)(2,1)S(1)}, u32[]{:S(2)}, u32[]{:S(2)}) %collective-permute-start) | collective-permute-done | bytes 65568 | tf_op jit(solution)/shard_map/ppermute | solution.py:429
  8.0 3.0 %collective-permute-done.3.value_ref = bf16[128,128]{1,0:T(8,128)(2,1)S(1)} collective-permute-done((bf16[128,128]{1,0:T(8,128)(2,1)S(1)}, bf16[128,128]{1,0:T(8,128)(2,1)S(1)}, u32[]{:S(2)}, u32[]{:S(2)}) %collective-permute-start.3) | collective-permute-done | bytes 32800 | tf_op jit(solution)/shard_map/ppermute | solution.py:429
  11.0 0.1 collective-permute-start.7
  11.1 0.5 %collective-permute-start.4 = (bf16[256,128]{1,0:T(8,128)(2,1)S(1)}, bf16[256,128]{1,0:T(8,128)(2,1)S(1)}, u32[]{:S(2)}, u32[]{:S(2)}) collective-permute-start(bf16[256,128]{1,0:T(8,128)(2,1)S(1)} %pad_maximum_fusion.refs_5_), channel_id=1, source_target_pairs={{0,8},{1,9},{2,10},{3,11},{4,12},{5,13},{6,14},{7,15},{8,0},{9,1},... | collective-permute-start | bytes 196616 | tf_op jit(solution)/shard_map/ppermute | solution.py:429
  11.5 0.0 collective-permute-done.5.refs_4_
  11.5 0.1 collective-permute-start.6
  11.6 0.5 %correlate_part.4 = (bf16[16,512]{1,0:T(8,128)(2,1)S(1)}, bf16[16,512]{1,0:T(8,128)(2,1)S(1)}) custom-call(bf16[2048,512]{1,0:T(8,128)(2,1)S(1)} %copy-done.3, bf16[256,128]{1,0:T(8,128)(2,1)S(1)} %collective-permute-done.after_ref.refs_1_, f32[64,128]{1,0:T(8,128)S(1)} %get-tuple-element.20.refs_2_, ...), custom_call_target="tpu_custom_call" | custom-call | flops 1000000000 | bytes 1000000 | tf_op jit(solution)/shard_map/correlate_part/pallas_call | solution.py:522
  12.1 2.3 %collective-permute-done.7.refs_6_.refs_3_ = bf16[128,128]{1,0:T(8,128)(2,1)S(1)} collective-permute-done((bf16[128,128]{1,0:T(8,128)(2,1)S(1)}, bf16[128,128]{1,0:T(8,128)(2,1)S(1)}, u32[]{:S(2)}, u32[]{:S(2)}) %collective-permute-start.7) | collective-permute-done | bytes 32800 | tf_op jit(solution)/shard_map/ppermute | solution.py:429
  14.4 0.4 %collective-permute-start.8 = (bf16[128,128]{1,0:T(8,128)(2,1)S(1)}, bf16[128,128]{1,0:T(8,128)(2,1)S(1)}, u32[]{:S(2)}, u32[]{:S(2)}) collective-permute-start(bf16[128,128]{1,0:T(8,128)(2,1)S(1)} %collective-permute-done.7.refs_6_.refs_3_), channel_id=1, source_target_pairs={{0,8},{1,9},{2,10},{3,11},{4,12},{5,13},{6,14},{7,15},{8,0},{9,1},... | collective-permute-start | bytes 98312 | tf_op jit(solution)/shard_map/ppermute | solution.py:429
  14.8 0.0 collective-permute-done.6.refs_5_
  14.8 0.0 collective-permute-done.4.refs_3_
  14.8 0.5 %correlate_part.6 = bf16[32,512]{1,0:T(8,128)(2,1)S(1)} custom-call(bf16[2048,512]{1,0:T(8,128)(2,1)S(1)} %copy-done.3, bf16[256,128]{1,0:T(8,128)(2,1)S(1)} %collective-permute-done.after_ref.refs_1_, f32[64,128]{1,0:T(8,128)S(1)} %get-tuple-element.20.refs_2_, bf16[256,128]{1,0:T(8,128)(2,1)S(1)} %collective-permute-done.4.refs_3_, ...), custom_call_target="tpu_custom_call" | custom-call | flops 1000000000 | bytes 1000000 | tf_op jit(solution)/shard_map/correlate_part/pallas_call | solution.py:522
  15.4 0.3 %collective-permute-done.8.refs_7_.refs_4_ = bf16[128,128]{1,0:T(8,128)(2,1)S(1)} collective-permute-done((bf16[128,128]{1,0:T(8,128)(2,1)S(1)}, bf16[128,128]{1,0:T(8,128)(2,1)S(1)}, u32[]{:S(2)}, u32[]{:S(2)}) %collective-permute-start.8) | collective-permute-done | bytes 32800 | tf_op jit(solution)/shard_map/ppermute | solution.py:429
  15.7 0.4 %correlate_part.7 = bf16[16,512]{1,0:T(8,128)(2,1)S(1)} custom-call(bf16[2048,512]{1,0:T(8,128)(2,1)S(1)} %copy-done.3, bf16[256,128]{1,0:T(8,128)(2,1)S(1)} %collective-permute-done.after_ref.refs_1_, f32[64,128]{1,0:T(8,128)S(1)} %get-tuple-element.20.refs_2_, bf16[128,128]{1,0:T(8,128)(2,1)S(1)} %collective-permute-done.7.refs_6_.refs_3_, ...), custom_call_target="tpu_custom_call" | custom-call | flops 1000000000 | bytes 1000000 | tf_op jit(solution)/shard_map/correlate_part/pallas_call | solution.py:522
  16.1 1.4 %collective-permute-start.9 = (bf16[64,512]{1,0:T(8,128)(2,1)S(1)}, bf16[64,512]{1,0:T(8,128)(2,1)S(1)}, u32[]{:S(2)}, u32[]{:S(2)}) collective-permute-start(bf16[64,512]{1,0:T(8,128)(2,1)S(1)} %pad_maximum_fusion.1), channel_id=1, source_target_pairs={{0,9},{1,8},{2,11},{3,10},{4,13},{5,12},{6,15},{7,14},{8,1},{9,0},... | collective-permute-start | bytes 196616 | tf_op jit(solution)/shard_map/ppermute | solution.py:429
  17.5 0.6 %correlate_part.5.refs_1_ = bf16[48,512]{1,0:T(8,128)(2,1)S(1)} custom-call(bf16[2048,512]{1,0:T(8,128)(2,1)S(1)} %copy-done.3, bf16[256,128]{1,0:T(8,128)(2,1)S(1)} %get-tuple-element.19.refs_6_.refs_3_.refs_1_, f32[64,128]{1,0:T(8,128)S(1)} %get-tuple-element.21.refs_4_.refs_2_, bf16[256,128]{1,0:T(8,128)(2,1)S(1)} %collective-permute-done.4.refs_3_, ...), custom_call_target="tpu_custom_call" | custom-call | flops 1000000000 | bytes 1000000 | tf_op jit(solution)/shard_map/correlate_part/pallas_call | solution.py:522
  18.1 2.1 %collective-permute-done.9.refs_2_ = bf16[64,512]{1,0:T(8,128)(2,1)S(1)} collective-permute-done((bf16[64,512]{1,0:T(8,128)(2,1)S(1)}, bf16[64,512]{1,0:T(8,128)(2,1)S(1)}, u32[]{:S(2)}, u32[]{:S(2)}) %collective-permute-start.9) | collective-permute-done | bytes 65568 | tf_op jit(solution)/shard_map/ppermute | solution.py:429
  20.2 0.7 %place_rows.1 = bf16[2,16,4,512]{3,2,1,0:T(4,128)(2,1)} custom-call(bf16[16,512]{1,0:T(8,128)(2,1)S(1)} %get-tuple-element.25.refs_0_, bf16[48,512]{1,0:T(8,128)(2,1)S(1)} %correlate_part.5.refs_1_, bf16[64,512]{1,0:T(8,128)(2,1)S(1)} %collective-permute-done.9.refs_2_), custom_call_target="tpu_custom_call" | custom-call | tf_op jit(solution)/shard_map/place_rows/pallas_call | solution.py:563
  (10 shorter events, 0.1 us)
Async XLA Ops:
  0.0 1.9 %copy-start = (bf16[4,4,2048]{2,1,0:T(4,128)(2,1)S(1)}, bf16[4,4,2048]{2,1,0:T(4,128)(2,1)}, u32[]{:S(2)}) copy-start(bf16[4,4,2048]{2,1,0:T(4,128)(2,1)} %own_ref.3) | copy-start | bytes 196612
  0.0 1.1 %copy-start.2 = (s32[2]{0:T(128)S(1)}, s32[2]{0:T(128)}, u32[]{:S(2)}) copy-start(s32[2]{0:T(128)} %ids_ref.1) | copy-start | bytes 28
  0.0 1.1 %copy-start.1 = (s32[128,4]{0,1:T(4,128)S(1)}, s32[128,4]{0,1:T(4,128)}, u32[]{:S(2)}) copy-start(s32[128,4]{0,1:T(4,128)} %param.5) | copy-start | bytes 6148
  0.0 1.9 %collective-permute-start.1 = (bf16[4,4,2048]{2,1,0:T(4,128)(2,1)}, bf16[4,4,2048]{2,1,0:T(4,128)(2,1)S(1)}, u32[]{:S(2)}, u32[]{:S(2)}) collective-permute-start(bf16[4,4,2048]{2,1,0:T(4,128)(2,1)} %own_ref.3), channel_id=1, source_target_pairs={{0,8},{1,9},{2,10},{3,11},{4,12},{5,13},{6,14},{7,15},{8,0},{9,1},... | collective-permute-start | bytes 196616 | tf_op jit(solution)/shard_map/ppermute | solution.py:429
  2.0 3.5 %collective-permute-start.2 = (bf16[8,2048]{1,0:T(8,128)(2,1)S(1)}, bf16[8,2048]{1,0:T(8,128)(2,1)S(1)}, u32[]{:S(2)}, u32[]{:S(2)}) collective-permute-start(bf16[8,2048]{1,0:T(8,128)(2,1)S(1)} %pick_rows.3), channel_id=1, source_target_pairs={{0,24},{1,25},{2,26},{3,27},{4,28},{5,29},{6,30},{7,31},{8,16},{9,... | collective-permute-start | bytes 98312 | tf_op jit(solution)/shard_map/ppermute | solution.py:429
  3.4 8.2 %copy-start.3 = (bf16[2048,512]{1,0:T(8,128)(2,1)S(1)}, bf16[2048,512]{1,0:T(8,128)(2,1)}, u32[]{:S(2)}) copy-start(bf16[2048,512]{1,0:T(8,128)(2,1)} %constant.2.clone.refs_0_) | copy-start | bytes 6291460
  4.0 4.0 %collective-permute-start = (bf16[256,128]{1,0:T(8,128)(2,1)S(1)}, bf16[256,128]{1,0:T(8,128)(2,1)S(1)}, u32[]{:S(2)}, u32[]{:S(2)}) collective-permute-start(bf16[256,128]{1,0:T(8,128)(2,1)S(1)} %get-tuple-element.19.refs_6_.refs_3_.refs_1_), channel_id=1, source_target_pairs={{0,9},{1,8},{2,11},{3,10},{4,13},{5,12},{6,15},{7,14},{8,1},{9,0},... | collective-permute-start | bytes 196616 | tf_op jit(solution)/shard_map/ppermute | solution.py:429
  5.9 5.1 %collective-permute-start.3 = (bf16[128,128]{1,0:T(8,128)(2,1)S(1)}, bf16[128,128]{1,0:T(8,128)(2,1)S(1)}, u32[]{:S(2)}, u32[]{:S(2)}) collective-permute-start(bf16[128,128]{1,0:T(8,128)(2,1)S(1)} %source_spectra.1), channel_id=1, source_target_pairs={{0,12},{1,13},{2,14},{3,15},{4,8},{5,9},{6,10},{7,11},{8,4},{9,5},... | collective-permute-start | bytes 98312 | tf_op jit(solution)/shard_map/ppermute | solution.py:429
  6.2 5.3 %collective-permute-start.5 = (bf16[128,128]{1,0:T(8,128)(2,1)S(1)}, bf16[128,128]{1,0:T(8,128)(2,1)S(1)}, u32[]{:S(2)}, u32[]{:S(2)}) collective-permute-start(bf16[128,128]{1,0:T(8,128)(2,1)S(1)} %source_spectra.1), channel_id=1, source_target_pairs={{0,10},{1,11},{2,8},{3,9},{4,14},{5,15},{6,12},{7,13},{8,2},{9,3},... | collective-permute-start | bytes 98312 | tf_op jit(solution)/shard_map/ppermute | solution.py:429
  11.0 3.5 %collective-permute-start.7 = (bf16[128,128]{1,0:T(8,128)(2,1)S(1)}, bf16[128,128]{1,0:T(8,128)(2,1)S(1)}, u32[]{:S(2)}, u32[]{:S(2)}) collective-permute-start(bf16[128,128]{1,0:T(8,128)(2,1)S(1)} %pass_on.1), channel_id=1, source_target_pairs={{0,10},{1,11},{2,8},{3,9},{4,14},{5,15},{6,12},{7,13},{8,2},{9,3},... | collective-permute-start | bytes 98312 | tf_op jit(solution)/shard_map/ppermute | solution.py:429
  11.1 3.8 %collective-permute-start.4 = (bf16[256,128]{1,0:T(8,128)(2,1)S(1)}, bf16[256,128]{1,0:T(8,128)(2,1)S(1)}, u32[]{:S(2)}, u32[]{:S(2)}) collective-permute-start(bf16[256,128]{1,0:T(8,128)(2,1)S(1)} %pad_maximum_fusion.refs_5_), channel_id=1, source_target_pairs={{0,8},{1,9},{2,10},{3,11},{4,12},{5,13},{6,14},{7,15},{8,0},{9,1},... | collective-permute-start | bytes 196616 | tf_op jit(solution)/shard_map/ppermute | solution.py:429
  11.5 3.3 %collective-permute-start.6 = (bf16[128,128]{1,0:T(8,128)(2,1)S(1)}, bf16[128,128]{1,0:T(8,128)(2,1)S(1)}, u32[]{:S(2)}, u32[]{:S(2)}) collective-permute-start(bf16[128,128]{1,0:T(8,128)(2,1)S(1)} %collective-permute-done.5.refs_4_), channel_id=1, source_target_pairs={{0,8},{1,9},{2,10},{3,11},{4,12},{5,13},{6,14},{7,15},{8,0},{9,1},... | collective-permute-start | bytes 98312 | tf_op jit(solution)/shard_map/ppermute | solution.py:429
  14.4 1.3 %collective-permute-start.8 = (bf16[128,128]{1,0:T(8,128)(2,1)S(1)}, bf16[128,128]{1,0:T(8,128)(2,1)S(1)}, u32[]{:S(2)}, u32[]{:S(2)}) collective-permute-start(bf16[128,128]{1,0:T(8,128)(2,1)S(1)} %collective-permute-done.7.refs_6_.refs_3_), channel_id=1, source_target_pairs={{0,8},{1,9},{2,10},{3,11},{4,12},{5,13},{6,14},{7,15},{8,0},{9,1},... | collective-permute-start | bytes 98312 | tf_op jit(solution)/shard_map/ppermute | solution.py:429
  16.1 4.1 %collective-permute-start.9 = (bf16[64,512]{1,0:T(8,128)(2,1)S(1)}, bf16[64,512]{1,0:T(8,128)(2,1)S(1)}, u32[]{:S(2)}, u32[]{:S(2)}) collective-permute-start(bf16[64,512]{1,0:T(8,128)(2,1)S(1)} %pad_maximum_fusion.1), channel_id=1, source_target_pairs={{0,9},{1,8},{2,11},{3,10},{4,13},{5,12},{6,15},{7,14},{8,1},{9,0},... | collective-permute-start | bytes 196616 | tf_op jit(solution)/shard_map/ppermute | solution.py:429

commit v8 on v7

--- a/solution.py
+++ b/solution.py
@@ -16,8 +16,7 @@
 RADIX = 16
 AXES = ("grp", "dev")
 TURN_PLANE, TURN_GATHER, TURN_LAST = 1, (1, 1), 1
-BIT_ORDER = (2, 1, 0)
-SMEM = pl.BlockSpec(memory_space=pltpu.SMEM)
+BIT_ORDER = (2, 0, 1)
 VMEM = pl.BlockSpec(memory_space=pltpu.VMEM)
 AHEAD = pl.CostEstimate(flops=5_000_000_000, bytes_accessed=1_000_000, transcendentals=0)
 BESIDE = pl.CostEstimate(flops=1_000_000_000, bytes_accessed=1_000_000, transcendentals=0)
@@ -224,42 +223,49 @@
     group, member = lax.axis_index("grp"), lax.axis_index("dev")
     core, plane = group % SRC_DEV, group // SRC_DEV
     flags = usable_ref[...].astype(jnp.float32).astype(jnp.bfloat16)
-    owning = [ids_ref[t] // halves for t in range(STEPS)]
-    within = [ids_ref[t] % halves for t in range(STEPS)]
+
+    def panel(step, shape):
+        chosen = jnp.broadcast_to(ids_ref[:, step : step + 1], shape)
+        return lax.div(chosen, halves), lax.rem(chosen, halves)
 
     row = lax.broadcasted_iota(jnp.int32, choice_ref.shape, 0)
     choice = jnp.zeros(choice_ref.shape, jnp.float32)
     for t in range(STEPS):
-        apart = (owning[t] + core) % SRC_DEV
-        choice = jnp.where(row == (t * SRC_DEV + apart) * halves + within[t], 1.0, choice)
+        owning, within = panel(t, choice_ref.shape)
+        apart = lax.rem(owning + core, SRC_DEV)
+        choice = jnp.where(row == (t * SRC_DEV + apart) * halves + within, 1.0, choice)
     choice_ref[...] = choice
 
     row = lax.broadcasted_iota(jnp.int32, info_ref.shape, 0)
     info = jnp.zeros(info_ref.shape, jnp.int32)
     for t in range(STEPS):
-        start = owning[t] * members * channels + within[t] * SRC_DEV
-        info = jnp.where(row == t, start, info)
+        owning, within = panel(t, info_ref.shape)
+        info = jnp.where(row == t, owning * (members * channels) + within * SRC_DEV, info)
     info_ref[...] = info
 
-    rows = STEPS * windows
-    row = lax.broadcasted_iota(jnp.int32, (rows, total), 0)
-    lane = lax.broadcasted_iota(jnp.int32, (rows, total), 1)
-    picks = jnp.zeros((rows, total), jnp.float32)
+    shape = (STEPS * windows, total)
+    row = lax.broadcasted_iota(jnp.int32, shape, 0)
+    lane = lax.broadcasted_iota(jnp.int32, shape, 1)
+    picks = jnp.zeros(shape, jnp.float32)
     for t in range(STEPS):
-        channel = (owning[t] * members + member) * channels + within[t] * SRC_DEV + core
+        owning, within = panel(t, shape)
+        channel = (owning * members + member) * channels + within * SRC_DEV + core
         picks = jnp.where((row // windows == t) & (lane == channel), 1.0, picks)
     mask_ref[...] = jnp.broadcast_to(at_window(flags_of(picks, flags)), mask_ref.shape)
 
-    row = lax.broadcasted_iota(jnp.int32, take_ref.shape[1:], 0)
+    shape = take_ref.shape[1:]
+    row = lax.broadcasted_iota(jnp.int32, shape, 0)
     for index in range(take_ref.shape[0]):
-        take = jnp.zeros(take_ref.shape[1:], jnp.float32)
+        take = jnp.zeros(shape, jnp.float32)
         for t in range(STEPS):
-            differs = ((owning[t] // SRC_DEV) ^ plane) >> index & 1
-            take = jnp.where(row // windows == t, differs.astype(jnp.float32), take)
+            owning, _ = panel(t, shape)
+            differs = (lax.div(owning, SRC_DEV) ^ plane) & (1 << index)
+            take = jnp.where((row // windows == t) & (differs != 0), 1.0, take)
         take_ref[index] = take
 
 
-def pick_kernel(flip, choice_ref, own_ref, other_ref, out_ref, samples):
+def pick_kernel(flip, choice_ref, own_ref, other_ref, after_ref, out_ref, samples):
+    del after_ref
     channels, windows, length = own_ref.shape
     halves = channels // SRC_DEV
     half = (lax.axis_index("grp") + flip) % SRC_DEV
@@ -462,29 +468,11 @@
             jax.ShapeDtypeStruct((plane_bits, source_rows, width), jnp.float32),
             jax.ShapeDtypeStruct((8, width), jnp.int32),
         ],
-        in_specs=[SMEM] + [VMEM] * 2,
+        in_specs=[VMEM] * 3,
         out_specs=[VMEM] * 4,
         compiler_params=PARAMS,
         name="choose_rows",
-    )(panel_ids, usable_rows, twiddle)
-
-    def pick(flip):
-        return pl.pallas_call(
-            functools.partial(pick_kernel, flip),
-            out_shape=jax.ShapeDtypeStruct((source_rows, length), records.dtype),
-            in_specs=[VMEM] * 3,
-            out_specs=VMEM,
-            scratch_shapes=[pltpu.VMEM((source_rows, length), jnp.float32)],
-            compiler_params=PARAMS,
-            name="pick_rows",
-        )(choice, records, records_other)
-
-    sent = pick(TURN_PLANE)
-    came = exchange(sent, SRC_DEV * (planes // 2) + TURN_PLANE, 0)
-    kept = pick(0) if TURN_PLANE else sent
-    for index in range(plane_bits - 2, -1, -1):
-        kept = jnp.where(take[index + 1][:, :1] > 0.0, came, kept)
-        came = exchange(kept, SRC_DEV << index, 0)
+    )(panel_ids[None, :], usable_rows, twiddle)
 
     row_count = channels * windows
     pairs = len(order) * STEPS * channels
@@ -505,6 +493,24 @@
         cost_estimate=AHEAD,
         name="receiver_spectra",
     )(info, usable_rows, records, twiddle, table)
+
+    def pick(flip):
+        return pl.pallas_call(
+            functools.partial(pick_kernel, flip),
+            out_shape=jax.ShapeDtypeStruct((source_rows, length), records.dtype),
+            in_specs=[VMEM] * 4,
+            out_specs=VMEM,
+            scratch_shapes=[pltpu.VMEM((source_rows, length), jnp.float32)],
+            compiler_params=PARAMS,
+            name="pick_rows",
+        )(choice, records, records_other, inverse)
+
+    sent = pick(TURN_PLANE)
+    came = exchange(sent, SRC_DEV * (planes // 2) + TURN_PLANE, 0)
+    kept = pick(0) if TURN_PLANE else sent
+    for index in range(plane_bits - 2, -1, -1):
+        kept = jnp.where(take[index + 1][:, :1] > 0.0, came, kept)
+        came = exchange(kept, SRC_DEV << index, 0)
 
     piece = pl.pallas_call(
         functools.partial(source_kernel, radius),

time: 21.3 us -> 21 us (0.986); the launches traced: 20.9 us -> 20.9 us
  Pallas kernels: 4.93 us -> 4.45 us
  waiting for transfers between devices: 9.23 us -> 9.64 us
    pallas_call x1, Pallas kernels: 0.77 us -> 0.28 us  [on_device(): pl.pallas_call(functools.partial(choice_kernel, halves, channels), out_sh...]
    ppermute x10, waiting for transfers between devices: 9.23 us -> 9.64 us  [exchange(): return lax.ppermute(value, AXES, pairs)]
  transfers between devices with their start and end apart: 10 -> 10, of which waited for: 5 -> 5; matrix products, arithmetic and copies ran while one was open for 0% -> 0% of each run, Pallas kernels for 18% -> 16%
where the time goes in v8:
time: 21 us; the launch traced here: 20.9 us
  waiting for transfers between devices  9.64 us (46%)
  starting transfers between devices  6.65 us (32%)
  Pallas kernels  4.45 us (21%)
    ppermute x10, waiting for transfers between devices, exchange(): return lax.ppermute(value, AXES, pairs)  9.64 us
    ppermute x10, starting transfers between devices, exchange(): return lax.ppermute(value, AXES, pairs)  6.65 us
    pallas_call x4, Pallas kernels, part(): pl.pallas_call(functools.partial(part_kernel, windows, first, len(sets)),...  2.02 us
    pallas_call x1, Pallas kernels, on_device(): pl.pallas_call(functools.partial(place_kernel, order, last_bit), out_shap...  0.69 us
    pallas_call x1, Pallas kernels, on_device(): pl.pallas_call(functools.partial(receiver_kernel, radius, order, last_bit...  0.56 us
  transfers between devices with their start and end apart: 10, of which 5 were waited for; matrix products, arithmetic and copies ran while one was open for 0% of the time, Pallas kernels for 16%

profile of v8, /device:TPU:25, one launch (start us, length us, event | category | flops | bytes accessed | tf_op | source)
XLA Modules:
  0.0 20.9 jit_solution(10147686295166807391)
XLA Ops:
  0.0 0.7 %collective-permute-start.1 = (bf16[4,4,2048]{2,1,0:T(4,128)(2,1)}, bf16[4,4,2048]{2,1,0:T(4,128)(2,1)S(1)}, u32[]{:S(2)}, u32[]{:S(2)}) collective-permute-start(bf16[4,4,2048]{2,1,0:T(4,128)(2,1)} %own_ref.3), channel_id=1, source_target_pairs={{0,8},{1,9},{2,10},{3,11},{4,12},{5,13},{6,14},{7,15},{8,0},{9,1},... | collective-permute-start | bytes 196616 | tf_op jit(solution)/shard_map/ppermute | solution.py:435
  0.8 0.4 %short_tables.1 = (bf16[2,512,256]{2,1,0:T(8,128)(2,1)S(1)}, f32[2,16,128]{2,1,0:T(8,128)S(1)}) custom-call(), custom_call_target="tpu_custom_call" | custom-call | flops 5000000000 | bytes 1000000 | tf_op jit(solution)/shard_map/short_tables/pallas_call | solution.py:450
  1.1 0.0 copy-done.2
  1.1 0.0 copy-done.1
  1.2 0.3 %choose_rows.1 = (f32[8,128]{1,0:T(8,128)S(1)}, f32[8,128]{1,0:T(8,128)S(1)}, f32[1,8,128]{2,1,0:T(8,128)S(1)}, s32[8,128]{1,0:T(8,128)S(1)}) custom-call(s32[1,2]{1,0:T(1,128)S(1)} %bitcast.6, s32[4,128]{1,0:T(4,128)S(1)} %bitcast.4, f32[2,16,128]{2,1,0:T(8,128)S(1)} %get-tuple-element.16.after_ref.twiddle_ref.refs_4_), custom_call_target="tpu_custom_call" | custom-call | tf_op jit(solution)/shard_map/choose_rows/pallas_call | solution.py:463
  1.4 0.6 %receiver_spectra.1 = (bf16[256,128]{1,0:T(8,128)(2,1)S(1)}, f32[64,128]{1,0:T(8,128)S(1)}, f32[64,128]{1,0:T(8,128)S(1)}) custom-call(s32[8,128]{1,0:T(8,128)S(1)} %get-tuple-element.17.info_ref, s32[4,128]{1,0:T(4,128)S(1)} %bitcast.5, bf16[4,4,2048]{2,1,0:T(4,128)(2,1)S(1)} %copy-done, f32[2,16,128]{2,1,0:T(8,128)S(1)} %get-tuple-element.16.after_ref.twiddle_ref.refs_4_, ...), custom_call_target="tpu_custom_call" | custom-call | flops 5000000000 | bytes 1000000 | tf_op jit(solution)/shard_map/receiver_spectra/pallas_call | solution.py:479
  2.0 0.0 collective-permute-done.1.other_ref
  2.0 0.1 pick_rows.3
  2.1 1.4 %collective-permute-start.2 = (bf16[8,2048]{1,0:T(8,128)(2,1)S(1)}, bf16[8,2048]{1,0:T(8,128)(2,1)S(1)}, u32[]{:S(2)}, u32[]{:S(2)}) collective-permute-start(bf16[8,2048]{1,0:T(8,128)(2,1)S(1)} %pick_rows.3), channel_id=1, source_target_pairs={{0,24},{1,25},{2,26},{3,27},{4,28},{5,29},{6,30},{7,31},{8,16},{9,... | collective-permute-start | bytes 98312 | tf_op jit(solution)/shard_map/ppermute | solution.py:435
  3.5 0.3 %collective-permute-start = (bf16[256,128]{1,0:T(8,128)(2,1)S(1)}, bf16[256,128]{1,0:T(8,128)(2,1)S(1)}, u32[]{:S(2)}, u32[]{:S(2)}) collective-permute-start(bf16[256,128]{1,0:T(8,128)(2,1)S(1)} %get-tuple-element.19.refs_6_.refs_3_.refs_1_), channel_id=1, source_target_pairs={{0,10},{1,11},{2,8},{3,9},{4,14},{5,15},{6,12},{7,13},{8,2},{9,3},... | collective-permute-start | bytes 196616 | tf_op jit(solution)/shard_map/ppermute | solution.py:435
  3.9 1.6 %collective-permute-done.2.refs_3_ = bf16[8,2048]{1,0:T(8,128)(2,1)S(1)} collective-permute-done((bf16[8,2048]{1,0:T(8,128)(2,1)S(1)}, bf16[8,2048]{1,0:T(8,128)(2,1)S(1)}, u32[]{:S(2)}, u32[]{:S(2)}) %collective-permute-start.2) | collective-permute-done | bytes 32800 | tf_op jit(solution)/shard_map/ppermute | solution.py:435
  5.5 0.4 %source_spectra.1 = bf16[128,128]{1,0:T(8,128)(2,1)S(1)} custom-call(f32[8,128]{1,0:T(8,128)S(1)} %bitcast.3, f32[8,128]{1,0:T(8,128)S(1)} %get-tuple-element.23.refs_1_, bf16[8,2048]{1,0:T(8,128)(2,1)S(1)} %pick_rows.2.refs_2_, bf16[8,2048]{1,0:T(8,128)(2,1)S(1)} %collective-permute-done.2.refs_3_, ...), custom_call_target="tpu_custom_call" | custom-call | tf_op jit(solution)/shard_map/source_spectra/pallas_call | solution.py:515
  5.9 0.3 %collective-permute-start.3 = (bf16[128,128]{1,0:T(8,128)(2,1)S(1)}, bf16[128,128]{1,0:T(8,128)(2,1)S(1)}, u32[]{:S(2)}, u32[]{:S(2)}) collective-permute-start(bf16[128,128]{1,0:T(8,128)(2,1)S(1)} %source_spectra.1), channel_id=1, source_target_pairs={{0,12},{1,13},{2,14},{3,15},{4,8},{5,9},{6,10},{7,11},{8,4},{9,5},... | collective-permute-start | bytes 98312 | tf_op jit(solution)/shard_map/ppermute | solution.py:435
  6.2 1.4 %collective-permute-start.5 = (bf16[128,128]{1,0:T(8,128)(2,1)S(1)}, bf16[128,128]{1,0:T(8,128)(2,1)S(1)}, u32[]{:S(2)}, u32[]{:S(2)}) collective-permute-start(bf16[128,128]{1,0:T(8,128)(2,1)S(1)} %source_spectra.1), channel_id=1, source_target_pairs={{0,9},{1,8},{2,11},{3,10},{4,13},{5,12},{6,15},{7,14},{8,1},{9,0},... | collective-permute-start | bytes 98312 | tf_op jit(solution)/shard_map/ppermute | solution.py:435
  7.5 0.0 collective-permute-done.after_ref.refs_1_
  7.5 3.4 %collective-permute-done.3.value_ref = bf16[128,128]{1,0:T(8,128)(2,1)S(1)} collective-permute-done((bf16[128,128]{1,0:T(8,128)(2,1)S(1)}, bf16[128,128]{1,0:T(8,128)(2,1)S(1)}, u32[]{:S(2)}, u32[]{:S(2)}) %collective-permute-start.3) | collective-permute-done | bytes 32800 | tf_op jit(solution)/shard_map/ppermute | solution.py:435
  10.9 1.6 %collective-permute-start.7 = (bf16[128,128]{1,0:T(8,128)(2,1)S(1)}, bf16[128,128]{1,0:T(8,128)(2,1)S(1)}, u32[]{:S(2)}, u32[]{:S(2)}) collective-permute-start(bf16[128,128]{1,0:T(8,128)(2,1)S(1)} %pass_on.1), channel_id=1, source_target_pairs={{0,9},{1,8},{2,11},{3,10},{4,13},{5,12},{6,15},{7,14},{8,1},{9,0},... | collective-permute-start | bytes 98312 | tf_op jit(solution)/shard_map/ppermute | solution.py:435
  12.5 0.1 collective-permute-start.4
  12.6 0.0 collective-permute-done.5.refs_4_
  12.6 0.4 %collective-permute-start.6 = (bf16[128,128]{1,0:T(8,128)(2,1)S(1)}, bf16[128,128]{1,0:T(8,128)(2,1)S(1)}, u32[]{:S(2)}, u32[]{:S(2)}) collective-permute-start(bf16[128,128]{1,0:T(8,128)(2,1)S(1)} %collective-permute-done.5.refs_4_), channel_id=1, source_target_pairs={{0,8},{1,9},{2,10},{3,11},{4,12},{5,13},{6,14},{7,15},{8,0},{9,1},... | collective-permute-start | bytes 98312 | tf_op jit(solution)/shard_map/ppermute | solution.py:435
  13.0 0.5 %correlate_part.4 = (bf16[16,512]{1,0:T(8,128)(2,1)S(1)}, bf16[16,512]{1,0:T(8,128)(2,1)S(1)}) custom-call(bf16[2048,512]{1,0:T(8,128)(2,1)S(1)} %copy-done.3, bf16[256,128]{1,0:T(8,128)(2,1)S(1)} %collective-permute-done.after_ref.refs_1_, f32[64,128]{1,0:T(8,128)S(1)} %get-tuple-element.20.refs_2_, ...), custom_call_target="tpu_custom_call" | custom-call | flops 1000000000 | bytes 1000000 | tf_op jit(solution)/shard_map/correlate_part/pallas_call | solution.py:528
  13.5 0.8 %collective-permute-done.7.refs_6_.refs_3_ = bf16[128,128]{1,0:T(8,128)(2,1)S(1)} collective-permute-done((bf16[128,128]{1,0:T(8,128)(2,1)S(1)}, bf16[128,128]{1,0:T(8,128)(2,1)S(1)}, u32[]{:S(2)}, u32[]{:S(2)}) %collective-permute-start.7) | collective-permute-done | bytes 32800 | tf_op jit(solution)/shard_map/ppermute | solution.py:435
  14.4 0.4 %collective-permute-start.8 = (bf16[128,128]{1,0:T(8,128)(2,1)S(1)}, bf16[128,128]{1,0:T(8,128)(2,1)S(1)}, u32[]{:S(2)}, u32[]{:S(2)}) collective-permute-start(bf16[128,128]{1,0:T(8,128)(2,1)S(1)} %collective-permute-done.7.refs_6_.refs_3_), channel_id=1, source_target_pairs={{0,8},{1,9},{2,10},{3,11},{4,12},{5,13},{6,14},{7,15},{8,0},{9,1},... | collective-permute-start | bytes 98312 | tf_op jit(solution)/shard_map/ppermute | solution.py:435
  14.8 0.0 collective-permute-done.6.refs_5_
  14.8 0.0 collective-permute-done.4.refs_3_
  14.8 0.5 %correlate_part.6 = bf16[32,512]{1,0:T(8,128)(2,1)S(1)} custom-call(bf16[2048,512]{1,0:T(8,128)(2,1)S(1)} %copy-done.3, bf16[256,128]{1,0:T(8,128)(2,1)S(1)} %collective-permute-done.after_ref.refs_1_, f32[64,128]{1,0:T(8,128)S(1)} %get-tuple-element.20.refs_2_, bf16[256,128]{1,0:T(8,128)(2,1)S(1)} %collective-permute-done.4.refs_3_, ...), custom_call_target="tpu_custom_call" | custom-call | flops 1000000000 | bytes 1000000 | tf_op jit(solution)/shard_map/correlate_part/pallas_call | solution.py:528
  15.3 0.3 %collective-permute-done.8.refs_7_.refs_4_ = bf16[128,128]{1,0:T(8,128)(2,1)S(1)} collective-permute-done((bf16[128,128]{1,0:T(8,128)(2,1)S(1)}, bf16[128,128]{1,0:T(8,128)(2,1)S(1)}, u32[]{:S(2)}, u32[]{:S(2)}) %collective-permute-start.8) | collective-permute-done | bytes 32800 | tf_op jit(solution)/shard_map/ppermute | solution.py:435
  15.6 0.4 %correlate_part.7 = bf16[16,512]{1,0:T(8,128)(2,1)S(1)} custom-call(bf16[2048,512]{1,0:T(8,128)(2,1)S(1)} %copy-done.3, bf16[256,128]{1,0:T(8,128)(2,1)S(1)} %collective-permute-done.after_ref.refs_1_, f32[64,128]{1,0:T(8,128)S(1)} %get-tuple-element.20.refs_2_, bf16[128,128]{1,0:T(8,128)(2,1)S(1)} %collective-permute-done.7.refs_6_.refs_3_, ...), custom_call_target="tpu_custom_call" | custom-call | flops 1000000000 | bytes 1000000 | tf_op jit(solution)/shard_map/correlate_part/pallas_call | solution.py:528
  16.1 0.1 collective-permute-start.9
  16.1 0.6 %correlate_part.5.refs_1_ = bf16[48,512]{1,0:T(8,128)(2,1)S(1)} custom-call(bf16[2048,512]{1,0:T(8,128)(2,1)S(1)} %copy-done.3, bf16[256,128]{1,0:T(8,128)(2,1)S(1)} %get-tuple-element.19.refs_6_.refs_3_.refs_1_, f32[64,128]{1,0:T(8,128)S(1)} %get-tuple-element.21.after_ref.refs_4_.refs_2_, bf16[256,128]{1,0:T(8,128)(2,1)S(1)} %collective-permute-done.4.refs_3_, ...), custom_call_target="tpu_custom_call" | custom-call | flops 1000000000 | bytes 1000000 | tf_op jit(solution)/shard_map/correlate_part/pallas_call | solution.py:528
  16.7 3.4 %collective-permute-done.9.refs_2_ = bf16[64,512]{1,0:T(8,128)(2,1)S(1)} collective-permute-done((bf16[64,512]{1,0:T(8,128)(2,1)S(1)}, bf16[64,512]{1,0:T(8,128)(2,1)S(1)}, u32[]{:S(2)}, u32[]{:S(2)}) %collective-permute-start.9) | collective-permute-done | bytes 65568 | tf_op jit(solution)/shard_map/ppermute | solution.py:435
  20.2 0.7 %place_rows.1 = bf16[2,16,4,512]{3,2,1,0:T(4,128)(2,1)} custom-call(bf16[16,512]{1,0:T(8,128)(2,1)S(1)} %get-tuple-element.25.refs_0_, bf16[48,512]{1,0:T(8,128)(2,1)S(1)} %correlate_part.5.refs_1_, bf16[64,512]{1,0:T(8,128)(2,1)S(1)} %collective-permute-done.9.refs_2_), custom_call_target="tpu_custom_call" | custom-call | tf_op jit(solution)/shard_map/place_rows/pallas_call | solution.py:569
  (10 shorter events, 0.1 us)
Async XLA Ops:
  0.0 1.4 %copy-start = (bf16[4,4,2048]{2,1,0:T(4,128)(2,1)S(1)}, bf16[4,4,2048]{2,1,0:T(4,128)(2,1)}, u32[]{:S(2)}) copy-start(bf16[4,4,2048]{2,1,0:T(4,128)(2,1)} %own_ref.3) | copy-start | bytes 196612
  0.0 1.1 %copy-start.2 = (s32[2]{0:T(128)S(1)}, s32[2]{0:T(128)}, u32[]{:S(2)}) copy-start(s32[2]{0:T(128)} %param.6) | copy-start | bytes 28
  0.0 1.1 %copy-start.1 = (s32[128,4]{0,1:T(4,128)S(1)}, s32[128,4]{0,1:T(4,128)}, u32[]{:S(2)}) copy-start(s32[128,4]{0,1:T(4,128)} %param.5) | copy-start | bytes 6148
  0.0 2.0 %collective-permute-start.1 = (bf16[4,4,2048]{2,1,0:T(4,128)(2,1)}, bf16[4,4,2048]{2,1,0:T(4,128)(2,1)S(1)}, u32[]{:S(2)}, u32[]{:S(2)}) collective-permute-start(bf16[4,4,2048]{2,1,0:T(4,128)(2,1)} %own_ref.3), channel_id=1, source_target_pairs={{0,8},{1,9},{2,10},{3,11},{4,12},{5,13},{6,14},{7,15},{8,0},{9,1},... | collective-permute-start | bytes 196616 | tf_op jit(solution)/shard_map/ppermute | solution.py:435
  1.4 11.6 %copy-start.3 = (bf16[2048,512]{1,0:T(8,128)(2,1)S(1)}, bf16[2048,512]{1,0:T(8,128)(2,1)}, u32[]{:S(2)}) copy-start(bf16[2048,512]{1,0:T(8,128)(2,1)} %constant.2.clone.refs_0_) | copy-start | bytes 6291460
  2.1 3.4 %collective-permute-start.2 = (bf16[8,2048]{1,0:T(8,128)(2,1)S(1)}, bf16[8,2048]{1,0:T(8,128)(2,1)S(1)}, u32[]{:S(2)}, u32[]{:S(2)}) collective-permute-start(bf16[8,2048]{1,0:T(8,128)(2,1)S(1)} %pick_rows.3), channel_id=1, source_target_pairs={{0,24},{1,25},{2,26},{3,27},{4,28},{5,29},{6,30},{7,31},{8,16},{9,... | collective-permute-start | bytes 98312 | tf_op jit(solution)/shard_map/ppermute | solution.py:435
  3.5 4.0 %collective-permute-start = (bf16[256,128]{1,0:T(8,128)(2,1)S(1)}, bf16[256,128]{1,0:T(8,128)(2,1)S(1)}, u32[]{:S(2)}, u32[]{:S(2)}) collective-permute-start(bf16[256,128]{1,0:T(8,128)(2,1)S(1)} %get-tuple-element.19.refs_6_.refs_3_.refs_1_), channel_id=1, source_target_pairs={{0,10},{1,11},{2,8},{3,9},{4,14},{5,15},{6,12},{7,13},{8,2},{9,3},... | collective-permute-start | bytes 196616 | tf_op jit(solution)/shard_map/ppermute | solution.py:435
  5.9 5.0 %collective-permute-start.3 = (bf16[128,128]{1,0:T(8,128)(2,1)S(1)}, bf16[128,128]{1,0:T(8,128)(2,1)S(1)}, u32[]{:S(2)}, u32[]{:S(2)}) collective-permute-start(bf16[128,128]{1,0:T(8,128)(2,1)S(1)} %source_spectra.1), channel_id=1, source_target_pairs={{0,12},{1,13},{2,14},{3,15},{4,8},{5,9},{6,10},{7,11},{8,4},{9,5},... | collective-permute-start | bytes 98312 | tf_op jit(solution)/shard_map/ppermute | solution.py:435
  6.2 6.5 %collective-permute-start.5 = (bf16[128,128]{1,0:T(8,128)(2,1)S(1)}, bf16[128,128]{1,0:T(8,128)(2,1)S(1)}, u32[]{:S(2)}, u32[]{:S(2)}) collective-permute-start(bf16[128,128]{1,0:T(8,128)(2,1)S(1)} %source_spectra.1), channel_id=1, source_target_pairs={{0,9},{1,8},{2,11},{3,10},{4,13},{5,12},{6,15},{7,14},{8,1},{9,0},... | collective-permute-start | bytes 98312 | tf_op jit(solution)/shard_map/ppermute | solution.py:435
  10.9 3.5 %collective-permute-start.7 = (bf16[128,128]{1,0:T(8,128)(2,1)S(1)}, bf16[128,128]{1,0:T(8,128)(2,1)S(1)}, u32[]{:S(2)}, u32[]{:S(2)}) collective-permute-start(bf16[128,128]{1,0:T(8,128)(2,1)S(1)} %pass_on.1), channel_id=1, source_target_pairs={{0,9},{1,8},{2,11},{3,10},{4,13},{5,12},{6,15},{7,14},{8,1},{9,0},... | collective-permute-start | bytes 98312 | tf_op jit(solution)/shard_map/ppermute | solution.py:435
  12.5 2.3 %collective-permute-start.4 = (bf16[256,128]{1,0:T(8,128)(2,1)S(1)}, bf16[256,128]{1,0:T(8,128)(2,1)S(1)}, u32[]{:S(2)}, u32[]{:S(2)}) collective-permute-start(bf16[256,128]{1,0:T(8,128)(2,1)S(1)} %pad_maximum_fusion.refs_5_), channel_id=1, source_target_pairs={{0,8},{1,9},{2,10},{3,11},{4,12},{5,13},{6,14},{7,15},{8,0},{9,1},... | collective-permute-start | bytes 196616 | tf_op jit(solution)/shard_map/ppermute | solution.py:435
  12.6 2.2 %collective-permute-start.6 = (bf16[128,128]{1,0:T(8,128)(2,1)S(1)}, bf16[128,128]{1,0:T(8,128)(2,1)S(1)}, u32[]{:S(2)}, u32[]{:S(2)}) collective-permute-start(bf16[128,128]{1,0:T(8,128)(2,1)S(1)} %collective-permute-done.5.refs_4_), channel_id=1, source_target_pairs={{0,8},{1,9},{2,10},{3,11},{4,12},{5,13},{6,14},{7,15},{8,0},{9,1},... | collective-permute-start | bytes 98312 | tf_op jit(solution)/shard_map/ppermute | solution.py:435
  14.4 1.3 %collective-permute-start.8 = (bf16[128,128]{1,0:T(8,128)(2,1)S(1)}, bf16[128,128]{1,0:T(8,128)(2,1)S(1)}, u32[]{:S(2)}, u32[]{:S(2)}) collective-permute-start(bf16[128,128]{1,0:T(8,128)(2,1)S(1)} %collective-permute-done.7.refs_6_.refs_3_), channel_id=1, source_target_pairs={{0,8},{1,9},{2,10},{3,11},{4,12},{5,13},{6,14},{7,15},{8,0},{9,1},... | collective-permute-start | bytes 98312 | tf_op jit(solution)/shard_map/ppermute | solution.py:435
  16.1 4.1 %collective-permute-start.9 = (bf16[64,512]{1,0:T(8,128)(2,1)S(1)}, bf16[64,512]{1,0:T(8,128)(2,1)S(1)}, u32[]{:S(2)}, u32[]{:S(2)}) collective-permute-start(bf16[64,512]{1,0:T(8,128)(2,1)S(1)} %pad_maximum_fusion.1), channel_id=1, source_target_pairs={{0,10},{1,11},{2,8},{3,9},{4,14},{5,15},{6,12},{7,13},{8,2},{9,3},... | collective-permute-start | bytes 196616 | tf_op jit(solution)/shard_map/ppermute | solution.py:435

commit v9 on v8

--- a/solution.py
+++ b/solution.py
@@ -45,9 +45,7 @@
         for part, values in enumerate(((c, -s), (s, c))):
             rows = slice((2 * h + part) * points, (2 * h + part + 1) * points)
             whole = jnp.concatenate(values, axis=1)
-            high = whole.astype(jnp.bfloat16)
-            table_ref[0, rows, :] = high
-            table_ref[1, rows, :] = (whole - high.astype(jnp.float32)).astype(jnp.bfloat16)
+            table_ref[rows, :] = whole.astype(jnp.bfloat16)
     residue = lax.broadcasted_iota(jnp.int32, (RADIX, points), 0) + 1
     sample = lax.broadcasted_iota(jnp.int32, (RADIX, points), 1)
     phases = (2.0 * math.pi / length) * (residue * sample).astype(jnp.float32)
@@ -122,11 +120,10 @@
     high = stacked.astype(jnp.bfloat16)
     low = (stacked - high.astype(jnp.float32)).astype(jnp.bfloat16)
     both = jnp.dot(
-        jnp.concatenate([high, low], axis=0), table_ref[0], preferred_element_type=jnp.float32
+        jnp.concatenate([high, low], axis=0), table_ref[...], preferred_element_type=jnp.float32
     )
     count = stacked.shape[0]
     out = both[:count] + both[count:]
-    out = out + jnp.dot(high, table_ref[1], preferred_element_type=jnp.float32)
     width = out.shape[1] // 2
     re = [out[q * rows : (q + 1) * rows, :width] for q in range(RADIX // 2)]
     im = [out[q * rows : (q + 1) * rows, width:] for q in range(RADIX // 2)]
@@ -450,7 +447,7 @@
     table, twiddle = pl.pallas_call(
         functools.partial(tables_kernel, length),
         out_shape=[
-            jax.ShapeDtypeStruct((2, 4 * points, 2 * points), jnp.bfloat16),
+            jax.ShapeDtypeStruct((4 * points, 2 * points), jnp.bfloat16),
             jax.ShapeDtypeStruct((2, RADIX, points), jnp.float32),
         ],
         in_specs=[],

time: 21 us -> 21 us (level)
  transfers between devices with their start and end apart: 10 -> 10, of which waited for: 5 -> 5; matrix products, arithmetic and copies ran while one was open for 0% -> 0% of each run, Pallas kernels for 16% -> 15%
where the time goes in v9:
time: 21 us; the launch traced here: 20.8 us
  waiting for transfers between devices  9.74 us (46%)
  starting transfers between devices  6.64 us (32%)
  Pallas kernels  4.33 us (21%)
    ppermute x10, waiting for transfers between devices, exchange(): return lax.ppermute(value, AXES, pairs)  9.74 us
    ppermute x10, starting transfers between devices, exchange(): return lax.ppermute(value, AXES, pairs)  6.64 us
    pallas_call x4, Pallas kernels, part(): pl.pallas_call(functools.partial(part_kernel, windows, first, len(sets)),...  2.02 us
    pallas_call x1, Pallas kernels, on_device(): pl.pallas_call(functools.partial(place_kernel, order, last_bit), out_shap...  0.69 us
    pallas_call x1, Pallas kernels, on_device(): pl.pallas_call(functools.partial(receiver_kernel, radius, order, last_bit...  0.52 us
  transfers between devices with their start and end apart: 10, of which 5 were waited for; matrix products, arithmetic and copies ran while one was open for 0% of the time, Pallas kernels for 15%

profile of v9, /device:TPU:25, one launch (start us, length us, event | category | flops | bytes accessed | tf_op | source)
XLA Modules:
  0.0 20.8 jit_solution(8470444832101216376)
XLA Ops:
  0.0 0.7 %collective-permute-start.1 = (bf16[4,4,2048]{2,1,0:T(4,128)(2,1)}, bf16[4,4,2048]{2,1,0:T(4,128)(2,1)S(1)}, u32[]{:S(2)}, u32[]{:S(2)}) collective-permute-start(bf16[4,4,2048]{2,1,0:T(4,128)(2,1)} %own_ref.3), channel_id=1, source_target_pairs={{0,8},{1,9},{2,10},{3,11},{4,12},{5,13},{6,14},{7,15},{8,0},{9,1},... | collective-permute-start | bytes 196616 | tf_op jit(solution)/shard_map/ppermute | solution.py:432
  0.8 0.3 %short_tables.1 = (bf16[512,256]{1,0:T(8,128)(2,1)S(1)}, f32[2,16,128]{2,1,0:T(8,128)S(1)}) custom-call(), custom_call_target="tpu_custom_call" | custom-call | flops 5000000000 | bytes 1000000 | tf_op jit(solution)/shard_map/short_tables/pallas_call | solution.py:447
  1.1 0.0 copy-done.2
  1.1 0.0 copy-done.1
  1.1 0.3 %choose_rows.1 = (f32[8,128]{1,0:T(8,128)S(1)}, f32[8,128]{1,0:T(8,128)S(1)}, f32[1,8,128]{2,1,0:T(8,128)S(1)}, s32[8,128]{1,0:T(8,128)S(1)}) custom-call(s32[1,2]{1,0:T(1,128)S(1)} %bitcast.6, s32[4,128]{1,0:T(4,128)S(1)} %bitcast.4, f32[2,16,128]{2,1,0:T(8,128)S(1)} %get-tuple-element.16.after_ref.twiddle_ref.refs_4_), custom_call_target="tpu_custom_call" | custom-call | tf_op jit(solution)/shard_map/choose_rows/pallas_call | solution.py:460
  1.4 0.5 %receiver_spectra.1 = (bf16[256,128]{1,0:T(8,128)(2,1)S(1)}, f32[64,128]{1,0:T(8,128)S(1)}, f32[64,128]{1,0:T(8,128)S(1)}) custom-call(s32[8,128]{1,0:T(8,128)S(1)} %get-tuple-element.17.info_ref, s32[4,128]{1,0:T(4,128)S(1)} %bitcast.5, bf16[4,4,2048]{2,1,0:T(4,128)(2,1)S(1)} %copy-done, f32[2,16,128]{2,1,0:T(8,128)S(1)} %get-tuple-element.16.after_ref.twiddle_ref.refs_4_, ...), custom_call_target="tpu_custom_call" | custom-call | flops 5000000000 | bytes 1000000 | tf_op jit(solution)/shard_map/receiver_spectra/pallas_call | solution.py:476
  1.9 0.0 collective-permute-done.1.other_ref
  1.9 0.1 pick_rows.3
  2.0 1.5 %collective-permute-start.2 = (bf16[8,2048]{1,0:T(8,128)(2,1)S(1)}, bf16[8,2048]{1,0:T(8,128)(2,1)S(1)}, u32[]{:S(2)}, u32[]{:S(2)}) collective-permute-start(bf16[8,2048]{1,0:T(8,128)(2,1)S(1)} %pick_rows.3), channel_id=1, source_target_pairs={{0,24},{1,25},{2,26},{3,27},{4,28},{5,29},{6,30},{7,31},{8,16},{9,... | collective-permute-start | bytes 98312 | tf_op jit(solution)/shard_map/ppermute | solution.py:432
  3.4 0.3 %collective-permute-start = (bf16[256,128]{1,0:T(8,128)(2,1)S(1)}, bf16[256,128]{1,0:T(8,128)(2,1)S(1)}, u32[]{:S(2)}, u32[]{:S(2)}) collective-permute-start(bf16[256,128]{1,0:T(8,128)(2,1)S(1)} %get-tuple-element.19.refs_6_.refs_3_.refs_1_), channel_id=1, source_target_pairs={{0,10},{1,11},{2,8},{3,9},{4,14},{5,15},{6,12},{7,13},{8,2},{9,3},... | collective-permute-start | bytes 196616 | tf_op jit(solution)/shard_map/ppermute | solution.py:432
  3.8 1.6 %collective-permute-done.2.refs_3_ = bf16[8,2048]{1,0:T(8,128)(2,1)S(1)} collective-permute-done((bf16[8,2048]{1,0:T(8,128)(2,1)S(1)}, bf16[8,2048]{1,0:T(8,128)(2,1)S(1)}, u32[]{:S(2)}, u32[]{:S(2)}) %collective-permute-start.2) | collective-permute-done | bytes 32800 | tf_op jit(solution)/shard_map/ppermute | solution.py:432
  5.4 0.4 %source_spectra.1 = bf16[128,128]{1,0:T(8,128)(2,1)S(1)} custom-call(f32[8,128]{1,0:T(8,128)S(1)} %bitcast.3, f32[8,128]{1,0:T(8,128)S(1)} %get-tuple-element.23.refs_1_, bf16[8,2048]{1,0:T(8,128)(2,1)S(1)} %pick_rows.2.refs_2_, bf16[8,2048]{1,0:T(8,128)(2,1)S(1)} %collective-permute-done.2.refs_3_, ...), custom_call_target="tpu_custom_call" | custom-call | tf_op jit(solution)/shard_map/source_spectra/pallas_call | solution.py:512
  5.8 0.3 %collective-permute-start.3 = (bf16[128,128]{1,0:T(8,128)(2,1)S(1)}, bf16[128,128]{1,0:T(8,128)(2,1)S(1)}, u32[]{:S(2)}, u32[]{:S(2)}) collective-permute-start(bf16[128,128]{1,0:T(8,128)(2,1)S(1)} %source_spectra.1), channel_id=1, source_target_pairs={{0,12},{1,13},{2,14},{3,15},{4,8},{5,9},{6,10},{7,11},{8,4},{9,5},... | collective-permute-start | bytes 98312 | tf_op jit(solution)/shard_map/ppermute | solution.py:432
  6.1 1.3 %collective-permute-start.5 = (bf16[128,128]{1,0:T(8,128)(2,1)S(1)}, bf16[128,128]{1,0:T(8,128)(2,1)S(1)}, u32[]{:S(2)}, u32[]{:S(2)}) collective-permute-start(bf16[128,128]{1,0:T(8,128)(2,1)S(1)} %source_spectra.1), channel_id=1, source_target_pairs={{0,9},{1,8},{2,11},{3,10},{4,13},{5,12},{6,15},{7,14},{8,1},{9,0},... | collective-permute-start | bytes 98312 | tf_op jit(solution)/shard_map/ppermute | solution.py:432
  7.4 0.0 collective-permute-done.after_ref.refs_1_
  7.4 3.5 %collective-permute-done.3.value_ref = bf16[128,128]{1,0:T(8,128)(2,1)S(1)} collective-permute-done((bf16[128,128]{1,0:T(8,128)(2,1)S(1)}, bf16[128,128]{1,0:T(8,128)(2,1)S(1)}, u32[]{:S(2)}, u32[]{:S(2)}) %collective-permute-start.3) | collective-permute-done | bytes 32800 | tf_op jit(solution)/shard_map/ppermute | solution.py:432
  10.9 1.6 %collective-permute-start.7 = (bf16[128,128]{1,0:T(8,128)(2,1)S(1)}, bf16[128,128]{1,0:T(8,128)(2,1)S(1)}, u32[]{:S(2)}, u32[]{:S(2)}) collective-permute-start(bf16[128,128]{1,0:T(8,128)(2,1)S(1)} %pass_on.1), channel_id=1, source_target_pairs={{0,9},{1,8},{2,11},{3,10},{4,13},{5,12},{6,15},{7,14},{8,1},{9,0},... | collective-permute-start | bytes 98312 | tf_op jit(solution)/shard_map/ppermute | solution.py:432
  12.5 0.1 collective-permute-start.4
  12.6 0.0 collective-permute-done.5.refs_4_
  12.6 0.4 %collective-permute-start.6 = (bf16[128,128]{1,0:T(8,128)(2,1)S(1)}, bf16[128,128]{1,0:T(8,128)(2,1)S(1)}, u32[]{:S(2)}, u32[]{:S(2)}) collective-permute-start(bf16[128,128]{1,0:T(8,128)(2,1)S(1)} %collective-permute-done.5.refs_4_), channel_id=1, source_target_pairs={{0,8},{1,9},{2,10},{3,11},{4,12},{5,13},{6,14},{7,15},{8,0},{9,1},... | collective-permute-start | bytes 98312 | tf_op jit(solution)/shard_map/ppermute | solution.py:432
  13.0 0.5 %correlate_part.4 = (bf16[16,512]{1,0:T(8,128)(2,1)S(1)}, bf16[16,512]{1,0:T(8,128)(2,1)S(1)}) custom-call(bf16[2048,512]{1,0:T(8,128)(2,1)S(1)} %copy-done.3, bf16[256,128]{1,0:T(8,128)(2,1)S(1)} %collective-permute-done.after_ref.refs_1_, f32[64,128]{1,0:T(8,128)S(1)} %get-tuple-element.20.refs_2_, ...), custom_call_target="tpu_custom_call" | custom-call | flops 1000000000 | bytes 1000000 | tf_op jit(solution)/shard_map/correlate_part/pallas_call | solution.py:525
  13.5 0.8 %collective-permute-done.7.refs_6_.refs_3_ = bf16[128,128]{1,0:T(8,128)(2,1)S(1)} collective-permute-done((bf16[128,128]{1,0:T(8,128)(2,1)S(1)}, bf16[128,128]{1,0:T(8,128)(2,1)S(1)}, u32[]{:S(2)}, u32[]{:S(2)}) %collective-permute-start.7) | collective-permute-done | bytes 32800 | tf_op jit(solution)/shard_map/ppermute | solution.py:432
  14.4 0.4 %collective-permute-start.8 = (bf16[128,128]{1,0:T(8,128)(2,1)S(1)}, bf16[128,128]{1,0:T(8,128)(2,1)S(1)}, u32[]{:S(2)}, u32[]{:S(2)}) collective-permute-start(bf16[128,128]{1,0:T(8,128)(2,1)S(1)} %collective-permute-done.7.refs_6_.refs_3_), channel_id=1, source_target_pairs={{0,8},{1,9},{2,10},{3,11},{4,12},{5,13},{6,14},{7,15},{8,0},{9,1},... | collective-permute-start | bytes 98312 | tf_op jit(solution)/shard_map/ppermute | solution.py:432
  14.7 0.0 collective-permute-done.6.refs_5_
  14.7 0.0 collective-permute-done.4.refs_3_
  14.8 0.5 %correlate_part.6 = bf16[32,512]{1,0:T(8,128)(2,1)S(1)} custom-call(bf16[2048,512]{1,0:T(8,128)(2,1)S(1)} %copy-done.3, bf16[256,128]{1,0:T(8,128)(2,1)S(1)} %collective-permute-done.after_ref.refs_1_, f32[64,128]{1,0:T(8,128)S(1)} %get-tuple-element.20.refs_2_, bf16[256,128]{1,0:T(8,128)(2,1)S(1)} %collective-permute-done.4.refs_3_, ...), custom_call_target="tpu_custom_call" | custom-call | flops 1000000000 | bytes 1000000 | tf_op jit(solution)/shard_map/correlate_part/pallas_call | solution.py:525
  15.3 0.3 %collective-permute-done.8.refs_7_.refs_4_ = bf16[128,128]{1,0:T(8,128)(2,1)S(1)} collective-permute-done((bf16[128,128]{1,0:T(8,128)(2,1)S(1)}, bf16[128,128]{1,0:T(8,128)(2,1)S(1)}, u32[]{:S(2)}, u32[]{:S(2)}) %collective-permute-start.8) | collective-permute-done | bytes 32800 | tf_op jit(solution)/shard_map/ppermute | solution.py:432
  15.6 0.4 %correlate_part.7 = bf16[16,512]{1,0:T(8,128)(2,1)S(1)} custom-call(bf16[2048,512]{1,0:T(8,128)(2,1)S(1)} %copy-done.3, bf16[256,128]{1,0:T(8,128)(2,1)S(1)} %collective-permute-done.after_ref.refs_1_, f32[64,128]{1,0:T(8,128)S(1)} %get-tuple-element.20.refs_2_, bf16[128,128]{1,0:T(8,128)(2,1)S(1)} %collective-permute-done.7.refs_6_.refs_3_, ...), custom_call_target="tpu_custom_call" | custom-call | flops 1000000000 | bytes 1000000 | tf_op jit(solution)/shard_map/correlate_part/pallas_call | solution.py:525
  16.0 0.1 collective-permute-start.9
  16.1 0.6 %correlate_part.5.refs_1_ = bf16[48,512]{1,0:T(8,128)(2,1)S(1)} custom-call(bf16[2048,512]{1,0:T(8,128)(2,1)S(1)} %copy-done.3, bf16[256,128]{1,0:T(8,128)(2,1)S(1)} %get-tuple-element.19.refs_6_.refs_3_.refs_1_, f32[64,128]{1,0:T(8,128)S(1)} %get-tuple-element.21.after_ref.refs_4_.refs_2_, bf16[256,128]{1,0:T(8,128)(2,1)S(1)} %collective-permute-done.4.refs_3_, ...), custom_call_target="tpu_custom_call" | custom-call | flops 1000000000 | bytes 1000000 | tf_op jit(solution)/shard_map/correlate_part/pallas_call | solution.py:525
  16.7 3.4 %collective-permute-done.9.refs_2_ = bf16[64,512]{1,0:T(8,128)(2,1)S(1)} collective-permute-done((bf16[64,512]{1,0:T(8,128)(2,1)S(1)}, bf16[64,512]{1,0:T(8,128)(2,1)S(1)}, u32[]{:S(2)}, u32[]{:S(2)}) %collective-permute-start.9) | collective-permute-done | bytes 65568 | tf_op jit(solution)/shard_map/ppermute | solution.py:432
  20.1 0.7 %place_rows.1 = bf16[2,16,4,512]{3,2,1,0:T(4,128)(2,1)} custom-call(bf16[16,512]{1,0:T(8,128)(2,1)S(1)} %get-tuple-element.25.refs_0_, bf16[48,512]{1,0:T(8,128)(2,1)S(1)} %correlate_part.5.refs_1_, bf16[64,512]{1,0:T(8,128)(2,1)S(1)} %collective-permute-done.9.refs_2_), custom_call_target="tpu_custom_call" | custom-call | tf_op jit(solution)/shard_map/place_rows/pallas_call | solution.py:566
  (10 shorter events, 0.1 us)
Async XLA Ops:
  0.0 1.4 %copy-start = (bf16[4,4,2048]{2,1,0:T(4,128)(2,1)S(1)}, bf16[4,4,2048]{2,1,0:T(4,128)(2,1)}, u32[]{:S(2)}) copy-start(bf16[4,4,2048]{2,1,0:T(4,128)(2,1)} %own_ref.3) | copy-start | bytes 196612
  0.0 1.1 %copy-start.2 = (s32[2]{0:T(128)S(1)}, s32[2]{0:T(128)}, u32[]{:S(2)}) copy-start(s32[2]{0:T(128)} %param.6) | copy-start | bytes 28
  0.0 1.1 %copy-start.1 = (s32[128,4]{0,1:T(4,128)S(1)}, s32[128,4]{0,1:T(4,128)}, u32[]{:S(2)}) copy-start(s32[128,4]{0,1:T(4,128)} %param.5) | copy-start | bytes 6148
  0.0 1.9 %collective-permute-start.1 = (bf16[4,4,2048]{2,1,0:T(4,128)(2,1)}, bf16[4,4,2048]{2,1,0:T(4,128)(2,1)S(1)}, u32[]{:S(2)}, u32[]{:S(2)}) collective-permute-start(bf16[4,4,2048]{2,1,0:T(4,128)(2,1)} %own_ref.3), channel_id=1, source_target_pairs={{0,8},{1,9},{2,10},{3,11},{4,12},{5,13},{6,14},{7,15},{8,0},{9,1},... | collective-permute-start | bytes 196616 | tf_op jit(solution)/shard_map/ppermute | solution.py:432
  1.4 11.6 %copy-start.3 = (bf16[2048,512]{1,0:T(8,128)(2,1)S(1)}, bf16[2048,512]{1,0:T(8,128)(2,1)}, u32[]{:S(2)}) copy-start(bf16[2048,512]{1,0:T(8,128)(2,1)} %constant.2.clone.refs_0_) | copy-start | bytes 6291460
  2.0 3.4 %collective-permute-start.2 = (bf16[8,2048]{1,0:T(8,128)(2,1)S(1)}, bf16[8,2048]{1,0:T(8,128)(2,1)S(1)}, u32[]{:S(2)}, u32[]{:S(2)}) collective-permute-start(bf16[8,2048]{1,0:T(8,128)(2,1)S(1)} %pick_rows.3), channel_id=1, source_target_pairs={{0,24},{1,25},{2,26},{3,27},{4,28},{5,29},{6,30},{7,31},{8,16},{9,... | collective-permute-start | bytes 98312 | tf_op jit(solution)/shard_map/ppermute | solution.py:432
  3.4 4.0 %collective-permute-start = (bf16[256,128]{1,0:T(8,128)(2,1)S(1)}, bf16[256,128]{1,0:T(8,128)(2,1)S(1)}, u32[]{:S(2)}, u32[]{:S(2)}) collective-permute-start(bf16[256,128]{1,0:T(8,128)(2,1)S(1)} %get-tuple-element.19.refs_6_.refs_3_.refs_1_), channel_id=1, source_target_pairs={{0,10},{1,11},{2,8},{3,9},{4,14},{5,15},{6,12},{7,13},{8,2},{9,3},... | collective-permute-start | bytes 196616 | tf_op jit(solution)/shard_map/ppermute | solution.py:432
  5.8 5.1 %collective-permute-start.3 = (bf16[128,128]{1,0:T(8,128)(2,1)S(1)}, bf16[128,128]{1,0:T(8,128)(2,1)S(1)}, u32[]{:S(2)}, u32[]{:S(2)}) collective-permute-start(bf16[128,128]{1,0:T(8,128)(2,1)S(1)} %source_spectra.1), channel_id=1, source_target_pairs={{0,12},{1,13},{2,14},{3,15},{4,8},{5,9},{6,10},{7,11},{8,4},{9,5},... | collective-permute-start | bytes 98312 | tf_op jit(solution)/shard_map/ppermute | solution.py:432
  6.1 6.5 %collective-permute-start.5 = (bf16[128,128]{1,0:T(8,128)(2,1)S(1)}, bf16[128,128]{1,0:T(8,128)(2,1)S(1)}, u32[]{:S(2)}, u32[]{:S(2)}) collective-permute-start(bf16[128,128]{1,0:T(8,128)(2,1)S(1)} %source_spectra.1), channel_id=1, source_target_pairs={{0,9},{1,8},{2,11},{3,10},{4,13},{5,12},{6,15},{7,14},{8,1},{9,0},... | collective-permute-start | bytes 98312 | tf_op jit(solution)/shard_map/ppermute | solution.py:432
  10.9 3.5 %collective-permute-start.7 = (bf16[128,128]{1,0:T(8,128)(2,1)S(1)}, bf16[128,128]{1,0:T(8,128)(2,1)S(1)}, u32[]{:S(2)}, u32[]{:S(2)}) collective-permute-start(bf16[128,128]{1,0:T(8,128)(2,1)S(1)} %pass_on.1), channel_id=1, source_target_pairs={{0,9},{1,8},{2,11},{3,10},{4,13},{5,12},{6,15},{7,14},{8,1},{9,0},... | collective-permute-start | bytes 98312 | tf_op jit(solution)/shard_map/ppermute | solution.py:432
  12.5 2.3 %collective-permute-start.4 = (bf16[256,128]{1,0:T(8,128)(2,1)S(1)}, bf16[256,128]{1,0:T(8,128)(2,1)S(1)}, u32[]{:S(2)}, u32[]{:S(2)}) collective-permute-start(bf16[256,128]{1,0:T(8,128)(2,1)S(1)} %pad_maximum_fusion.refs_5_), channel_id=1, source_target_pairs={{0,8},{1,9},{2,10},{3,11},{4,12},{5,13},{6,14},{7,15},{8,0},{9,1},... | collective-permute-start | bytes 196616 | tf_op jit(solution)/shard_map/ppermute | solution.py:432
  12.6 2.2 %collective-permute-start.6 = (bf16[128,128]{1,0:T(8,128)(2,1)S(1)}, bf16[128,128]{1,0:T(8,128)(2,1)S(1)}, u32[]{:S(2)}, u32[]{:S(2)}) collective-permute-start(bf16[128,128]{1,0:T(8,128)(2,1)S(1)} %collective-permute-done.5.refs_4_), channel_id=1, source_target_pairs={{0,8},{1,9},{2,10},{3,11},{4,12},{5,13},{6,14},{7,15},{8,0},{9,1},... | collective-permute-start | bytes 98312 | tf_op jit(solution)/shard_map/ppermute | solution.py:432
  14.4 1.3 %collective-permute-start.8 = (bf16[128,128]{1,0:T(8,128)(2,1)S(1)}, bf16[128,128]{1,0:T(8,128)(2,1)S(1)}, u32[]{:S(2)}, u32[]{:S(2)}) collective-permute-start(bf16[128,128]{1,0:T(8,128)(2,1)S(1)} %collective-permute-done.7.refs_6_.refs_3_), channel_id=1, source_target_pairs={{0,8},{1,9},{2,10},{3,11},{4,12},{5,13},{6,14},{7,15},{8,0},{9,1},... | collective-permute-start | bytes 98312 | tf_op jit(solution)/shard_map/ppermute | solution.py:432
  16.0 4.1 %collective-permute-start.9 = (bf16[64,512]{1,0:T(8,128)(2,1)S(1)}, bf16[64,512]{1,0:T(8,128)(2,1)S(1)}, u32[]{:S(2)}, u32[]{:S(2)}) collective-permute-start(bf16[64,512]{1,0:T(8,128)(2,1)S(1)} %pad_maximum_fusion.1), channel_id=1, source_target_pairs={{0,10},{1,11},{2,8},{3,9},{4,14},{5,15},{6,12},{7,13},{8,2},{9,3},... | collective-permute-start | bytes 196616 | tf_op jit(solution)/shard_map/ppermute | solution.py:432

commit v10 on v9

--- a/solution.py
+++ b/solution.py
@@ -32,13 +32,22 @@
     return np.concatenate(order)
 
 
+def turned_cos_sin(index, count):
+    angle = (index - count // 2).astype(jnp.float32) * (2.0 * math.pi / count)
+    square = angle * angle
+    cosine = sine = jnp.zeros_like(angle)
+    for n in range(8, -1, -1):
+        cosine = cosine * square + (-1) ** n / math.factorial(2 * n)
+        sine = sine * square + (-1) ** n / math.factorial(2 * n + 1)
+    return -cosine, -sine * angle
+
+
 def tables_kernel(length, table_ref, twiddle_ref):
     points = length // RADIX
     per = points // 2
     row = lax.broadcasted_iota(jnp.int32, (points, points), 0)
     lane = lax.broadcasted_iota(jnp.int32, (points, points), 1)
-    phases = (2.0 * math.pi / points) * (row * (lane % per) % points).astype(jnp.float32)
-    cosine, sine = jnp.cos(phases), jnp.sin(phases)
+    cosine, sine = turned_cos_sin(row * (lane % per) % points, points)
     for h in range(2):
         inside = (lane >= per) if h else (lane < per)
         c, s = jnp.where(inside, cosine, 0.0), jnp.where(inside, sine, 0.0)
@@ -48,9 +57,9 @@
             table_ref[rows, :] = whole.astype(jnp.bfloat16)
     residue = lax.broadcasted_iota(jnp.int32, (RADIX, points), 0) + 1
     sample = lax.broadcasted_iota(jnp.int32, (RADIX, points), 1)
-    phases = (2.0 * math.pi / length) * (residue * sample).astype(jnp.float32)
-    twiddle_ref[0] = jnp.cos(phases)
-    twiddle_ref[1] = -jnp.sin(phases)
+    cosine, sine = turned_cos_sin(residue * sample % length, length)
+    twiddle_ref[0] = cosine
+    twiddle_ref[1] = -sine
 
 
 def lag_table(length, bin_count, lag_count):

time: 21 us -> 21 us (level)
  transfers between devices with their start and end apart: 10 -> 10, of which waited for: 5 -> 6; matrix products, arithmetic and copies ran while one was open for 0% -> 0% of each run, Pallas kernels for 15% -> 14%
where the time goes in v10:
time: 21 us; the launch traced here: 20.9 us
  waiting for transfers between devices  9.95 us (47%)
  starting transfers between devices  6.68 us (32%)
  Pallas kernels  4.16 us (20%)
    ppermute x10, waiting for transfers between devices, exchange(): return lax.ppermute(value, AXES, pairs)  9.95 us
    ppermute x10, starting transfers between devices, exchange(): return lax.ppermute(value, AXES, pairs)  6.68 us
    pallas_call x4, Pallas kernels, part(): pl.pallas_call(functools.partial(part_kernel, windows, first, len(sets)),...  2.02 us
    pallas_call x1, Pallas kernels, on_device(): pl.pallas_call(functools.partial(place_kernel, order, last_bit), out_shap...  0.69 us
    pallas_call x1, Pallas kernels, on_device(): pl.pallas_call(functools.partial(receiver_kernel, radius, order, last_bit...  0.52 us
  transfers between devices with their start and end apart: 10, of which 6 were waited for; matrix products, arithmetic and copies ran while one was open for 0% of the time, Pallas kernels for 14%

profile of v10, /device:TPU:25, one launch (start us, length us, event | category | flops | bytes accessed | tf_op | source)
XLA Modules:
  0.0 20.9 jit_solution(16681783382935478464)
XLA Ops:
  0.0 0.7 %collective-permute-start.1 = (bf16[4,4,2048]{2,1,0:T(4,128)(2,1)}, bf16[4,4,2048]{2,1,0:T(4,128)(2,1)S(1)}, u32[]{:S(2)}, u32[]{:S(2)}) collective-permute-start(bf16[4,4,2048]{2,1,0:T(4,128)(2,1)} %own_ref.3), channel_id=1, source_target_pairs={{0,8},{1,9},{2,10},{3,11},{4,12},{5,13},{6,14},{7,15},{8,0},{9,1},... | collective-permute-start | bytes 196616 | tf_op jit(solution)/shard_map/ppermute | solution.py:441
  0.8 0.2 short_tables.1
  0.9 0.0 copy-done.2
  0.9 0.0 copy-done.1
  0.9 0.3 %choose_rows.1 = (f32[8,128]{1,0:T(8,128)S(1)}, f32[8,128]{1,0:T(8,128)S(1)}, f32[1,8,128]{2,1,0:T(8,128)S(1)}, s32[8,128]{1,0:T(8,128)S(1)}) custom-call(s32[1,2]{1,0:T(1,128)S(1)} %bitcast.6, s32[4,128]{1,0:T(4,128)S(1)} %bitcast.4, f32[2,16,128]{2,1,0:T(8,128)S(1)} %get-tuple-element.16.after_ref.twiddle_ref.refs_4_), custom_call_target="tpu_custom_call" | custom-call | tf_op jit(solution)/shard_map/choose_rows/pallas_call | solution.py:469
  1.2 0.0 copy-done
  1.2 0.5 %receiver_spectra.1 = (bf16[256,128]{1,0:T(8,128)(2,1)S(1)}, f32[64,128]{1,0:T(8,128)S(1)}, f32[64,128]{1,0:T(8,128)S(1)}) custom-call(s32[8,128]{1,0:T(8,128)S(1)} %get-tuple-element.17.info_ref, s32[4,128]{1,0:T(4,128)S(1)} %bitcast.5, bf16[4,4,2048]{2,1,0:T(4,128)(2,1)S(1)} %copy-done, f32[2,16,128]{2,1,0:T(8,128)S(1)} %get-tuple-element.16.after_ref.twiddle_ref.refs_4_, ...), custom_call_target="tpu_custom_call" | custom-call | flops 5000000000 | bytes 1000000 | tf_op jit(solution)/shard_map/receiver_spectra/pallas_call | solution.py:485
  1.8 0.1 collective-permute-done.1.other_ref
  1.9 1.5 %collective-permute-start.2 = (bf16[8,2048]{1,0:T(8,128)(2,1)S(1)}, bf16[8,2048]{1,0:T(8,128)(2,1)S(1)}, u32[]{:S(2)}, u32[]{:S(2)}) collective-permute-start(bf16[8,2048]{1,0:T(8,128)(2,1)S(1)} %pick_rows.3), channel_id=1, source_target_pairs={{0,24},{1,25},{2,26},{3,27},{4,28},{5,29},{6,30},{7,31},{8,16},{9,... | collective-permute-start | bytes 98312 | tf_op jit(solution)/shard_map/ppermute | solution.py:441
  3.4 0.2 collective-permute-start
  3.7 1.7 %collective-permute-done.2.refs_3_ = bf16[8,2048]{1,0:T(8,128)(2,1)S(1)} collective-permute-done((bf16[8,2048]{1,0:T(8,128)(2,1)S(1)}, bf16[8,2048]{1,0:T(8,128)(2,1)S(1)}, u32[]{:S(2)}, u32[]{:S(2)}) %collective-permute-start.2) | collective-permute-done | bytes 32800 | tf_op jit(solution)/shard_map/ppermute | solution.py:441
  5.4 0.4 %source_spectra.1 = bf16[128,128]{1,0:T(8,128)(2,1)S(1)} custom-call(f32[8,128]{1,0:T(8,128)S(1)} %bitcast.3, f32[8,128]{1,0:T(8,128)S(1)} %get-tuple-element.23.refs_1_, bf16[8,2048]{1,0:T(8,128)(2,1)S(1)} %pick_rows.2.refs_2_, bf16[8,2048]{1,0:T(8,128)(2,1)S(1)} %collective-permute-done.2.refs_3_, ...), custom_call_target="tpu_custom_call" | custom-call | tf_op jit(solution)/shard_map/source_spectra/pallas_call | solution.py:521
  5.7 0.4 %collective-permute-start.3 = (bf16[128,128]{1,0:T(8,128)(2,1)S(1)}, bf16[128,128]{1,0:T(8,128)(2,1)S(1)}, u32[]{:S(2)}, u32[]{:S(2)}) collective-permute-start(bf16[128,128]{1,0:T(8,128)(2,1)S(1)} %source_spectra.1), channel_id=1, source_target_pairs={{0,12},{1,13},{2,14},{3,15},{4,8},{5,9},{6,10},{7,11},{8,4},{9,5},... | collective-permute-start | bytes 98312 | tf_op jit(solution)/shard_map/ppermute | solution.py:441
  6.1 1.3 %collective-permute-start.5 = (bf16[128,128]{1,0:T(8,128)(2,1)S(1)}, bf16[128,128]{1,0:T(8,128)(2,1)S(1)}, u32[]{:S(2)}, u32[]{:S(2)}) collective-permute-start(bf16[128,128]{1,0:T(8,128)(2,1)S(1)} %source_spectra.1), channel_id=1, source_target_pairs={{0,9},{1,8},{2,11},{3,10},{4,13},{5,12},{6,15},{7,14},{8,1},{9,0},... | collective-permute-start | bytes 98312 | tf_op jit(solution)/shard_map/ppermute | solution.py:441
  7.4 0.0 collective-permute-done.after_ref.refs_1_
  7.4 3.5 %collective-permute-done.3.value_ref = bf16[128,128]{1,0:T(8,128)(2,1)S(1)} collective-permute-done((bf16[128,128]{1,0:T(8,128)(2,1)S(1)}, bf16[128,128]{1,0:T(8,128)(2,1)S(1)}, u32[]{:S(2)}, u32[]{:S(2)}) %collective-permute-start.3) | collective-permute-done | bytes 32800 | tf_op jit(solution)/shard_map/ppermute | solution.py:441
  10.9 1.6 %collective-permute-start.7 = (bf16[128,128]{1,0:T(8,128)(2,1)S(1)}, bf16[128,128]{1,0:T(8,128)(2,1)S(1)}, u32[]{:S(2)}, u32[]{:S(2)}) collective-permute-start(bf16[128,128]{1,0:T(8,128)(2,1)S(1)} %pass_on.1), channel_id=1, source_target_pairs={{0,9},{1,8},{2,11},{3,10},{4,13},{5,12},{6,15},{7,14},{8,1},{9,0},... | collective-permute-start | bytes 98312 | tf_op jit(solution)/shard_map/ppermute | solution.py:441
  12.5 0.1 collective-permute-start.4
  12.6 0.0 collective-permute-done.5.refs_4_
  12.7 0.4 %collective-permute-start.6 = (bf16[128,128]{1,0:T(8,128)(2,1)S(1)}, bf16[128,128]{1,0:T(8,128)(2,1)S(1)}, u32[]{:S(2)}, u32[]{:S(2)}) collective-permute-start(bf16[128,128]{1,0:T(8,128)(2,1)S(1)} %collective-permute-done.5.refs_4_), channel_id=1, source_target_pairs={{0,8},{1,9},{2,10},{3,11},{4,12},{5,13},{6,14},{7,15},{8,0},{9,1},... | collective-permute-start | bytes 98312 | tf_op jit(solution)/shard_map/ppermute | solution.py:441
  13.1 0.5 %correlate_part.4 = (bf16[16,512]{1,0:T(8,128)(2,1)S(1)}, bf16[16,512]{1,0:T(8,128)(2,1)S(1)}) custom-call(bf16[2048,512]{1,0:T(8,128)(2,1)S(1)} %copy-done.3, bf16[256,128]{1,0:T(8,128)(2,1)S(1)} %collective-permute-done.after_ref.refs_1_, f32[64,128]{1,0:T(8,128)S(1)} %get-tuple-element.20.refs_2_, ...), custom_call_target="tpu_custom_call" | custom-call | flops 1000000000 | bytes 1000000 | tf_op jit(solution)/shard_map/correlate_part/pallas_call | solution.py:534
  13.6 0.8 %collective-permute-done.7.refs_6_.refs_3_ = bf16[128,128]{1,0:T(8,128)(2,1)S(1)} collective-permute-done((bf16[128,128]{1,0:T(8,128)(2,1)S(1)}, bf16[128,128]{1,0:T(8,128)(2,1)S(1)}, u32[]{:S(2)}, u32[]{:S(2)}) %collective-permute-start.7) | collective-permute-done | bytes 32800 | tf_op jit(solution)/shard_map/ppermute | solution.py:441
  14.4 0.4 %collective-permute-start.8 = (bf16[128,128]{1,0:T(8,128)(2,1)S(1)}, bf16[128,128]{1,0:T(8,128)(2,1)S(1)}, u32[]{:S(2)}, u32[]{:S(2)}) collective-permute-start(bf16[128,128]{1,0:T(8,128)(2,1)S(1)} %collective-permute-done.7.refs_6_.refs_3_), channel_id=1, source_target_pairs={{0,8},{1,9},{2,10},{3,11},{4,12},{5,13},{6,14},{7,15},{8,0},{9,1},... | collective-permute-start | bytes 98312 | tf_op jit(solution)/shard_map/ppermute | solution.py:441
  14.8 0.0 collective-permute-done.6.refs_5_
  14.8 0.0 collective-permute-done.4.refs_3_
  14.8 0.5 %correlate_part.6 = bf16[32,512]{1,0:T(8,128)(2,1)S(1)} custom-call(bf16[2048,512]{1,0:T(8,128)(2,1)S(1)} %copy-done.3, bf16[256,128]{1,0:T(8,128)(2,1)S(1)} %collective-permute-done.after_ref.refs_1_, f32[64,128]{1,0:T(8,128)S(1)} %get-tuple-element.20.refs_2_, bf16[256,128]{1,0:T(8,128)(2,1)S(1)} %collective-permute-done.4.refs_3_, ...), custom_call_target="tpu_custom_call" | custom-call | flops 1000000000 | bytes 1000000 | tf_op jit(solution)/shard_map/correlate_part/pallas_call | solution.py:534
  15.3 0.3 %collective-permute-done.8.refs_7_.refs_4_ = bf16[128,128]{1,0:T(8,128)(2,1)S(1)} collective-permute-done((bf16[128,128]{1,0:T(8,128)(2,1)S(1)}, bf16[128,128]{1,0:T(8,128)(2,1)S(1)}, u32[]{:S(2)}, u32[]{:S(2)}) %collective-permute-start.8) | collective-permute-done | bytes 32800 | tf_op jit(solution)/shard_map/ppermute | solution.py:441
  15.7 0.4 %correlate_part.7 = bf16[16,512]{1,0:T(8,128)(2,1)S(1)} custom-call(bf16[2048,512]{1,0:T(8,128)(2,1)S(1)} %copy-done.3, bf16[256,128]{1,0:T(8,128)(2,1)S(1)} %collective-permute-done.after_ref.refs_1_, f32[64,128]{1,0:T(8,128)S(1)} %get-tuple-element.20.refs_2_, bf16[128,128]{1,0:T(8,128)(2,1)S(1)} %collective-permute-done.7.refs_6_.refs_3_, ...), custom_call_target="tpu_custom_call" | custom-call | flops 1000000000 | bytes 1000000 | tf_op jit(solution)/shard_map/correlate_part/pallas_call | solution.py:534
  16.1 0.1 collective-permute-start.9
  16.2 0.6 %correlate_part.5.refs_1_ = bf16[48,512]{1,0:T(8,128)(2,1)S(1)} custom-call(bf16[2048,512]{1,0:T(8,128)(2,1)S(1)} %copy-done.3, bf16[256,128]{1,0:T(8,128)(2,1)S(1)} %get-tuple-element.19.refs_6_.refs_3_.refs_1_, f32[64,128]{1,0:T(8,128)S(1)} %get-tuple-element.21.after_ref.refs_4_.refs_2_, bf16[256,128]{1,0:T(8,128)(2,1)S(1)} %collective-permute-done.4.refs_3_, ...), custom_call_target="tpu_custom_call" | custom-call | flops 1000000000 | bytes 1000000 | tf_op jit(solution)/shard_map/correlate_part/pallas_call | solution.py:534
  16.7 3.4 %collective-permute-done.9.refs_2_ = bf16[64,512]{1,0:T(8,128)(2,1)S(1)} collective-permute-done((bf16[64,512]{1,0:T(8,128)(2,1)S(1)}, bf16[64,512]{1,0:T(8,128)(2,1)S(1)}, u32[]{:S(2)}, u32[]{:S(2)}) %collective-permute-start.9) | collective-permute-done | bytes 65568 | tf_op jit(solution)/shard_map/ppermute | solution.py:441
  20.2 0.7 %place_rows.1 = bf16[2,16,4,512]{3,2,1,0:T(4,128)(2,1)} custom-call(bf16[16,512]{1,0:T(8,128)(2,1)S(1)} %get-tuple-element.25.refs_0_, bf16[48,512]{1,0:T(8,128)(2,1)S(1)} %correlate_part.5.refs_1_, bf16[64,512]{1,0:T(8,128)(2,1)S(1)} %collective-permute-done.9.refs_2_), custom_call_target="tpu_custom_call" | custom-call | tf_op jit(solution)/shard_map/place_rows/pallas_call | solution.py:575
  (10 shorter events, 0.1 us)
Async XLA Ops:
  0.0 1.2 %copy-start = (bf16[4,4,2048]{2,1,0:T(4,128)(2,1)S(1)}, bf16[4,4,2048]{2,1,0:T(4,128)(2,1)}, u32[]{:S(2)}) copy-start(bf16[4,4,2048]{2,1,0:T(4,128)(2,1)} %own_ref.3) | copy-start | bytes 196612
  0.0 0.9 %copy-start.2 = (s32[2]{0:T(128)S(1)}, s32[2]{0:T(128)}, u32[]{:S(2)}) copy-start(s32[2]{0:T(128)} %param.6) | copy-start | bytes 28
  0.0 0.9 %copy-start.1 = (s32[128,4]{0,1:T(4,128)S(1)}, s32[128,4]{0,1:T(4,128)}, u32[]{:S(2)}) copy-start(s32[128,4]{0,1:T(4,128)} %param.5) | copy-start | bytes 6148
  0.0 1.9 %collective-permute-start.1 = (bf16[4,4,2048]{2,1,0:T(4,128)(2,1)}, bf16[4,4,2048]{2,1,0:T(4,128)(2,1)S(1)}, u32[]{:S(2)}, u32[]{:S(2)}) collective-permute-start(bf16[4,4,2048]{2,1,0:T(4,128)(2,1)} %own_ref.3), channel_id=1, source_target_pairs={{0,8},{1,9},{2,10},{3,11},{4,12},{5,13},{6,14},{7,15},{8,0},{9,1},... | collective-permute-start | bytes 196616 | tf_op jit(solution)/shard_map/ppermute | solution.py:441
  1.2 11.8 %copy-start.3 = (bf16[2048,512]{1,0:T(8,128)(2,1)S(1)}, bf16[2048,512]{1,0:T(8,128)(2,1)}, u32[]{:S(2)}) copy-start(bf16[2048,512]{1,0:T(8,128)(2,1)} %constant.2.clone.refs_0_) | copy-start | bytes 6291460
  1.9 3.4 %collective-permute-start.2 = (bf16[8,2048]{1,0:T(8,128)(2,1)S(1)}, bf16[8,2048]{1,0:T(8,128)(2,1)S(1)}, u32[]{:S(2)}, u32[]{:S(2)}) collective-permute-start(bf16[8,2048]{1,0:T(8,128)(2,1)S(1)} %pick_rows.3), channel_id=1, source_target_pairs={{0,24},{1,25},{2,26},{3,27},{4,28},{5,29},{6,30},{7,31},{8,16},{9,... | collective-permute-start | bytes 98312 | tf_op jit(solution)/shard_map/ppermute | solution.py:441
  3.4 4.0 %collective-permute-start = (bf16[256,128]{1,0:T(8,128)(2,1)S(1)}, bf16[256,128]{1,0:T(8,128)(2,1)S(1)}, u32[]{:S(2)}, u32[]{:S(2)}) collective-permute-start(bf16[256,128]{1,0:T(8,128)(2,1)S(1)} %get-tuple-element.19.refs_6_.refs_3_.refs_1_), channel_id=1, source_target_pairs={{0,10},{1,11},{2,8},{3,9},{4,14},{5,15},{6,12},{7,13},{8,2},{9,3},... | collective-permute-start | bytes 196616 | tf_op jit(solution)/shard_map/ppermute | solution.py:441
  5.7 5.2 %collective-permute-start.3 = (bf16[128,128]{1,0:T(8,128)(2,1)S(1)}, bf16[128,128]{1,0:T(8,128)(2,1)S(1)}, u32[]{:S(2)}, u32[]{:S(2)}) collective-permute-start(bf16[128,128]{1,0:T(8,128)(2,1)S(1)} %source_spectra.1), channel_id=1, source_target_pairs={{0,12},{1,13},{2,14},{3,15},{4,8},{5,9},{6,10},{7,11},{8,4},{9,5},... | collective-permute-start | bytes 98312 | tf_op jit(solution)/shard_map/ppermute | solution.py:441
  6.1 6.5 %collective-permute-start.5 = (bf16[128,128]{1,0:T(8,128)(2,1)S(1)}, bf16[128,128]{1,0:T(8,128)(2,1)S(1)}, u32[]{:S(2)}, u32[]{:S(2)}) collective-permute-start(bf16[128,128]{1,0:T(8,128)(2,1)S(1)} %source_spectra.1), channel_id=1, source_target_pairs={{0,9},{1,8},{2,11},{3,10},{4,13},{5,12},{6,15},{7,14},{8,1},{9,0},... | collective-permute-start | bytes 98312 | tf_op jit(solution)/shard_map/ppermute | solution.py:441
  10.9 3.5 %collective-permute-start.7 = (bf16[128,128]{1,0:T(8,128)(2,1)S(1)}, bf16[128,128]{1,0:T(8,128)(2,1)S(1)}, u32[]{:S(2)}, u32[]{:S(2)}) collective-permute-start(bf16[128,128]{1,0:T(8,128)(2,1)S(1)} %pass_on.1), channel_id=1, source_target_pairs={{0,9},{1,8},{2,11},{3,10},{4,13},{5,12},{6,15},{7,14},{8,1},{9,0},... | collective-permute-start | bytes 98312 | tf_op jit(solution)/shard_map/ppermute | solution.py:441
  12.5 2.3 %collective-permute-start.4 = (bf16[256,128]{1,0:T(8,128)(2,1)S(1)}, bf16[256,128]{1,0:T(8,128)(2,1)S(1)}, u32[]{:S(2)}, u32[]{:S(2)}) collective-permute-start(bf16[256,128]{1,0:T(8,128)(2,1)S(1)} %pad_maximum_fusion.refs_5_), channel_id=1, source_target_pairs={{0,8},{1,9},{2,10},{3,11},{4,12},{5,13},{6,14},{7,15},{8,0},{9,1},... | collective-permute-start | bytes 196616 | tf_op jit(solution)/shard_map/ppermute | solution.py:441
  12.7 2.2 %collective-permute-start.6 = (bf16[128,128]{1,0:T(8,128)(2,1)S(1)}, bf16[128,128]{1,0:T(8,128)(2,1)S(1)}, u32[]{:S(2)}, u32[]{:S(2)}) collective-permute-start(bf16[128,128]{1,0:T(8,128)(2,1)S(1)} %collective-permute-done.5.refs_4_), channel_id=1, source_target_pairs={{0,8},{1,9},{2,10},{3,11},{4,12},{5,13},{6,14},{7,15},{8,0},{9,1},... | collective-permute-start | bytes 98312 | tf_op jit(solution)/shard_map/ppermute | solution.py:441
  14.4 1.3 %collective-permute-start.8 = (bf16[128,128]{1,0:T(8,128)(2,1)S(1)}, bf16[128,128]{1,0:T(8,128)(2,1)S(1)}, u32[]{:S(2)}, u32[]{:S(2)}) collective-permute-start(bf16[128,128]{1,0:T(8,128)(2,1)S(1)} %collective-permute-done.7.refs_6_.refs_3_), channel_id=1, source_target_pairs={{0,8},{1,9},{2,10},{3,11},{4,12},{5,13},{6,14},{7,15},{8,0},{9,1},... | collective-permute-start | bytes 98312 | tf_op jit(solution)/shard_map/ppermute | solution.py:441
  16.1 4.1 %collective-permute-start.9 = (bf16[64,512]{1,0:T(8,128)(2,1)S(1)}, bf16[64,512]{1,0:T(8,128)(2,1)S(1)}, u32[]{:S(2)}, u32[]{:S(2)}) collective-permute-start(bf16[64,512]{1,0:T(8,128)(2,1)S(1)} %pad_maximum_fusion.1), channel_id=1, source_target_pairs={{0,10},{1,11},{2,8},{3,9},{4,14},{5,15},{6,12},{7,13},{8,2},{9,3},... | collective-permute-start | bytes 196616 | tf_op jit(solution)/shard_map/ppermute | solution.py:441

commit v11 on v9

--- a/solution.py
+++ b/solution.py
@@ -559,10 +559,11 @@
     pieces += [second, exchange(second, 1, 0)]
     mine, other = (receivers, inverse), (theirs, inverse_theirs)
     early_theirs, early = part(0, [other, mine], held)
-    (next_theirs,) = part(pairs // 4, [other], *pieces[1:4])
-    (late_theirs,) = part(pairs // 4 * 3, [other], *pieces[4:])
+    (next_theirs,) = part(pairs // 4, [other], *pieces[1:3])
+    (more_theirs,) = part(pairs // 8 * 5, [other], *pieces[3:5])
+    (late_theirs,) = part(pairs // 8 * 7, [other], *pieces[5:])
     (late,) = part(pairs // 4, [mine], *pieces[1:])
-    back = exchange(jnp.concatenate([early_theirs, next_theirs, late_theirs], axis=0), TURN_LAST, last_bit)
+    back = exchange(jnp.concatenate([early_theirs, next_theirs, more_theirs, late_theirs], axis=0), TURN_LAST, last_bit)
     return pl.pallas_call(
         functools.partial(place_kernel, order, last_bit),
         out_shape=jax.ShapeDtypeStruct(

time: 21 us -> 21.1 us (level)
  waiting for transfers between devices: 9.74 us -> 9.31 us
  Pallas kernels: 4.33 us -> 4.74 us
    ppermute x10, waiting for transfers between devices: 9.74 us -> 9.31 us  [exchange(): return lax.ppermute(value, AXES, pairs)]
    pallas_call x4 -> x5, Pallas kernels: 2.02 us -> 2.44 us  [part(): pl.pallas_call(functools.partial(part_kernel, windows, first, len(sets)),...]
  transfers between devices with their start and end apart: 10 -> 10, of which waited for: 5 -> 4; matrix products, arithmetic and copies ran while one was open for 0% -> 0% of each run, Pallas kernels for 15% -> 17%
where the time goes in v11:
time: 21.1 us; the launch traced here: 20.8 us
  waiting for transfers between devices  9.31 us (44%)
  starting transfers between devices  6.62 us (31%)
  Pallas kernels  4.74 us (22%)
    ppermute x10, waiting for transfers between devices, exchange(): return lax.ppermute(value, AXES, pairs)  9.31 us
    ppermute x10, starting transfers between devices, exchange(): return lax.ppermute(value, AXES, pairs)  6.62 us
    pallas_call x5, Pallas kernels, part(): pl.pallas_call(functools.partial(part_kernel, windows, first, len(sets)),...  2.44 us
    pallas_call x1, Pallas kernels, on_device(): pl.pallas_call(functools.partial(place_kernel, order, last_bit), out_shap...  0.69 us
    pallas_call x1, Pallas kernels, on_device(): pl.pallas_call(functools.partial(receiver_kernel, radius, order, last_bit...  0.52 us
  transfers between devices with their start and end apart: 10, of which 4 were waited for; matrix products, arithmetic and copies ran while one was open for 0% of the time, Pallas kernels for 17%

profile of v11, /device:TPU:25, one launch (start us, length us, event | category | flops | bytes accessed | tf_op | source)
XLA Modules:
  0.0 20.8 jit_solution(14912895049039426776)
XLA Ops:
  0.0 0.7 %collective-permute-start.1 = (bf16[4,4,2048]{2,1,0:T(4,128)(2,1)}, bf16[4,4,2048]{2,1,0:T(4,128)(2,1)S(1)}, u32[]{:S(2)}, u32[]{:S(2)}) collective-permute-start(bf16[4,4,2048]{2,1,0:T(4,128)(2,1)} %own_ref.3), channel_id=1, source_target_pairs={{0,8},{1,9},{2,10},{3,11},{4,12},{5,13},{6,14},{7,15},{8,0},{9,1},... | collective-permute-start | bytes 196616 | tf_op jit(solution)/shard_map/ppermute | solution.py:432
  0.8 0.3 %short_tables.1 = (bf16[512,256]{1,0:T(8,128)(2,1)S(1)}, f32[2,16,128]{2,1,0:T(8,128)S(1)}) custom-call(), custom_call_target="tpu_custom_call" | custom-call | flops 5000000000 | bytes 1000000 | tf_op jit(solution)/shard_map/short_tables/pallas_call | solution.py:447
  1.1 0.0 copy-done.2
  1.1 0.3 %choose_rows.1 = (f32[8,128]{1,0:T(8,128)S(1)}, f32[8,128]{1,0:T(8,128)S(1)}, f32[1,8,128]{2,1,0:T(8,128)S(1)}, s32[8,128]{1,0:T(8,128)S(1)}) custom-call(s32[1,2]{1,0:T(1,128)S(1)} %bitcast.6, s32[4,128]{1,0:T(4,128)S(1)} %bitcast.4, f32[2,16,128]{2,1,0:T(8,128)S(1)} %get-tuple-element.16.after_ref.twiddle_ref.refs_4_), custom_call_target="tpu_custom_call" | custom-call | tf_op jit(solution)/shard_map/choose_rows/pallas_call | solution.py:460
  1.4 0.5 %receiver_spectra.1 = (bf16[256,128]{1,0:T(8,128)(2,1)S(1)}, f32[64,128]{1,0:T(8,128)S(1)}, f32[64,128]{1,0:T(8,128)S(1)}) custom-call(s32[8,128]{1,0:T(8,128)S(1)} %get-tuple-element.17.info_ref, s32[4,128]{1,0:T(4,128)S(1)} %bitcast.5, bf16[4,4,2048]{2,1,0:T(4,128)(2,1)S(1)} %copy-done, f32[2,16,128]{2,1,0:T(8,128)S(1)} %get-tuple-element.16.after_ref.twiddle_ref.refs_4_, ...), custom_call_target="tpu_custom_call" | custom-call | flops 5000000000 | bytes 1000000 | tf_op jit(solution)/shard_map/receiver_spectra/pallas_call | solution.py:476
  1.9 0.0 collective-permute-done.1.other_ref
  1.9 0.1 pick_rows.3
  2.0 1.5 %collective-permute-start.2 = (bf16[8,2048]{1,0:T(8,128)(2,1)S(1)}, bf16[8,2048]{1,0:T(8,128)(2,1)S(1)}, u32[]{:S(2)}, u32[]{:S(2)}) collective-permute-start(bf16[8,2048]{1,0:T(8,128)(2,1)S(1)} %pick_rows.3), channel_id=1, source_target_pairs={{0,24},{1,25},{2,26},{3,27},{4,28},{5,29},{6,30},{7,31},{8,16},{9,... | collective-permute-start | bytes 98312 | tf_op jit(solution)/shard_map/ppermute | solution.py:432
  3.4 0.3 %collective-permute-start = (bf16[256,128]{1,0:T(8,128)(2,1)S(1)}, bf16[256,128]{1,0:T(8,128)(2,1)S(1)}, u32[]{:S(2)}, u32[]{:S(2)}) collective-permute-start(bf16[256,128]{1,0:T(8,128)(2,1)S(1)} %get-tuple-element.19.refs_6_.refs_3_.refs_1_), channel_id=1, source_target_pairs={{0,10},{1,11},{2,8},{3,9},{4,14},{5,15},{6,12},{7,13},{8,2},{9,3},... | collective-permute-start | bytes 196616 | tf_op jit(solution)/shard_map/ppermute | solution.py:432
  3.8 1.6 %collective-permute-done.2.refs_3_ = bf16[8,2048]{1,0:T(8,128)(2,1)S(1)} collective-permute-done((bf16[8,2048]{1,0:T(8,128)(2,1)S(1)}, bf16[8,2048]{1,0:T(8,128)(2,1)S(1)}, u32[]{:S(2)}, u32[]{:S(2)}) %collective-permute-start.2) | collective-permute-done | bytes 32800 | tf_op jit(solution)/shard_map/ppermute | solution.py:432
  5.4 0.4 %source_spectra.1 = bf16[128,128]{1,0:T(8,128)(2,1)S(1)} custom-call(f32[8,128]{1,0:T(8,128)S(1)} %bitcast.3, f32[8,128]{1,0:T(8,128)S(1)} %get-tuple-element.23.refs_1_, bf16[8,2048]{1,0:T(8,128)(2,1)S(1)} %pick_rows.2.refs_2_, bf16[8,2048]{1,0:T(8,128)(2,1)S(1)} %collective-permute-done.2.refs_3_, ...), custom_call_target="tpu_custom_call" | custom-call | tf_op jit(solution)/shard_map/source_spectra/pallas_call | solution.py:512
  5.8 0.3 %collective-permute-start.3 = (bf16[128,128]{1,0:T(8,128)(2,1)S(1)}, bf16[128,128]{1,0:T(8,128)(2,1)S(1)}, u32[]{:S(2)}, u32[]{:S(2)}) collective-permute-start(bf16[128,128]{1,0:T(8,128)(2,1)S(1)} %source_spectra.1), channel_id=1, source_target_pairs={{0,12},{1,13},{2,14},{3,15},{4,8},{5,9},{6,10},{7,11},{8,4},{9,5},... | collective-permute-start | bytes 98312 | tf_op jit(solution)/shard_map/ppermute | solution.py:432
  6.1 1.3 %collective-permute-start.5 = (bf16[128,128]{1,0:T(8,128)(2,1)S(1)}, bf16[128,128]{1,0:T(8,128)(2,1)S(1)}, u32[]{:S(2)}, u32[]{:S(2)}) collective-permute-start(bf16[128,128]{1,0:T(8,128)(2,1)S(1)} %source_spectra.1), channel_id=1, source_target_pairs={{0,9},{1,8},{2,11},{3,10},{4,13},{5,12},{6,15},{7,14},{8,1},{9,0},... | collective-permute-start | bytes 98312 | tf_op jit(solution)/shard_map/ppermute | solution.py:432
  7.4 0.0 collective-permute-done.after_ref.refs_1_
  7.4 3.5 %collective-permute-done.3.value_ref = bf16[128,128]{1,0:T(8,128)(2,1)S(1)} collective-permute-done((bf16[128,128]{1,0:T(8,128)(2,1)S(1)}, bf16[128,128]{1,0:T(8,128)(2,1)S(1)}, u32[]{:S(2)}, u32[]{:S(2)}) %collective-permute-start.3) | collective-permute-done | bytes 32800 | tf_op jit(solution)/shard_map/ppermute | solution.py:432
  10.9 1.6 %collective-permute-start.7 = (bf16[128,128]{1,0:T(8,128)(2,1)S(1)}, bf16[128,128]{1,0:T(8,128)(2,1)S(1)}, u32[]{:S(2)}, u32[]{:S(2)}) collective-permute-start(bf16[128,128]{1,0:T(8,128)(2,1)S(1)} %pass_on.1), channel_id=1, source_target_pairs={{0,9},{1,8},{2,11},{3,10},{4,13},{5,12},{6,15},{7,14},{8,1},{9,0},... | collective-permute-start | bytes 98312 | tf_op jit(solution)/shard_map/ppermute | solution.py:432
  12.5 0.1 collective-permute-start.4
  12.6 0.0 collective-permute-done.5.refs_4_
  12.6 0.4 %collective-permute-start.6 = (bf16[128,128]{1,0:T(8,128)(2,1)S(1)}, bf16[128,128]{1,0:T(8,128)(2,1)S(1)}, u32[]{:S(2)}, u32[]{:S(2)}) collective-permute-start(bf16[128,128]{1,0:T(8,128)(2,1)S(1)} %collective-permute-done.5.refs_4_), channel_id=1, source_target_pairs={{0,8},{1,9},{2,10},{3,11},{4,12},{5,13},{6,14},{7,15},{8,0},{9,1},... | collective-permute-start | bytes 98312 | tf_op jit(solution)/shard_map/ppermute | solution.py:432
  13.0 0.5 %correlate_part.5 = (bf16[16,512]{1,0:T(8,128)(2,1)S(1)}, bf16[16,512]{1,0:T(8,128)(2,1)S(1)}) custom-call(bf16[2048,512]{1,0:T(8,128)(2,1)S(1)} %copy-done.3, bf16[256,128]{1,0:T(8,128)(2,1)S(1)} %collective-permute-done.after_ref.refs_1_, f32[64,128]{1,0:T(8,128)S(1)} %get-tuple-element.20.refs_2_, ...), custom_call_target="tpu_custom_call" | custom-call | flops 1000000000 | bytes 1000000 | tf_op jit(solution)/shard_map/correlate_part/pallas_call | solution.py:525
  13.5 0.8 %collective-permute-done.7.refs_6_.refs_4_ = bf16[128,128]{1,0:T(8,128)(2,1)S(1)} collective-permute-done((bf16[128,128]{1,0:T(8,128)(2,1)S(1)}, bf16[128,128]{1,0:T(8,128)(2,1)S(1)}, u32[]{:S(2)}, u32[]{:S(2)}) %collective-permute-start.7) | collective-permute-done | bytes 32800 | tf_op jit(solution)/shard_map/ppermute | solution.py:432
  14.4 0.4 %collective-permute-start.8 = (bf16[128,128]{1,0:T(8,128)(2,1)S(1)}, bf16[128,128]{1,0:T(8,128)(2,1)S(1)}, u32[]{:S(2)}, u32[]{:S(2)}) collective-permute-start(bf16[128,128]{1,0:T(8,128)(2,1)S(1)} %collective-permute-done.7.refs_6_.refs_4_), channel_id=1, source_target_pairs={{0,8},{1,9},{2,10},{3,11},{4,12},{5,13},{6,14},{7,15},{8,0},{9,1},... | collective-permute-start | bytes 98312 | tf_op jit(solution)/shard_map/ppermute | solution.py:432
  14.7 0.0 collective-permute-done.6.refs_5_.refs_3_
  14.7 0.4 %correlate_part.8 = bf16[16,512]{1,0:T(8,128)(2,1)S(1)} custom-call(bf16[2048,512]{1,0:T(8,128)(2,1)S(1)} %copy-done.3, bf16[256,128]{1,0:T(8,128)(2,1)S(1)} %collective-permute-done.after_ref.refs_1_, f32[64,128]{1,0:T(8,128)S(1)} %get-tuple-element.20.refs_2_, bf16[128,128]{1,0:T(8,128)(2,1)S(1)} %collective-permute-done.6.refs_5_.refs_3_, ...), custom_call_target="tpu_custom_call" | custom-call | flops 1000000000 | bytes 1000000 | tf_op jit(solution)/shard_map/correlate_part/pallas_call | solution.py:525
  15.2 0.0 collective-permute-done.4.refs_3_
  15.2 0.5 %correlate_part.7 = bf16[24,512]{1,0:T(8,128)(2,1)S(1)} custom-call(bf16[2048,512]{1,0:T(8,128)(2,1)S(1)} %copy-done.3, bf16[256,128]{1,0:T(8,128)(2,1)S(1)} %collective-permute-done.after_ref.refs_1_, f32[64,128]{1,0:T(8,128)S(1)} %get-tuple-element.20.refs_2_, bf16[256,128]{1,0:T(8,128)(2,1)S(1)} %collective-permute-done.4.refs_3_, ...), custom_call_target="tpu_custom_call" | custom-call | flops 1000000000 | bytes 1000000 | tf_op jit(solution)/shard_map/correlate_part/pallas_call | solution.py:525
  15.7 0.0 collective-permute-done.8.refs_7_.refs_3_
  15.7 0.4 %correlate_part.9 = bf16[8,512]{1,0:T(8,128)(2,1)S(1)} custom-call(bf16[2048,512]{1,0:T(8,128)(2,1)S(1)} %copy-done.3, bf16[256,128]{1,0:T(8,128)(2,1)S(1)} %collective-permute-done.after_ref.refs_1_, f32[64,128]{1,0:T(8,128)S(1)} %get-tuple-element.20.refs_2_, bf16[128,128]{1,0:T(8,128)(2,1)S(1)} %collective-permute-done.8.refs_7_.refs_3_), custom_call_target="tpu_custom_call" | custom-call | flops 1000000000 | bytes 1000000 | tf_op jit(solution)/shard_map/correlate_part/pallas_call | solution.py:525
  16.1 0.0 collective-permute-start.9
  16.1 0.6 %correlate_part.6.refs_1_ = bf16[48,512]{1,0:T(8,128)(2,1)S(1)} custom-call(bf16[2048,512]{1,0:T(8,128)(2,1)S(1)} %copy-done.3, bf16[256,128]{1,0:T(8,128)(2,1)S(1)} %get-tuple-element.19.refs_6_.refs_3_.refs_1_, f32[64,128]{1,0:T(8,128)S(1)} %get-tuple-element.21.after_ref.refs_4_.refs_2_, bf16[256,128]{1,0:T(8,128)(2,1)S(1)} %collective-permute-done.4.refs_3_, ...), custom_call_target="tpu_custom_call" | custom-call | flops 1000000000 | bytes 1000000 | tf_op jit(solution)/shard_map/correlate_part/pallas_call | solution.py:525
  16.7 3.4 %collective-permute-done.9.refs_2_ = bf16[64,512]{1,0:T(8,128)(2,1)S(1)} collective-permute-done((bf16[64,512]{1,0:T(8,128)(2,1)S(1)}, bf16[64,512]{1,0:T(8,128)(2,1)S(1)}, u32[]{:S(2)}, u32[]{:S(2)}) %collective-permute-start.9) | collective-permute-done | bytes 65568 | tf_op jit(solution)/shard_map/ppermute | solution.py:432
  20.1 0.7 %place_rows.1 = bf16[2,16,4,512]{3,2,1,0:T(4,128)(2,1)} custom-call(bf16[16,512]{1,0:T(8,128)(2,1)S(1)} %get-tuple-element.25.refs_0_, bf16[48,512]{1,0:T(8,128)(2,1)S(1)} %correlate_part.6.refs_1_, bf16[64,512]{1,0:T(8,128)(2,1)S(1)} %collective-permute-done.9.refs_2_), custom_call_target="tpu_custom_call" | custom-call | tf_op jit(solution)/shard_map/place_rows/pallas_call | solution.py:567
  (11 shorter events, 0.1 us)
Async XLA Ops:
  0.0 1.4 %copy-start = (bf16[4,4,2048]{2,1,0:T(4,128)(2,1)S(1)}, bf16[4,4,2048]{2,1,0:T(4,128)(2,1)}, u32[]{:S(2)}) copy-start(bf16[4,4,2048]{2,1,0:T(4,128)(2,1)} %own_ref.3) | copy-start | bytes 196612
  0.0 1.1 %copy-start.2 = (s32[2]{0:T(128)S(1)}, s32[2]{0:T(128)}, u32[]{:S(2)}) copy-start(s32[2]{0:T(128)} %param.6) | copy-start | bytes 28
  0.0 1.1 %copy-start.1 = (s32[128,4]{0,1:T(4,128)S(1)}, s32[128,4]{0,1:T(4,128)}, u32[]{:S(2)}) copy-start(s32[128,4]{0,1:T(4,128)} %param.5) | copy-start | bytes 6148
  0.0 1.9 %collective-permute-start.1 = (bf16[4,4,2048]{2,1,0:T(4,128)(2,1)}, bf16[4,4,2048]{2,1,0:T(4,128)(2,1)S(1)}, u32[]{:S(2)}, u32[]{:S(2)}) collective-permute-start(bf16[4,4,2048]{2,1,0:T(4,128)(2,1)} %own_ref.3), channel_id=1, source_target_pairs={{0,8},{1,9},{2,10},{3,11},{4,12},{5,13},{6,14},{7,15},{8,0},{9,1},... | collective-permute-start | bytes 196616 | tf_op jit(solution)/shard_map/ppermute | solution.py:432
  1.4 11.6 %copy-start.3 = (bf16[2048,512]{1,0:T(8,128)(2,1)S(1)}, bf16[2048,512]{1,0:T(8,128)(2,1)}, u32[]{:S(2)}) copy-start(bf16[2048,512]{1,0:T(8,128)(2,1)} %constant.2.clone.refs_0_) | copy-start | bytes 6291460
  2.0 3.4 %collective-permute-start.2 = (bf16[8,2048]{1,0:T(8,128)(2,1)S(1)}, bf16[8,2048]{1,0:T(8,128)(2,1)S(1)}, u32[]{:S(2)}, u32[]{:S(2)}) collective-permute-start(bf16[8,2048]{1,0:T(8,128)(2,1)S(1)} %pick_rows.3), channel_id=1, source_target_pairs={{0,24},{1,25},{2,26},{3,27},{4,28},{5,29},{6,30},{7,31},{8,16},{9,... | collective-permute-start | bytes 98312 | tf_op jit(solution)/shard_map/ppermute | solution.py:432
  3.4 4.0 %collective-permute-start = (bf16[256,128]{1,0:T(8,128)(2,1)S(1)}, bf16[256,128]{1,0:T(8,128)(2,1)S(1)}, u32[]{:S(2)}, u32[]{:S(2)}) collective-permute-start(bf16[256,128]{1,0:T(8,128)(2,1)S(1)} %get-tuple-element.19.refs_6_.refs_3_.refs_1_), channel_id=1, source_target_pairs={{0,10},{1,11},{2,8},{3,9},{4,14},{5,15},{6,12},{7,13},{8,2},{9,3},... | collective-permute-start | bytes 196616 | tf_op jit(solution)/shard_map/ppermute | solution.py:432
  5.8 5.1 %collective-permute-start.3 = (bf16[128,128]{1,0:T(8,128)(2,1)S(1)}, bf16[128,128]{1,0:T(8,128)(2,1)S(1)}, u32[]{:S(2)}, u32[]{:S(2)}) collective-permute-start(bf16[128,128]{1,0:T(8,128)(2,1)S(1)} %source_spectra.1), channel_id=1, source_target_pairs={{0,12},{1,13},{2,14},{3,15},{4,8},{5,9},{6,10},{7,11},{8,4},{9,5},... | collective-permute-start | bytes 98312 | tf_op jit(solution)/shard_map/ppermute | solution.py:432
  6.1 6.5 %collective-permute-start.5 = (bf16[128,128]{1,0:T(8,128)(2,1)S(1)}, bf16[128,128]{1,0:T(8,128)(2,1)S(1)}, u32[]{:S(2)}, u32[]{:S(2)}) collective-permute-start(bf16[128,128]{1,0:T(8,128)(2,1)S(1)} %source_spectra.1), channel_id=1, source_target_pairs={{0,9},{1,8},{2,11},{3,10},{4,13},{5,12},{6,15},{7,14},{8,1},{9,0},... | collective-permute-start | bytes 98312 | tf_op jit(solution)/shard_map/ppermute | solution.py:432
  10.9 3.5 %collective-permute-start.7 = (bf16[128,128]{1,0:T(8,128)(2,1)S(1)}, bf16[128,128]{1,0:T(8,128)(2,1)S(1)}, u32[]{:S(2)}, u32[]{:S(2)}) collective-permute-start(bf16[128,128]{1,0:T(8,128)(2,1)S(1)} %pass_on.1), channel_id=1, source_target_pairs={{0,9},{1,8},{2,11},{3,10},{4,13},{5,12},{6,15},{7,14},{8,1},{9,0},... | collective-permute-start | bytes 98312 | tf_op jit(solution)/shard_map/ppermute | solution.py:432
  12.5 2.7 %collective-permute-start.4 = (bf16[256,128]{1,0:T(8,128)(2,1)S(1)}, bf16[256,128]{1,0:T(8,128)(2,1)S(1)}, u32[]{:S(2)}, u32[]{:S(2)}) collective-permute-start(bf16[256,128]{1,0:T(8,128)(2,1)S(1)} %pad_maximum_fusion.refs_5_), channel_id=1, source_target_pairs={{0,8},{1,9},{2,10},{3,11},{4,12},{5,13},{6,14},{7,15},{8,0},{9,1},... | collective-permute-start | bytes 196616 | tf_op jit(solution)/shard_map/ppermute | solution.py:432
  12.6 2.2 %collective-permute-start.6 = (bf16[128,128]{1,0:T(8,128)(2,1)S(1)}, bf16[128,128]{1,0:T(8,128)(2,1)S(1)}, u32[]{:S(2)}, u32[]{:S(2)}) collective-permute-start(bf16[128,128]{1,0:T(8,128)(2,1)S(1)} %collective-permute-done.5.refs_4_), channel_id=1, source_target_pairs={{0,8},{1,9},{2,10},{3,11},{4,12},{5,13},{6,14},{7,15},{8,0},{9,1},... | collective-permute-start | bytes 98312 | tf_op jit(solution)/shard_map/ppermute | solution.py:432
  14.4 1.3 %collective-permute-start.8 = (bf16[128,128]{1,0:T(8,128)(2,1)S(1)}, bf16[128,128]{1,0:T(8,128)(2,1)S(1)}, u32[]{:S(2)}, u32[]{:S(2)}) collective-permute-start(bf16[128,128]{1,0:T(8,128)(2,1)S(1)} %collective-permute-done.7.refs_6_.refs_4_), channel_id=1, source_target_pairs={{0,8},{1,9},{2,10},{3,11},{4,12},{5,13},{6,14},{7,15},{8,0},{9,1},... | collective-permute-start | bytes 98312 | tf_op jit(solution)/shard_map/ppermute | solution.py:432
  16.1 4.0 %collective-permute-start.9 = (bf16[64,512]{1,0:T(8,128)(2,1)S(1)}, bf16[64,512]{1,0:T(8,128)(2,1)S(1)}, u32[]{:S(2)}, u32[]{:S(2)}) collective-permute-start(bf16[64,512]{1,0:T(8,128)(2,1)S(1)} %pad_maximum_fusion.1), channel_id=1, source_target_pairs={{0,10},{1,11},{2,8},{3,9},{4,14},{5,15},{6,12},{7,13},{8,2},{9,3},... | collective-permute-start | bytes 196616 | tf_op jit(solution)/shard_map/ppermute | solution.py:432
